TPU v7x, 128 devices: a whole 4x4x4 slice. The times are simulated.
128 devices in a mesh: ctx: 128 (over z, x, y, core).
Axes of the slice: x: 4, y: 4, z: 4, core: 2. Of those that a mesh axis runs over, the one named last changes fastest.
Arguments:
- queries: bfloat16 [65536, 2048], P('ctx'), may hold values from -13 to 13
- keys: bfloat16 [65536, 2048], P('ctx'), may hold values from -13 to 13
- values: bfloat16 [65536, 2048], P('ctx'), may hold values from -6 to 6
- chosen: int32 [128, 16, 3], P('ctx'), may hold values from 0 to 127, as said below
Outputs:
- attended: bfloat16 [65536, 2048], P('ctx')
Inputs may be any that keep to these rules, and one draw needn't show every extreme that they name: chosen[b, h, :] are three different blocks, none equal to b; over the 48 entries of one query block no block appears more than 1 times, and some block appears exactly 1 times.
All inputs are finite; a program needn't handle non-finite values.
Results may differ from a plain program's by a relative error of at most 0.0049.
Values may be sent and summed in bfloat16 or wider, within the bound.
No kernel may reach another device: no remote copies, remote signals or barrier semaphores. Data moves between devices by JAX's collectives and lax.ppermute only.
A program may use at most 192 MiB of HBM per device.

v0:
```python
import math

import jax
import jax.numpy as jnp
from jax import lax
from jax.sharding import PartitionSpec as P

HEAD = 128


def slot_heads(owners, num_dev, capacity, head_count):
    total = owners.shape[0]
    order = jnp.arange(total, dtype=jnp.int32)
    earlier = (owners[None, :] == owners[:, None]) & (order[None, :] < order[:, None])
    ranking = jnp.sum(earlier.astype(jnp.int32), axis=1)
    matches = (owners[None, None, :] == jnp.arange(num_dev, dtype=jnp.int32)[:, None, None]) & (
        ranking[None, None, :] == jnp.arange(capacity, dtype=jnp.int32)[None, :, None]
    )
    which_head = order // 3
    table = jnp.sum(jnp.where(matches, which_head[None, None, :], 0), axis=2)
    filled = jnp.any(matches, axis=2)
    return (jnp.where(filled, table, head_count), ranking)


def attend_group(query_grp, own_key, own_value, sel_key, sel_value, allowed, scale):
    score_own = (
        jnp.einsum("qhd,khd->hqk", query_grp, own_key, preferred_element_type=jnp.float32) * scale
    )
    score_own = jnp.where(allowed[None], score_own, -jnp.inf)
    score_sel = (
        jnp.einsum("qhd,khjd->hqjk", query_grp, sel_key, preferred_element_type=jnp.float32) * scale
    )
    highest = jnp.maximum(jnp.max(score_own, axis=-1), jnp.max(score_sel, axis=(2, 3)))
    denom = jnp.sum(jnp.exp(score_own - highest[..., None]), axis=-1) + jnp.sum(
        jnp.exp(score_sel - highest[:, :, None, None]), axis=(2, 3)
    )
    weight_own = (jnp.exp(score_own - highest[..., None]) / denom[..., None]).astype(jnp.bfloat16)
    weight_sel = (jnp.exp(score_sel - highest[:, :, None, None]) / denom[:, :, None, None]).astype(
        jnp.bfloat16
    )
    output = jnp.einsum("hqk,khd->qhd", weight_own, own_value, preferred_element_type=jnp.float32)
    output = output + jnp.einsum(
        "hqjk,khjd->qhd", weight_sel, sel_value, preferred_element_type=jnp.float32
    )
    return output


def body(queries, keys, values, chosen):
    num_dev = lax.axis_size("ctx")
    block_rows = keys.shape[0]
    head_count = keys.shape[1] // HEAD
    capacity = (3 * head_count + num_dev - 2) // (num_dev - 1)
    owners = chosen.reshape(-1)
    table, ranking = slot_heads(owners, num_dev, capacity, head_count)
    key_heads = keys.reshape(block_rows, head_count, HEAD)
    value_heads = values.reshape(block_rows, head_count, HEAD)
    paired = jnp.concatenate([key_heads, value_heads], axis=-1)
    padded = jnp.concatenate([paired, jnp.zeros((block_rows, 1, 2 * HEAD), jnp.bfloat16)], axis=1)
    wanted = lax.all_to_all(table, "ctx", split_axis=0, concat_axis=0, tiled=True)
    tiles = jnp.take(padded, wanted.reshape(-1), axis=1)
    arrived = lax.all_to_all(
        tiles.reshape(block_rows, wanted.shape[0], wanted.shape[1], 2 * HEAD),
        "ctx",
        split_axis=1,
        concat_axis=1,
        tiled=True,
    )
    slot_index = owners * capacity + ranking
    picked = jnp.take(arrived.reshape(block_rows, num_dev * capacity, 2 * HEAD), slot_index, axis=1)
    picked = picked.reshape(block_rows, head_count, 3, 2 * HEAD)
    query_heads = queries.reshape(block_rows, head_count, HEAD)
    row_iota = jnp.arange(block_rows)[:, None]
    col_iota = jnp.arange(block_rows)[None, :]
    allowed = col_iota <= row_iota
    scale = 1.0 / math.sqrt(HEAD)
    results = []
    for group in range(head_count // 4):
        first = group * 4
        last = first + 4
        results.append(
            attend_group(
                query_heads[:, first:last],
                key_heads[:, first:last],
                value_heads[:, first:last],
                picked[:, first:last, :, :HEAD],
                picked[:, first:last, :, HEAD:],
                allowed,
                scale,
            )
        )
    output = jnp.concatenate(results, axis=1)
    return output.astype(jnp.bfloat16).reshape(block_rows, head_count * HEAD)


def solution(mesh):
    placed = (P("ctx", None), P("ctx", None), P("ctx", None), P("ctx", None, None))
    return jax.shard_map(
        body, mesh=mesh, in_specs=placed, out_specs=P("ctx", None), check_vma=False
    )
```

profile of v0, /device:TPU:102, one launch (start us, length us, event | category | flops | bytes accessed | tf_op | source)
XLA Modules:
  0.0 716.3 jit_solution(7918380799099652429)
XLA Ops:
  0.0 0.8 copy.121
  0.8 0.1 reshape.376
  0.9 0.2 convert_reduce_fusion
  1.1 0.1 fusion.94
  1.2 0.1 select_reduce_fusion
  1.3 0.7 copy.124
  2.0 9.8 %all-to-all-start = ((s32[128,1,1]{2,1,0:T(1,128)}), s32[128,1,1]{2,1,0:T(1,128)S(1)}, u32[]{:S(2)}, u32[]{:S(2)}) async-start(s32[128,1,1]{2,1,0:T(1,128)} %copy.124), calls=%async_computation | async-start | bytes 131072 | tf_op jit(solution)/shard_map/all_to_all | solution.py:59
  11.8 2.9 copy.119
  14.7 0.0 copy-start.2
  14.7 4.6 copy.125
  19.3 3.6 fusion.15
  22.9 0.0 copy-done.2
  22.9 0.0 all-to-all-done
  22.9 2.4 reduce.2
  25.3 14.7 %gather_fusion = bf16[128,512,256]{1,2,0:T(8,128)(2,1)} fusion(bf16[512,17,256]{0,2,1:T(8,128)(2,1)} %fusion.15, s32[1024]{0:T(1024)S(1)} %pad_clamp_fusion.1), kind=kCustom, calls=%fused_computation | custom fusion | bytes 67109376 | tf_op jit(solution)/shard_map/jit(_take)/gather | solution.py:60
  40.0 22.8 %fusion = bf16[512,128,1,256]{0,3,2,1:T(8,128)(2,1)} fusion(bf16[128,512,256]{1,2,0:T(8,128)(2,1)} %gather_fusion, pred[128]{0:T(512)(128)(4,1)S(1)} %compare_and_fusion), kind=kLoop, calls=%fused_computation.3 | loop fusion | flops 16777216 | bytes 67108992 | tf_op jit(solution)/shard_map/jit(_take)/select_n | solution.py:60
  62.8 10.3 %all-to-all-start.1 = ((bf16[512,128,1,256]{0,3,2,1:T(8,128)(2,1)}), bf16[512,128,1,256]{0,3,2,1:T(8,128)(2,1)}, u32[]{:S(2)}, u32[]{:S(2)}) async-start(bf16[512,128,1,256]{0,3,2,1:T(8,128)(2,1)} %fusion), calls=%async_computation.1 | async-start | bytes 67108864 | tf_op jit(solution)/shard_map/all_to_all | solution.py:61
  73.2 0.1 reshape.379
  73.3 0.1 reduce_sum.95
  73.4 0.1 copy.122
  73.4 0.0 copy-done.9
  73.5 0.1 copy.123
  73.6 2.9 copy.117
  76.4 0.0 copy-start.3
  76.5 0.1 iota_compare_fusion.1
  76.6 3.9 fusion.80
  80.4 0.0 copy-done.3
  80.4 2.7 fusion.83
  83.1 2.9 fusion.16
  86.0 496.5 %all-to-all-done.1 = bf16[512,128,1,256]{0,3,2,1:T(8,128)(2,1)} async-done(((bf16[512,128,1,256]{0,3,2,1:T(8,128)(2,1)}), bf16[512,128,1,256]{0,3,2,1:T(8,128)(2,1)}, u32[]{:S(2)}, u32[]{:S(2)}) %all-to-all-start.1) | async-done | bytes 33554464 | tf_op jit(solution)/shard_map/all_to_all | solution.py:61
  582.5 10.5 %gather_fusion.1 = bf16[48,512,256]{1,2,0:T(8,128)(2,1)} fusion(bf16[512,128,256]{0,2,1:T(8,128)(2,1)} %bitcast.8, s32[1024]{0:T(1024)S(1)} %pad_clamp_fusion), kind=kCustom, calls=%fused_computation.1 | custom fusion | bytes 25166016 | tf_op jit(solution)/shard_map/jit(_take)/gather | solution.py:69
  593.1 16.6 %copy.128 = bf16[512,48,256]{2,0,1:T(8,128)(2,1)} copy(bf16[512,48,256]{0,2,1:T(8,128)(2,1)} %bitcast.178) | data formatting | bytes 25165824 | tf_op jit(solution)/shard_map/jit(_take)/gather | solution.py:69
  609.7 6.7 broadcast_select_fusion
  616.4 0.0 copy-start
  616.4 6.7 bitcast_reduce_fusion.3
  623.1 6.4 bitcast_reduce_fusion.2
  629.5 1.8 bitcast_reduce_fusion
  631.3 0.0 copy-done
  631.3 6.3 bitcast_reduce_fusion.1
  637.5 6.6 fusion.5
  644.2 8.7 %fusion.20 = (f32[4,512]{1,0:T(4,128)S(1)}, f32[4,512]{1,0:T(4,128)S(1)}, f32[4,512]{1,0:T(4,128)S(1)}, f32[4,512]{1,0:T(4,128)S(1)}, f32[4,512,512]{1,2,0:T(8,128)}) fusion(f32[4,512,512]{1,2,0:T(8,128)} %get-tuple-element.13, f32[4,512]{1,0:T(4,128)S(1)} %max.44, pred[512,512]{0,1:T(8,128)(4,1)S(1)} %iota_compare_fusion.1, f32[4,512,512]{1,2,0:T(8,128)} %fusion.83, ...), kind=kOutput, calls=%fused_computation.49 | convolution fusion | flops 282058752 | bytes 19701760 | tf_op jit(solution)/shard_map/qhd,khd->hqk/dot_general | solution.py:27
  652.9 0.0 copy-done.10
  652.9 2.5 fusion.43
  655.4 8.6 %fusion.77 = bf16[512,4,128]{0,2,1:T(8,128)(2,1)} fusion(f32[512,4,128]{0,2,1:T(8,128)S(1)} %fusion.43, f32[4,512,3,512]{3,1,2,0:T(8,128)} %get-tuple-element.15, f32[4,512]{1,0:T(4,128)S(1)} %add.131, f32[4,512]{1,0:T(4,128)S(1)} %max.44, bf16[512,16,3,256]{3,0,2,1:T(8,128)(2,1)} %copy-done), kind=kOutput, calls=%fused_computation.85 | convolution fusion | flops 818413568 | bytes 15745024 | tf_op jit(solution)/shard_map/hqjk,khjd->qhd/dot_general | solution.py:42
  664.1 6.8 fusion.6
  670.9 0.0 copy-done.1
  670.9 0.0 copy-start.4
  670.9 0.0 copy-start.5
  670.9 5.3 fusion.21
  676.2 0.0 copy-done.4
  676.2 1.5 fusion.42
  677.7 8.6 %fusion.74 = bf16[512,4,128]{0,2,1:T(8,128)(2,1)} fusion(f32[512,4,128]{0,2,1:T(8,128)S(1)} %fusion.42, f32[4,512,3,512]{3,1,2,0:T(8,128)} %get-tuple-element.18, f32[4,512]{1,0:T(4,128)S(1)} %add.133, f32[4,512]{1,0:T(4,128)S(1)} %max.45, bf16[512,16,3,256]{3,0,2,1:T(8,128)(2,1)} %copy-done), kind=kOutput, calls=%fused_computation.84 | convolution fusion | flops 818413568 | bytes 15745024 | tf_op jit(solution)/shard_map/hqjk,khjd->qhd/dot_general | solution.py:42
  686.3 6.6 fusion.7
  692.9 3.6 fusion.41
  696.5 8.6 %fusion.71 = bf16[512,4,128]{0,2,1:T(8,128)(2,1)} fusion(f32[512,4,128]{0,2,1:T(8,128)S(1)} %fusion.41, f32[4,512,3,512]{3,1,2,0:T(8,128)} %get-tuple-element.20, f32[4,512]{1,0:T(4,128)S(1)} %add.135, f32[4,512]{1,0:T(4,128)S(1)} %max.46, bf16[512,16,3,256]{3,0,2,1:T(8,128)(2,1)} %copy-done), kind=kOutput, calls=%fused_computation.83 | convolution fusion | flops 818413568 | bytes 15745024 | tf_op jit(solution)/shard_map/hqjk,khjd->qhd/dot_general | solution.py:42
  705.1 2.3 fusion.8
  707.4 1.4 fusion.40
  708.9 0.0 copy-start.8
  708.9 4.2 fusion.68
  713.2 0.0 copy-done.6
  713.2 0.0 copy-done.7
  713.2 0.0 copy-done.8
  713.2 0.3 pad_maximum_fusion
  713.5 2.4 copy.147
  (23 shorter events, 0.1 us)
Async XLA Ops:
  2.0 20.9 %all-to-all-start = ((s32[128,1,1]{2,1,0:T(1,128)}), s32[128,1,1]{2,1,0:T(1,128)S(1)}, u32[]{:S(2)}, u32[]{:S(2)}) async-start(s32[128,1,1]{2,1,0:T(1,128)} %copy.124), calls=%async_computation | async-start | bytes 131072 | tf_op jit(solution)/shard_map/all_to_all | solution.py:59
  14.7 8.2 %copy-start.2 = (bf16[512,2048]{0,1:T(8,128)(2,1)}, bf16[512,2048]{0,1:T(8,128)(2,1)S(1)}, u32[]{:S(2)}) copy-start(bf16[512,2048]{0,1:T(8,128)(2,1)S(1)} %copy.119) | copy-start | bytes 6291460
  62.8 10.6 %copy-start.9 = (s32[1,16,3]{1,0,2:T(1,128)S(1)}, s32[1,16,3]{1,0,2:T(1,128)}, u32[]{:S(2)}) copy-start(s32[1,16,3]{1,0,2:T(1,128)} %param.7) | copy-start | bytes 580
  62.8 519.7 %all-to-all-start.1 = ((bf16[512,128,1,256]{0,3,2,1:T(8,128)(2,1)}), bf16[512,128,1,256]{0,3,2,1:T(8,128)(2,1)}, u32[]{:S(2)}, u32[]{:S(2)}) async-start(bf16[512,128,1,256]{0,3,2,1:T(8,128)(2,1)} %fusion), calls=%async_computation.1 | async-start | bytes 67108864 | tf_op jit(solution)/shard_map/all_to_all | solution.py:61
  76.4 4.0 copy-start.3
  616.4 14.9 %copy-start = (bf16[512,16,3,256]{3,0,2,1:T(8,128)(2,1)}, bf16[512,16,3,256]{3,0,2,1:T(8,128)(2,1)S(1)}, u32[]{:S(2)}) copy-start(bf16[512,16,3,256]{3,0,2,1:T(8,128)(2,1)S(1)} %broadcast_select_fusion) | copy-start | bytes 37748740
  644.2 8.8 %copy-start.10 = (f32[4,512,512]{1,2,0:T(8,128)S(1)}, f32[4,512,512]{1,2,0:T(8,128)}, u32[]{:S(2)}) copy-start(f32[4,512,512]{1,2,0:T(8,128)} %get-tuple-element.13) | copy-start | bytes 12582916
  664.1 6.8 copy-start.1
  670.9 5.3 copy-start.4
  670.9 5.3 copy-start.5
  708.9 4.3 copy-start.6
  708.9 4.3 copy-start.7
  708.9 4.3 copy-start.8
where the time goes:
time: 724 us; the launch traced here: 716 us
  waiting for transfers between devices  497 us (69%)
  matrix products  78.2 us (11%)
  other arithmetic  64 us (9%)
  local copies, waits for them, and re-layouts  56.5 us (8%)
  starting transfers between devices  20.2 us (3%)
    all_to_all x1, waiting for transfers between devices, body(): lax.all_to_all(tiles.reshape(block_rows, wanted.shape[0], wanted.shape[1]...  497 us
    dot_general x4, matrix products, attend_group(): jnp.einsum('hqjk,khjd->qhd', weight_sel, sel_value, preferred_element_typ...  30 us
    gather x2, local copies, waits for them, and re-layouts, body(): jnp.take(arrived.reshape(block_rows, num_dev * capacity, 2 * HEAD), slot_...  27.1 us
    select_n x2, other arithmetic, body(): tiles = jnp.take(padded, wanted.reshape(-1), axis=1)  22.8 us
    reduce_sum x4, other arithmetic, attend_group(): jnp.sum(jnp.exp(score_sel - highest[:, :, None, None]), axis=(2, 3))  22.4 us
    dot_general x4, matrix products, attend_group(): jnp.einsum('qhd,khjd->hqjk', query_grp, sel_key, preferred_element_type=j...  21.1 us
    dot_general x4, matrix products, attend_group(): jnp.einsum('qhd,khd->hqk', query_grp, own_key, preferred_element_type=jnp...  18.2 us
    gather x1, local copies, waits for them, and re-layouts, body(): tiles = jnp.take(padded, wanted.reshape(-1), axis=1)  14.7 us
  transfers between devices with their start and end apart: 2, of which 1 were waited for; matrix products, arithmetic and copies ran while one was open for 3% of the time, Pallas kernels for 0%

commit v1 on v0

v1 whole, which is shorter than its diff:
```python
import math

import jax
import jax.numpy as jnp
from jax import lax
from jax.experimental import pallas as pl
from jax.experimental.pallas import tpu as pltpu
from jax.sharding import PartitionSpec as P

HEAD = 128
HEADS = 16
BLOCK = 512
DEVICES = 128
CHIPS = 64
SCALE = math.log2(math.e) / math.sqrt(HEAD)

ONE = [(1, 0, 0), (3, 0, 0), (0, 1, 0), (0, 3, 0), (0, 0, 1), (0, 0, 3)]
PARTNER = 6
SHIFTS = [(0, 0, 0, 1)] * PARTNER
SHIFTS += [(*s, c) for s in ONE for c in (0, 1)]
KINDS = len(SHIFTS)
SPARE = 4
PIECE = 16
SLOT_ROWS = 2 * BLOCK + SPARE * PIECE

ROW_DIRECT = CHIPS
ROW_SPARE = ROW_DIRECT + CHIPS
ROW_FORWARD = ROW_SPARE + CHIPS
ROW_FORWARD_HEAD = ROW_FORWARD + 32
ROW_FROM = ROW_FORWARD_HEAD + 32
ROW_FROM_RANK = ROW_FROM + 8
ROW_FROM_HEAD = ROW_FROM_RANK + 8
ROW_PARTNER = ROW_FROM_HEAD + 8
ROW_LEFT = ROW_PARTNER + 1
ROWS = ROW_PARTNER + 8


def through(device, shift):
    z, x, y, c = device // 32, device // 8 % 4, device // 2 % 4, device % 2
    dz, dx, dy, dc = shift
    return (((z + dz) % 4 * 4 + (x + dx) % 4) * 4 + (y + dy) % 4) * 2 + (c ^ dc)


def shift_pairs(shift):
    return [(through(b, shift), b) for b in range(DEVICES)]


def roll_lanes(array, amount):
    amount = amount % DEVICES
    return pltpu.roll(array, amount, 1) if amount else array


def permuted(array, shift, lane, inverse=False):
    dz, dx, dy, dc = shift
    if inverse:
        dz, dx, dy = -dz % 4, -dx % 4, -dy % 4
    if dz:
        array = roll_lanes(array, -32 * dz)
    if dx:
        inside = (lane // 8) % 4 + dx < 4
        array = jnp.where(inside, roll_lanes(array, -8 * dx), roll_lanes(array, 32 - 8 * dx))
    if dy:
        inside = (lane // 2) % 4 + dy < 4
        array = jnp.where(inside, roll_lanes(array, -2 * dy), roll_lanes(array, 8 - 2 * dy))
    if dc:
        array = jnp.where(lane % 2 == 0, roll_lanes(array, -1), roll_lanes(array, 1))
    return array


def plan_kernel(chosen_ref, out_ref):
    chip = lax.broadcasted_iota(jnp.int32, (CHIPS, DEVICES), 0)
    lane = lax.broadcasted_iota(jnp.int32, (CHIPS, DEVICES), 1)
    even = jnp.zeros((CHIPS, DEVICES), jnp.int32)
    odd = jnp.zeros((CHIPS, DEVICES), jnp.int32)
    for entry in range(3 * HEADS):
        owner = chosen_ref[entry : entry + 1, :]
        even = even + jnp.where(owner == 2 * chip, entry // 3 + 1, 0)
        odd = odd + jnp.where(owner == 2 * chip + 1, entry // 3 + 1, 0)
    home = lane // 2 == chip
    partner = jnp.sum(jnp.where(home, even + odd, 0), axis=0, keepdims=True)
    even = jnp.where(home, 0, even)
    odd = jnp.where(home, 0, odd)
    waiting = jnp.where(even > 0, odd, 0)
    slot = jnp.where(even > 0, even - 1, jnp.where(odd > 0, odd + 15, 0))
    direct = jnp.where(even > 0, even, odd)
    free = jnp.where(home, 0, jnp.where(direct > 0, 0, 1))
    options = jnp.zeros((CHIPS, DEVICES), jnp.int32)
    for shift in sorted(set(SHIFTS)):
        options = options + permuted(free, shift, lane)
    score = options * 64 + (chip + 17 * lane) % 64
    big = 1 << 20
    out_ref[...] = jnp.zeros((ROWS, DEVICES), jnp.int32)
    for kind, shift in enumerate(SHIFTS):
        able = (waiting > 0) & (permuted(free, shift, lane) > 0)
        rated = jnp.where(able, score, big)
        best = jnp.min(rated, axis=0, keepdims=True)
        picked = able & (rated == best)
        head = jnp.sum(jnp.where(picked, waiting, 0), axis=0, keepdims=True)
        back = permuted(jnp.where(picked, waiting + 16, 0), shift, lane, inverse=True)
        waiting = jnp.where(picked, 0, waiting)
        slot = jnp.where(back > 0, back - 1, slot)
        free = jnp.where(back > 0, 0, free)
        forward = jnp.sum(jnp.where(back > 0, chip, 0), axis=0, keepdims=True)
        out_ref[ROW_FORWARD + kind : ROW_FORWARD + kind + 1, :] = forward
        out_ref[ROW_FORWARD_HEAD + kind : ROW_FORWARD_HEAD + kind + 1, :] = head
    before = lax.broadcasted_iota(jnp.int32, (DEVICES, DEVICES), 0)
    after = lax.broadcasted_iota(jnp.int32, (DEVICES, DEVICES), 1)
    earlier = jnp.where((before < after) & (before % 2 == after % 2), 1.0, 0.0)
    rank = jnp.dot(
        jnp.where(waiting > 0, 1.0, 0.0), earlier, preferred_element_type=jnp.float32
    ).astype(jnp.int32)
    spare = jnp.zeros((CHIPS, DEVICES), jnp.int32)
    for index in range(SPARE):
        for core in range(2):
            chosen = (rank == index) & (lane % 2 == core)
            head = jnp.sum(jnp.where(chosen, waiting, 0), axis=1, keepdims=True)
            spare = jnp.where(lane == 2 * index + core, head, spare)
    out_ref[ROW_SPARE : ROW_SPARE + CHIPS, :] = spare
    excess = jnp.where((waiting > 0) & (rank >= SPARE), 1, 0)
    for index in range(SPARE):
        best = jnp.min(jnp.where(waiting > 0, chip, big), axis=0, keepdims=True)
        picked = (waiting > 0) & (chip == best)
        out_ref[ROW_FROM + index : ROW_FROM + index + 1, :] = jnp.where(best < big, best, 0)
        out_ref[ROW_FROM_RANK + index : ROW_FROM_RANK + index + 1, :] = jnp.minimum(
            jnp.sum(jnp.where(picked, rank, 0), axis=0, keepdims=True), SPARE - 1
        )
        out_ref[ROW_FROM_HEAD + index : ROW_FROM_HEAD + index + 1, :] = jnp.sum(
            jnp.where(picked, waiting, 0), axis=0, keepdims=True
        )
        waiting = jnp.where(picked, 0, waiting)
    excess = excess + waiting
    out_ref[ROW_PARTNER : ROW_PARTNER + 1, :] = partner
    left = jnp.max(jnp.max(excess, axis=0, keepdims=True), axis=1, keepdims=True)
    out_ref[ROW_LEFT : ROW_LEFT + 1, :] = jnp.broadcast_to(left, (1, DEVICES))
    out_ref[0:CHIPS, :] = slot
    out_ref[ROW_DIRECT : ROW_DIRECT + CHIPS, :] = direct


def make_plan(chosen_all):
    return pl.pallas_call(
        plan_kernel,
        out_shape=jax.ShapeDtypeStruct((ROWS, DEVICES), jnp.int32),
        name="plan",
    )(chosen_all)


def columns(head):
    return pl.ds(pl.multiple_of(head * HEAD, HEAD), HEAD)


def pack_kernel(plan, me_ref, keys, values, other_keys, other_values, send, sem):
    me = me_ref[0]
    chip, core = me // 2, me % 2

    def one_slot(dest, carry):
        code = plan[chip, 2 * dest + core]
        head = code % 16

        @pl.when(code // 16 == core)
        def _():
            for half, source in enumerate((keys, values)):
                pltpu.make_async_copy(
                    source.at[:, columns(head)], send.at[dest, pl.ds(half * BLOCK, BLOCK)], sem
                ).start()

        @pl.when(code // 16 != core)
        def _():
            for half, source in enumerate((other_keys, other_values)):
                pltpu.make_async_copy(
                    source.at[:, columns(head)], send.at[dest, pl.ds(half * BLOCK, BLOCK)], sem
                ).start()

        return carry

    lax.fori_loop(0, CHIPS, one_slot, 0)

    def one_spare(index, carry):
        head = jnp.maximum(plan[ROW_SPARE + chip, 2 * index + core] - 1, 0)
        into = pl.ds(pl.multiple_of(2 * BLOCK + index * PIECE, PIECE), PIECE)

        def one_piece(piece, carry):
            rows = pl.ds(pl.multiple_of(piece * PIECE, PIECE), PIECE)

            @pl.when(core == 1)
            def _():
                for half, source in enumerate((keys, values)):
                    pltpu.make_async_copy(
                        source.at[rows, columns(head)], send.at[2 * piece + half, into], sem
                    ).start()

            @pl.when(core == 0)
            def _():
                for half, source in enumerate((other_keys, other_values)):
                    pltpu.make_async_copy(
                        source.at[rows, columns(head)], send.at[2 * piece + half, into], sem
                    ).start()

            return carry

        return lax.fori_loop(0, CHIPS // 2, one_piece, carry)

    lax.fori_loop(0, SPARE, one_spare, 0)
    pltpu.make_async_copy(send, send, sem).wait()


ANY = pl.BlockSpec(memory_space=pl.ANY)
SMEM = pl.BlockSpec(memory_space=pltpu.SMEM)


def tiles(count):
    return jax.ShapeDtypeStruct((count, 2 * BLOCK, HEAD), jnp.bfloat16)


def pack(plan, me, keys, values, other_keys, other_values):
    return pl.pallas_call(
        pack_kernel,
        in_specs=[SMEM, SMEM, ANY, ANY, ANY, ANY],
        out_specs=ANY,
        out_shape=jax.ShapeDtypeStruct((CHIPS, SLOT_ROWS, HEAD), jnp.bfloat16),
        scratch_shapes=[pltpu.SemaphoreType.DMA],
        name="pack",
    )(plan, me, keys, values, other_keys, other_values)


def forward_kernel(plan, me_ref, arrived, pieces, *rest):
    outs, sems = rest[:-1], rest[-1]
    me = me_ref[0]
    core = me % 2
    for kind in range(KINDS):
        out = outs[0].at[kind] if kind < PARTNER else outs[kind - PARTNER + 1].at[0]
        pltpu.make_async_copy(
            arrived.at[plan[ROW_FORWARD + kind, me], pl.ds(0, 2 * BLOCK)], out, sems.at[kind]
        ).start()

    def one_dest(dest, carry):
        for index in range(SPARE):
            chip = plan[ROW_FROM + index, 2 * dest + core]
            rank = plan[ROW_FROM_RANK + index, 2 * dest + core]
            row = pl.multiple_of(2 * BLOCK + rank * PIECE, PIECE)
            pltpu.make_async_copy(
                arrived.at[chip, pl.ds(row, PIECE)],
                pieces.at[dest, pl.ds(index * PIECE, PIECE)],
                sems.at[KINDS],
            ).start()
        return carry

    lax.fori_loop(0, CHIPS, one_dest, 0)
    pltpu.make_async_copy(pieces, pieces, sems.at[KINDS]).wait()
    for kind in range(KINDS):
        out = outs[0].at[kind] if kind < PARTNER else outs[kind - PARTNER + 1].at[0]
        pltpu.make_async_copy(arrived.at[0, pl.ds(0, 2 * BLOCK)], out, sems.at[kind]).wait()


def forward(plan, me, arrived):
    return pl.pallas_call(
        forward_kernel,
        in_specs=[SMEM, SMEM, ANY],
        out_specs=[ANY] * (KINDS - PARTNER + 2),
        out_shape=[jax.ShapeDtypeStruct((CHIPS, SPARE * PIECE, HEAD), jnp.bfloat16)]
        + [tiles(PARTNER)]
        + [tiles(1)] * (KINDS - PARTNER),
        scratch_shapes=[pltpu.SemaphoreType.DMA((KINDS + 1,))],
        name="forward",
    )(plan, me, arrived)


def scores_of(query, key):
    return lax.dot_general(
        query, key, (((1,), (1,)), ((), ())), preferred_element_type=jnp.float32
    )


def attend_kernel(
    plan, me_ref, query, own_key, own_value, other_keys, other_values, arrived, *rest
):
    count = KINDS - PARTNER + 1
    forwarded, pieces = rest[:count], rest[count]
    out = rest[count + 1]
    where, filled, key_buf, value_buf, sems = rest[count + 2 :]
    me = me_ref[0]
    step = pl.program_id(0)

    def note(head_plus, code):
        @pl.when(head_plus > 0)
        def _():
            at = filled[head_plus - 1]
            where[(head_plus - 1) * 3 + jnp.minimum(at, 2)] = code
            filled[head_plus - 1] = at + 1

    def fetch(head, slot):
        for j in range(3):
            code = where[head * 3 + j]
            into_key = key_buf.at[slot, j]
            into_value = value_buf.at[slot, j, :, pl.ds(0, HEAD)]

            def start(source_key, source_value):
                pltpu.make_async_copy(source_key, into_key, sems.at[slot, j, 0]).start()
                pltpu.make_async_copy(source_value, into_value, sems.at[slot, j, 1]).start()

            @pl.when(code < CHIPS)
            def _():
                start(arrived.at[code, pl.ds(0, BLOCK)], arrived.at[code, pl.ds(BLOCK, BLOCK)])

            @pl.when((code >= 64) & (code < 64 + PARTNER))
            def _():
                ref = forwarded[0].at[code - 64]
                start(ref.at[pl.ds(0, BLOCK)], ref.at[pl.ds(BLOCK, BLOCK)])

            for kind in range(PARTNER, KINDS):

                @pl.when(code == 64 + kind)
                def _():
                    ref = forwarded[kind - PARTNER + 1]
                    start(ref.at[0, pl.ds(0, BLOCK)], ref.at[0, pl.ds(BLOCK, BLOCK)])

            @pl.when((code >= 96) & (code < 128))
            def _():
                from_row = pl.ds(pl.multiple_of((code - 96) * PIECE, PIECE), PIECE)

                def one_piece(piece, carry):
                    rows = pl.ds(pl.multiple_of(piece * PIECE, PIECE), PIECE)
                    pltpu.make_async_copy(
                        pieces.at[2 * piece, from_row], into_key.at[rows], sems.at[slot, j, 0]
                    ).start()
                    pltpu.make_async_copy(
                        pieces.at[2 * piece + 1, from_row],
                        into_value.at[rows],
                        sems.at[slot, j, 1],
                    ).start()
                    return carry

                lax.fori_loop(0, BLOCK // PIECE, one_piece, 0)

            @pl.when(code == 128)
            def _():
                start(other_keys.at[:, columns(head)], other_values.at[:, columns(head)])

    @pl.when(step == 0)
    def _():
        for h in range(HEADS):
            filled[h] = 0
            for j in range(3):
                where[h * 3 + j] = 0
        value_buf[...] = jnp.ones(value_buf.shape, value_buf.dtype)

        def direct(chip, carry):
            note(plan[ROW_DIRECT + chip, me], chip)
            return carry

        lax.fori_loop(0, CHIPS, direct, 0)

        def moved(kind, carry):
            note(plan[ROW_FORWARD_HEAD + kind, me], 64 + kind)
            return carry

        lax.fori_loop(0, KINDS, moved, 0)

        def shared(index, carry):
            note(plan[ROW_FROM_HEAD + index, me], 96 + index)
            return carry

        lax.fori_loop(0, SPARE, shared, 0)
        note(plan[ROW_PARTNER, me], 128)
        fetch(0, 0)

    slot = step % 2

    @pl.when(step + 1 < HEADS)
    def _():
        fetch(step + 1, 1 - slot)

    for j in range(3):
        pltpu.make_async_copy(
            arrived.at[0, pl.ds(0, BLOCK)], key_buf.at[slot, j], sems.at[slot, j, 0]
        ).wait()
        pltpu.make_async_copy(
            arrived.at[0, pl.ds(BLOCK, BLOCK)],
            value_buf.at[slot, j, :, pl.ds(0, HEAD)],
            sems.at[slot, j, 1],
        ).wait()

    rows = 256
    for part in range(BLOCK // rows):
        length = (part + 1) * rows
        q = query[part * rows : length, :]
        own = scores_of(q, own_key[0:length, :])
        row_iota = lax.broadcasted_iota(jnp.int32, (rows, length), 0) + part * rows
        col_iota = lax.broadcasted_iota(jnp.int32, (rows, length), 1)
        own = jnp.where(col_iota <= row_iota, own, -jnp.inf)
        others = [scores_of(q, key_buf[slot, j]) for j in range(3)]
        highest = jnp.max(own, axis=1, keepdims=True)
        for other in others:
            highest = jnp.maximum(highest, jnp.max(other, axis=1, keepdims=True))
        weight = jnp.exp2((own - highest) * SCALE).astype(jnp.bfloat16)
        ones = jnp.ones((length, HEAD), jnp.bfloat16)
        total = jnp.dot(
            weight,
            jnp.concatenate([own_value[0:length, :], ones], axis=1),
            preferred_element_type=jnp.float32,
        )
        for j, other in enumerate(others):
            weight = jnp.exp2((other - highest) * SCALE).astype(jnp.bfloat16)
            total = total + jnp.dot(
                weight, value_buf[slot, j], preferred_element_type=jnp.float32
            )
        out[part * rows : length, :] = (total[:, :HEAD] / total[:, HEAD:]).astype(jnp.bfloat16)


def attend(plan, me, queries, keys, values, other_keys, other_values, arrived, forwarded, pieces):
    block = pl.BlockSpec((BLOCK, HEAD), lambda h: (0, h))
    return pl.pallas_call(
        attend_kernel,
        grid=(HEADS,),
        in_specs=[SMEM, SMEM, block, block, block] + [ANY] * (4 + len(forwarded)),
        out_specs=block,
        out_shape=jax.ShapeDtypeStruct((BLOCK, HEADS * HEAD), jnp.bfloat16),
        scratch_shapes=[
            pltpu.SMEM((3 * HEADS,), jnp.int32),
            pltpu.SMEM((HEADS,), jnp.int32),
            pltpu.VMEM((2, 3, BLOCK, HEAD), jnp.bfloat16),
            pltpu.VMEM((2, 3, BLOCK, 2 * HEAD), jnp.bfloat16),
            pltpu.SemaphoreType.DMA((2, 3, 2)),
        ],
        compiler_params=pltpu.CompilerParams(vmem_limit_bytes=48 * 1024 * 1024),
        name="attend",
    )(plan, me, queries, keys, values, other_keys, other_values, arrived, *forwarded, pieces)


LANES = [[2 * chip + core for chip in range(CHIPS)] for core in range(2)]
SWAP = [(device, device ^ 1) for device in range(DEVICES)]


def exchange(array):
    return lax.all_to_all(array, "ctx", 0, 0, axis_index_groups=LANES, tiled=True)


def full_attention(queries, keys, values, chosen_all, me):
    heads = jnp.arange(3 * HEADS, dtype=jnp.int32) // 3
    mine = lax.dynamic_index_in_dim(chosen_all, me, 0, keepdims=False)
    wants = chosen_all == me
    which = jnp.max(jnp.where(wants, heads[None, :], 0), axis=1)
    key_heads = keys.reshape(BLOCK, HEADS, HEAD).transpose(1, 0, 2)
    value_heads = values.reshape(BLOCK, HEADS, HEAD).transpose(1, 0, 2)
    got_key = lax.all_to_all(jnp.take(key_heads, which, axis=0), "ctx", 0, 0, tiled=True)
    got_value = lax.all_to_all(jnp.take(value_heads, which, axis=0), "ctx", 0, 0, tiled=True)
    q_heads = queries.reshape(BLOCK, HEADS, HEAD).transpose(1, 0, 2)
    allowed = jnp.arange(4 * BLOCK)[None, :] >= BLOCK
    allowed = allowed | (jnp.arange(4 * BLOCK)[None, :] <= jnp.arange(BLOCK)[:, None])

    def one_head(head):
        picks = lax.dynamic_slice(mine, (3 * head,), (3,))
        k = jnp.concatenate([key_heads[head], got_key[picks].reshape(3 * BLOCK, HEAD)], axis=0)
        v = jnp.concatenate([value_heads[head], got_value[picks].reshape(3 * BLOCK, HEAD)], axis=0)
        s = jnp.where(allowed, scores_of(q_heads[head], k), -jnp.inf)
        weight = jnp.exp2((s - jnp.max(s, axis=1, keepdims=True)) * SCALE)
        total = jnp.sum(weight, axis=1, keepdims=True)
        o = jnp.dot(weight.astype(jnp.bfloat16), v, preferred_element_type=jnp.float32)
        return (o / total).astype(jnp.bfloat16)

    out = lax.map(one_head, jnp.arange(HEADS))
    return out.transpose(1, 0, 2).reshape(BLOCK, HEADS * HEAD)


def body(queries, keys, values, chosen):
    me = lax.axis_index("ctx").astype(jnp.int32)
    me_ref = me.reshape(1)
    other_keys = lax.ppermute(keys, "ctx", SWAP)
    other_values = lax.ppermute(values, "ctx", SWAP)
    chosen_all = lax.all_gather(chosen.reshape(1, 3 * HEADS), "ctx", axis=0, tiled=True)
    plan = make_plan(chosen_all.T)
    send = pack(plan, me_ref, keys, values, other_keys, other_values)
    arrived = exchange(send)
    pieces, *outgoing = forward(plan, me_ref, arrived)
    pieces = exchange(pieces)
    forwarded = [
        lax.ppermute(array, "ctx", shift_pairs(SHIFTS[0] if n == 0 else SHIFTS[PARTNER + n - 1]))
        for n, array in enumerate(outgoing)
    ]
    out = attend(
        plan, me_ref, queries, keys, values, other_keys, other_values, arrived, forwarded, pieces
    )
    return lax.cond(
        plan[ROW_LEFT, 0] > 0,
        lambda: full_attention(queries, keys, values, chosen_all, me),
        lambda: out,
    )


def solution(mesh):
    placed = (P("ctx", None), P("ctx", None), P("ctx", None), P("ctx", None, None))
    return jax.shard_map(
        body, mesh=mesh, in_specs=placed, out_specs=P("ctx", None), check_vma=False
    )
```

time: 724 us -> 1090 us (1.51)
  the two profiles are of different devices: /device:TPU:102 before, /device:TPU:7 now
where the time goes in v1:
time: 1090 us
  Pallas kernels  774 us (71%)
  blocking collectives  239 us (22%)
  starting transfers between devices  28.6 us (3%)
  waiting for transfers between devices  24.9 us (2%)
  local copies, waits for them, and re-layouts  19 us (2%)
    pallas_call x1, Pallas kernels, pack(): pl.pallas_call(pack_kernel, in_specs=[SMEM, SMEM, ANY, ANY, ANY, ANY], ou...  544 us
    all_to_all x1, blocking collectives, exchange(): lax.all_to_all(array, 'ctx', 0, 0, axis_index_groups=LANES, tiled=True)  207 us
    pallas_call x1, Pallas kernels, forward(): pl.pallas_call(forward_kernel, in_specs=[SMEM, SMEM, ANY], out_specs=[ANY...  179 us
    pallas_call x1, Pallas kernels, attend(): pl.pallas_call(attend_kernel, grid=(HEADS,), in_specs=[SMEM, SMEM, block,...  44.9 us
    all_gather x1, blocking collectives, body(): lax.all_gather(chosen.reshape(1, 3 * HEADS), 'ctx', axis=0, tiled=True)  32.5 us
    ppermute x13, waiting for transfers between devices, body(): lax.ppermute(array, 'ctx', shift_pairs(SHIFTS[0] if n == 0 else SHIFTS[PA...  24.8 us
  transfers between devices with their start and end apart: 16, of which 6 were waited for; matrix products, arithmetic and copies ran while one was open for 0% of the time, Pallas kernels for 0%

profile of v1, /device:TPU:7, one launch (start us, length us, event | category | flops | bytes accessed | tf_op | source)
XLA Modules:
  0.0 1086.5 jit_solution(4672246516192664097)
XLA Ops:
  0.0 0.7 collective-permute-start
  0.7 0.0 collective-permute-start.1
  0.7 0.8 copy.29
  1.4 0.1 reshape.98
  1.5 32.5 %all-gather = s32[128,1,48]{2,1,0:T(1,128)S(1)} all-gather(s32[1,1,48]{2,1,0:T(1,128)S(1)} %reshape.98), channel_id=1, replica_groups=mesh['ctx'=128] {'ctx'}, dimensions={0}, use_global_device_ids=true | all-gather | bytes 24768 | tf_op jit(solution)/shard_map/all_gather | solution.py:469
  34.0 0.1 copy.30
  34.1 5.4 plan.1
  39.5 0.0 collective-permute-done.other_keys
  39.5 0.0 collective-permute-done.1.other_values
  39.5 1.3 copy-done.20
  40.8 544.2 %pack.1 = bf16[64,1088,128]{2,1,0:T(8,128)(2,1)} custom-call(s32[288,128]{1,0:T(8,128)} %plan.1, s32[1]{0:T(128)} %bitcast.13.me_ref, bf16[512,2048]{1,0:T(8,128)(2,1)} %own_key.1, bf16[512,2048]{1,0:T(8,128)(2,1)} %own_value.1, bf16[512,2048]{1,0:T(8,128)(2,1)} %copy-done.20, bf16[512,2048]{1,0:T(8,128)(2,1)} %collective-permute-done.1.other_values), custom_call_target="tpu_custom_call" | custom-call | tf_op jit(solution)/shard_map/pack/pallas_call | solution.py:215
  585.0 0.0 copy-done.22
  585.0 207.0 %all_to_all.19.arrived = bf16[64,1088,128]{2,1,0:T(8,128)(2,1)} all-to-all(bf16[64,1088,128]{2,1,0:T(8,128)(2,1)} %pack.1), channel_id=1, replica_groups={{0,2,4,6,8,10,12,14,16,18,20,22,24,26,28,30,32,34,36,38,40,42,44,46,48,..., dimensions={0} | all-to-all | bytes 35651584 | tf_op jit(solution)/shard_map/all_to_all | solution.py:434
  792.0 179.3 %forward.1 = (bf16[64,64,128]{2,1,0:T(8,128)(2,1)}, bf16[6,1024,128]{2,1,0:T(8,128)(2,1)}, bf16[1,1024,128]{2,1,0:T(8,128)(2,1)}, bf16[1,1024,128]{2,1,0:T(8,128...) custom-call(s32[288,128]{1,0:T(8,128)} %plan.1, ...), custom_call_target="tpu_custom_call" | custom-call | tf_op jit(solution)/shard_map/forward/pallas_call | solution.py:255
  971.3 1.0 collective-permute-start.2
  972.3 12.7 %all-to-all-start.3 = ((bf16[64,64,128]{2,1,0:T(8,128)(2,1)}), bf16[64,64,128]{2,1,0:T(8,128)(2,1)S(1)}, u32[]{:S(2)}, u32[]{:S(2)}) async-start(bf16[64,64,128]{2,1,0:T(8,128)(2,1)} %get-tuple-element.177), calls=%async_computation.3 | async-start | bytes 2097152 | tf_op jit(solution)/shard_map/all_to_all | solution.py:434
  985.0 0.7 collective-permute-start.10
  985.7 2.5 collective-permute-start.11
  988.2 0.7 collective-permute-start.12
  988.9 0.9 collective-permute-start.13
  989.8 13.7 %collective-permute-done.10.rest_8_ = bf16[1,1024,128]{2,1,0:T(8,128)(2,1)S(1)} collective-permute-done((bf16[1,1024,128]{2,1,0:T(8,128)(2,1)}, bf16[1,1024,128]{2,1,0:T(8,128)(2,1)S(1)}, u32[]{:S(2)}, u32[]{:S(2)}) %collective-permute-start.10) | collective-permute-done | bytes 262176 | tf_op jit(solution)/shard_map/ppermute | solution.py:476
  1003.5 0.7 collective-permute-start.14
  1004.3 0.0 collective-permute-done.11.rest_9_
  1004.3 2.7 collective-permute-start.3
  1006.9 2.8 collective-permute-done.12.rest_10_
  1009.8 2.6 collective-permute-start.4
  1012.3 0.0 collective-permute-done.13.rest_11_
  1012.4 0.7 copy-done.1
  1013.1 0.0 collective-permute-start.5
  1013.1 0.0 collective-permute-done.14.rest_12_
  1013.1 0.7 copy-done.3
  1013.8 0.7 collective-permute-start.6
  1014.5 0.0 collective-permute-done.3.rest_1_
  1014.5 0.7 copy-done.5
  1015.2 0.5 collective-permute-start.7
  1015.7 2.9 collective-permute-done.4.rest_2_
  1018.6 0.7 copy-done.7
  1019.2 1.4 collective-permute-start.8
  1020.7 1.2 collective-permute-done.5.rest_3_
  1021.9 0.7 copy-done.9
  1022.6 0.8 collective-permute-start.9
  1023.4 0.6 slice.12
  1024.6 3.8 collective-permute-done.6.rest_4_
  1028.5 0.7 copy-done.11
  1029.1 0.0 collective-permute-done.7.rest_5_
  1029.1 0.7 copy-done.13
  1029.9 0.4 collective-permute-done.8.rest_6_
  1030.3 0.7 copy-done.15
  1031.0 0.0 collective-permute-done.9.rest_7_
  1031.0 0.7 copy-done.17
  1031.7 0.0 all-to-all-done.3.rest_13_
  1031.7 0.0 collective-permute-done.2.rest_0_
  1031.7 0.9 copy-done.2
  1032.7 0.9 copy-done.4
  1033.6 0.9 copy-done.6
  1034.6 0.9 copy-done.8
  1035.5 0.9 copy-done.10
  1036.5 0.9 copy-done.12
  1037.4 0.9 copy-done.14
  1038.4 0.9 copy-done.16
  1039.3 0.9 copy-done.18
  1040.3 44.9 %attend.1 = bf16[512,2048]{1,0:T(8,128)(2,1)S(1)} custom-call(s32[288,128]{1,0:T(8,128)S(1)} %copy-done, s32[1]{0:T(128)} %bitcast.13.me_ref, bf16[512,2048]{1,0:T(8,128)(2,1)} %query.1, bf16[512,2048]{1,0:T(8,128)(2,1)} %own_key.1, bf16[512,2048]{1,0:T(8,128)(2,1)} %own_value.1, bf16[512,2048]{1,0:T(8,128)(2,1)} %copy-done.20, ...), custom_call_target="tpu_custom_call" | custom-call | tf_op jit(solution)/shard_map/attend/pallas_call | solution.py:411
  1085.2 0.0 copy-start.21
  1085.2 1.3 copy-done.21
  (23 shorter events, 0.0 us)
Async XLA Ops:
  0.0 39.5 %collective-permute-start = (bf16[512,2048]{1,0:T(8,128)(2,1)}, bf16[512,2048]{1,0:T(8,128)(2,1)S(1)}, u32[]{:S(2)}, u32[]{:S(2)}) collective-permute-start(bf16[512,2048]{1,0:T(8,128)(2,1)} %own_key.1), channel_id=1, source_target_pairs={{0,1},{1,0},{2,3},{3,2},{4,5},{5,4},{6,7},{7,6},{8,9},{9,8},{10,11... | collective-permute-start | bytes 6291464 | tf_op jit(solution)/shard_map/ppermute | solution.py:467
  0.7 38.8 %collective-permute-start.1 = (bf16[512,2048]{1,0:T(8,128)(2,1)}, bf16[512,2048]{1,0:T(8,128)(2,1)}, u32[]{:S(2)}, u32[]{:S(2)}) collective-permute-start(bf16[512,2048]{1,0:T(8,128)(2,1)} %own_value.1), channel_id=1, source_target_pairs={{0,1},{1,0},{2,3},{3,2},{4,5},{5,4},{6,7},{7,6},{8,9},{9,8},{10,11... | collective-permute-start | bytes 6291464 | tf_op jit(solution)/shard_map/ppermute | solution.py:468
  34.1 551.0 %copy-start.22 = (s32[128,1,48]{0,2,1:T(8,128)}, s32[128,1,48]{0,2,1:T(8,128)S(1)}, u32[]{:S(2)}) copy-start(s32[128,1,48]{0,2,1:T(8,128)S(1)} %copy.30) | copy-start | bytes 73732
  39.5 1.3 copy-start.20
  792.0 231.3 %copy-start = (s32[288,128]{1,0:T(8,128)S(1)}, s32[288,128]{1,0:T(8,128)}, u32[]{:S(2)}) copy-start(s32[288,128]{1,0:T(8,128)} %plan.1) | copy-start | bytes 442372
  971.3 60.4 %collective-permute-start.2 = (bf16[6,1024,128]{2,1,0:T(8,128)(2,1)}, bf16[6,1024,128]{2,1,0:T(8,128)(2,1)S(1)}, u32[]{:S(2)}, u32[]{:S(2)}) collective-permute-start(bf16[6,1024,128]{2,1,0:T(8,128)(2,1)} %get-tuple-element.164), channel_id=1, source_target_pairs={{1,0},{0,1},{3,2},{2,3},{5,4},{4,5},{7,6},{6,7},{9,8},{8,9},{11,10... | collective-permute-start | bytes 4718600 | tf_op jit(solution)/shard_map/ppermute | solution.py:476
  972.3 59.4 %all-to-all-start.3 = ((bf16[64,64,128]{2,1,0:T(8,128)(2,1)}), bf16[64,64,128]{2,1,0:T(8,128)(2,1)S(1)}, u32[]{:S(2)}, u32[]{:S(2)}) async-start(bf16[64,64,128]{2,1,0:T(8,128)(2,1)} %get-tuple-element.177), calls=%async_computation.3 | async-start | bytes 2097152 | tf_op jit(solution)/shard_map/all_to_all | solution.py:434
  985.0 18.5 %collective-permute-start.10 = (bf16[1,1024,128]{2,1,0:T(8,128)(2,1)}, bf16[1,1024,128]{2,1,0:T(8,128)(2,1)S(1)}, u32[]{:S(2)}, u32[]{:S(2)}) collective-permute-start(bf16[1,1024,128]{2,1,0:T(8,128)(2,1)} %get-tuple-element.172), channel_id=1, source_target_pairs={{25,0},{24,1},{27,2},{26,3},{29,4},{28,5},{31,6},{30,7},{1,8},{0,9... | collective-permute-start | bytes 786440 | tf_op jit(solution)/shard_map/ppermute | solution.py:476
  985.7 18.5 %collective-permute-start.11 = (bf16[1,1024,128]{2,1,0:T(8,128)(2,1)}, bf16[1,1024,128]{2,1,0:T(8,128)(2,1)S(1)}, u32[]{:S(2)}, u32[]{:S(2)}) collective-permute-start(bf16[1,1024,128]{2,1,0:T(8,128)(2,1)} %get-tuple-element.173), channel_id=1, source_target_pairs={{2,0},{3,1},{4,2},{5,3},{6,4},{7,5},{0,6},{1,7},{10,8},{11,9},{12,... | collective-permute-start | bytes 786440 | tf_op jit(solution)/shard_map/ppermute | solution.py:476
  988.2 21.5 %collective-permute-start.12 = (bf16[1,1024,128]{2,1,0:T(8,128)(2,1)}, bf16[1,1024,128]{2,1,0:T(8,128)(2,1)S(1)}, u32[]{:S(2)}, u32[]{:S(2)}) collective-permute-start(bf16[1,1024,128]{2,1,0:T(8,128)(2,1)} %get-tuple-element.174), channel_id=1, source_target_pairs={{3,0},{2,1},{5,2},{4,3},{7,4},{6,5},{1,6},{0,7},{11,8},{10,9},{13,... | collective-permute-start | bytes 786440 | tf_op jit(solution)/shard_map/ppermute | solution.py:476
  988.9 23.5 %collective-permute-start.13 = (bf16[1,1024,128]{2,1,0:T(8,128)(2,1)}, bf16[1,1024,128]{2,1,0:T(8,128)(2,1)S(1)}, u32[]{:S(2)}, u32[]{:S(2)}) collective-permute-start(bf16[1,1024,128]{2,1,0:T(8,128)(2,1)} %get-tuple-element.175), channel_id=1, source_target_pairs={{6,0},{7,1},{0,2},{1,3},{2,4},{3,5},{4,6},{5,7},{14,8},{15,9},{8,1... | collective-permute-start | bytes 786440 | tf_op jit(solution)/shard_map/ppermute | solution.py:476
  1003.5 9.6 collective-permute-start.14
  1004.3 10.2 collective-permute-start.3
  1009.8 8.8 collective-permute-start.4
  1012.4 0.7 copy-start.1
  1013.1 8.8 collective-permute-start.5
  1013.1 0.7 copy-start.3
  1013.8 14.6 %collective-permute-start.6 = (bf16[1,1024,128]{2,1,0:T(8,128)(2,1)}, bf16[1,1024,128]{2,1,0:T(8,128)(2,1)S(1)}, u32[]{:S(2)}, u32[]{:S(2)}) collective-permute-start(bf16[1,1024,128]{2,1,0:T(8,128)(2,1)} %get-tuple-element.168), channel_id=1, source_target_pairs={{97,0},{96,1},{99,2},{98,3},{101,4},{100,5},{103,6},{102,7},{105,8... | collective-permute-start | bytes 786440 | tf_op jit(solution)/shard_map/ppermute | solution.py:476
  1014.5 0.7 copy-start.5
  1015.2 14.0 %collective-permute-start.7 = (bf16[1,1024,128]{2,1,0:T(8,128)(2,1)}, bf16[1,1024,128]{2,1,0:T(8,128)(2,1)S(1)}, u32[]{:S(2)}, u32[]{:S(2)}) collective-permute-start(bf16[1,1024,128]{2,1,0:T(8,128)(2,1)} %get-tuple-element.169), channel_id=1, source_target_pairs={{8,0},{9,1},{10,2},{11,3},{12,4},{13,5},{14,6},{15,7},{16,8},{17,9... | collective-permute-start | bytes 786440 | tf_op jit(solution)/shard_map/ppermute | solution.py:476
  1018.6 0.7 copy-start.7
  1019.2 11.0 %collective-permute-start.8 = (bf16[1,1024,128]{2,1,0:T(8,128)(2,1)}, bf16[1,1024,128]{2,1,0:T(8,128)(2,1)S(1)}, u32[]{:S(2)}, u32[]{:S(2)}) collective-permute-start(bf16[1,1024,128]{2,1,0:T(8,128)(2,1)} %get-tuple-element.170), channel_id=1, source_target_pairs={{9,0},{8,1},{11,2},{10,3},{13,4},{12,5},{15,6},{14,7},{17,8},{16,9... | collective-permute-start | bytes 786440 | tf_op jit(solution)/shard_map/ppermute | solution.py:476
  1021.9 0.7 copy-start.9
  1022.6 8.4 collective-permute-start.9
  1028.4 0.7 copy-start.11
  1029.1 0.7 copy-start.13
  1030.3 0.7 copy-start.15
  1031.0 0.7 copy-start.17
  1031.7 1.0 copy-start.2
  1032.7 0.9 copy-start.4
  1033.6 0.9 copy-start.6
  1034.6 0.9 copy-start.8
  1035.5 0.9 copy-start.10
  1036.5 0.9 copy-start.12
  1037.4 0.9 copy-start.14
  1038.4 0.9 copy-start.16
  1039.3 0.9 copy-start.18
  1085.2 1.3 copy-start.21

commit v2 on v1

--- a/solution.py
+++ b/solution.py
@@ -205,6 +205,8 @@
 
 ANY = pl.BlockSpec(memory_space=pl.ANY)
 SMEM = pl.BlockSpec(memory_space=pltpu.SMEM)
+VMEM = pl.BlockSpec(memory_space=pltpu.VMEM)
+BIG = pltpu.CompilerParams(vmem_limit_bytes=48 * 1024 * 1024)
 
 
 def tiles(count):
@@ -214,10 +216,11 @@
 def pack(plan, me, keys, values, other_keys, other_values):
     return pl.pallas_call(
         pack_kernel,
-        in_specs=[SMEM, SMEM, ANY, ANY, ANY, ANY],
+        in_specs=[SMEM, SMEM, VMEM, VMEM, VMEM, VMEM],
         out_specs=ANY,
         out_shape=jax.ShapeDtypeStruct((CHIPS, SLOT_ROWS, HEAD), jnp.bfloat16),
         scratch_shapes=[pltpu.SemaphoreType.DMA],
+        compiler_params=BIG,
         name="pack",
     )(plan, me, keys, values, other_keys, other_values)
 
@@ -255,11 +258,12 @@
     return pl.pallas_call(
         forward_kernel,
         in_specs=[SMEM, SMEM, ANY],
-        out_specs=[ANY] * (KINDS - PARTNER + 2),
+        out_specs=[VMEM] * (KINDS - PARTNER + 2),
         out_shape=[jax.ShapeDtypeStruct((CHIPS, SPARE * PIECE, HEAD), jnp.bfloat16)]
         + [tiles(PARTNER)]
         + [tiles(1)] * (KINDS - PARTNER),
         scratch_shapes=[pltpu.SemaphoreType.DMA((KINDS + 1,))],
+        compiler_params=BIG,
         name="forward",
     )(plan, me, arrived)
 
@@ -421,7 +425,7 @@
             pltpu.VMEM((2, 3, BLOCK, 2 * HEAD), jnp.bfloat16),
             pltpu.SemaphoreType.DMA((2, 3, 2)),
         ],
-        compiler_params=pltpu.CompilerParams(vmem_limit_bytes=48 * 1024 * 1024),
+        compiler_params=BIG,
         name="attend",
     )(plan, me, queries, keys, values, other_keys, other_values, arrived, *forwarded, pieces)
 
@@ -466,7 +470,8 @@
     me_ref = me.reshape(1)
     other_keys = lax.ppermute(keys, "ctx", SWAP)
     other_values = lax.ppermute(values, "ctx", SWAP)
-    chosen_all = lax.all_gather(chosen.reshape(1, 3 * HEADS), "ctx", axis=0, tiled=True)
+    spread = jnp.broadcast_to(chosen.reshape(1, 3 * HEADS), (DEVICES, 3 * HEADS))
+    chosen_all = lax.all_to_all(spread, "ctx", 0, 0, tiled=True)
     plan = make_plan(chosen_all.T)
     send = pack(plan, me_ref, keys, values, other_keys, other_values)
     arrived = exchange(send)

time: 1090 us -> 388 us (0.36)
  Pallas kernels: 774 us -> 75.5 us
  blocking collectives: 239 us -> 203 us
  starting transfers between devices: 28.6 us -> 45.6 us
    pallas_call x2, Pallas kernels: 723 us -> 25.1 us  [the longest x1 15.6 us: forward(): pl.pallas_call(forward_kernel, in_specs=[SMEM, SMEM, ANY], out_specs=[VME...]
    all_gather x1 -> x0, blocking collectives: 32.5 us -> none  [body(): lax.all_gather(chosen.reshape(1, 3 * HEADS), 'ctx', axis=0, tiled=True)]
    unnamed x46 -> x69, local copies, waits for them, and re-layouts: 18.4 us -> 26.1 us
  transfers between devices with their start and end apart: 16 -> 17, of which waited for: 6 -> 7; matrix products, arithmetic and copies ran while one was open for 0% -> 1% of each run, Pallas kernels for 0% -> 1%
where the time goes in v2:
time: 388 us; the launch traced here: 385 us
  blocking collectives  203 us (52%)
  Pallas kernels  75.5 us (19%)
  starting transfers between devices  45.6 us (12%)
  waiting for transfers between devices  32.8 us (8%)
  local copies, waits for them, and re-layouts  27.5 us (7%)
    all_to_all x1, blocking collectives, exchange(): lax.all_to_all(array, 'ctx', 0, 0, axis_index_groups=LANES, tiled=True)  203 us
    pallas_call x1, Pallas kernels, attend(): pl.pallas_call(attend_kernel, grid=(HEADS,), in_specs=[SMEM, SMEM, block,...  45 us
    unnamed x69, local copies, waits for them, and re-layouts  26.1 us
    ppermute x13, waiting for transfers between devices, body(): lax.ppermute(array, 'ctx', shift_pairs(SHIFTS[0] if n == 0 else SHIFTS[PA...  24.9 us
    all_to_all x1, starting transfers between devices, exchange(): lax.all_to_all(array, 'ctx', 0, 0, axis_index_groups=LANES, tiled=True)  18.9 us
    pallas_call x1, Pallas kernels, forward(): pl.pallas_call(forward_kernel, in_specs=[SMEM, SMEM, ANY], out_specs=[VME...  15.6 us
    ppermute x13, starting transfers between devices, body(): lax.ppermute(array, 'ctx', shift_pairs(SHIFTS[0] if n == 0 else SHIFTS[PA...  15.4 us
    all_to_all x1, starting transfers between devices, body(): chosen_all = lax.all_to_all(spread, 'ctx', 0, 0, tiled=True)  10.6 us
  transfers between devices with their start and end apart: 17, of which 7 were waited for; matrix products, arithmetic and copies ran while one was open for 1% of the time, Pallas kernels for 1%

profile of v2, /device:TPU:7, one launch (start us, length us, event | category | flops | bytes accessed | tf_op | source)
XLA Modules:
  0.0 385.2 jit_solution(16814337598097223740)
XLA Ops:
  0.0 0.7 collective-permute-start
  0.7 0.8 copy.27
  1.4 0.1 broadcast_in_dim.55
  1.5 0.7 broadcast_in_dim.56
  2.2 10.6 %all-to-all-start.2 = ((s32[128,1,48]{2,1,0:T(1,128)}), s32[128,1,48]{2,1,0:T(1,128)S(1)}, u32[]{:S(2)}, u32[]{:S(2)}) async-start(s32[128,1,48]{2,1,0:T(1,128)} %broadcast_in_dim.56), calls=%async_computation.2 | async-start | bytes 131072 | tf_op jit(solution)/shard_map/all_to_all | solution.py:474
  12.8 7.9 %all-to-all-done.2 = s32[128,1,48]{2,1,0:T(1,128)S(1)} async-done(((s32[128,1,48]{2,1,0:T(1,128)}), s32[128,1,48]{2,1,0:T(1,128)S(1)}, u32[]{:S(2)}, u32[]{:S(2)}) %all-to-all-start.2) | async-done | bytes 24608 | tf_op jit(solution)/shard_map/all_to_all | solution.py:474
  20.7 0.1 copy.28
  20.8 5.4 %plan.1 = s32[288,128]{1,0:T(8,128)} custom-call(s32[48,128]{1,0:T(8,128)S(1)} %bitcast.60), custom_call_target="tpu_custom_call" | custom-call | tf_op jit(solution)/shard_map/plan/pallas_call | solution.py:140
  26.2 1.0 copy-done.1
  27.2 9.5 %pack.1 = bf16[64,1088,128]{2,1,0:T(8,128)(2,1)} custom-call(s32[288,128]{1,0:T(8,128)S(1)} %copy-done.1, s32[1]{0:T(128)} %bitcast.13.me_ref, bf16[512,2048]{1,0:T(8,128)(2,1)} %own_key.1, bf16[512,2048]{1,0:T(8,128)(2,1)} %own_value.1, bf16[512,2048]{1,0:T(8,128)(2,1)S(1)} %collective-permute-done.other_keys, ...), custom_call_target="tpu_custom_call" | custom-call | tf_op jit(solution)/shard_map/pack/pallas_call | solution.py:217
  36.8 203.0 %all_to_all.28.arrived = bf16[64,1088,128]{2,1,0:T(8,128)(2,1)} all-to-all(bf16[64,1088,128]{2,1,0:T(8,128)(2,1)} %pack.1), channel_id=1, replica_groups={{0,2,4,6,8,10,12,14,16,18,20,22,24,26,28,30,32,34,36,38,40,42,44,46,48,..., dimensions={0} | all-to-all | bytes 35651584 | tf_op jit(solution)/shard_map/all_to_all | solution.py:438
  239.9 15.6 %forward.1 = (bf16[64,64,128]{2,1,0:T(8,128)(2,1)S(1)}, bf16[6,1024,128]{2,1,0:T(8,128)(2,1)}, bf16[1,1024,128]{2,1,0:T(8,128)(2,1)S(1)}, bf16[1,1024,128]{2,1,0...) custom-call(s32[288,128]{1,0:T(8,128)S(1)} %copy-done.1, ...), custom_call_target="tpu_custom_call" | custom-call | tf_op jit(solution)/shard_map/forward/pallas_call | solution.py:258
  255.4 1.0 copy-done.3
  256.4 0.7 copy-done.22
  257.1 0.7 copy-done.23
  257.8 0.7 copy-done.24
  258.6 0.7 copy-done.25
  259.3 0.7 copy-done.26
  260.0 0.7 copy-done.27
  260.7 0.7 copy-done.28
  261.4 0.7 copy-done.29
  262.1 0.7 copy-done.30
  262.8 0.7 copy-done.31
  263.5 1.3 collective-permute-start.2
  264.7 18.9 %all-to-all-start.4 = ((bf16[64,64,128]{2,1,0:T(8,128)(2,1)}), bf16[64,64,128]{2,1,0:T(8,128)(2,1)S(1)}, u32[]{:S(2)}, u32[]{:S(2)}) async-start(bf16[64,64,128]{2,1,0:T(8,128)(2,1)} %copy-done.3), calls=%async_computation.4 | async-start | bytes 2097152 | tf_op jit(solution)/shard_map/all_to_all | solution.py:438
  283.6 0.7 collective-permute-start.10
  284.3 2.5 collective-permute-start.11
  286.8 0.7 collective-permute-start.12
  287.5 0.9 collective-permute-start.13
  288.4 13.7 %collective-permute-done.10.rest_8_ = bf16[1,1024,128]{2,1,0:T(8,128)(2,1)S(1)} collective-permute-done((bf16[1,1024,128]{2,1,0:T(8,128)(2,1)}, bf16[1,1024,128]{2,1,0:T(8,128)(2,1)S(1)}, u32[]{:S(2)}, u32[]{:S(2)}) %collective-permute-start.10) | collective-permute-done | bytes 262176 | tf_op jit(solution)/shard_map/ppermute | solution.py:481
  302.1 0.8 collective-permute-start.14
  302.9 2.7 collective-permute-start.3
  305.6 2.8 collective-permute-done.12.rest_10_
  308.4 2.6 collective-permute-start.4
  311.0 0.7 copy-done.4
  311.7 0.7 copy-done.6
  312.4 0.7 collective-permute-start.6
  313.1 0.7 copy-done.8
  313.8 0.5 collective-permute-start.7
  314.3 3.0 collective-permute-done.4.rest_2_
  317.2 0.7 copy-done.10
  317.9 1.4 collective-permute-start.8
  319.3 1.2 collective-permute-done.5.rest_3_
  320.5 0.7 copy-done.12
  321.2 0.8 collective-permute-start.9
  322.0 0.6 slice.12
  323.2 3.8 collective-permute-done.6.rest_4_
  327.0 0.7 copy-done.14
  327.8 0.7 copy-done.16
  328.5 0.4 collective-permute-done.8.rest_6_
  328.8 0.7 copy-done.18
  329.6 0.7 copy-done.20
  330.3 0.9 copy-done.5
  331.2 0.9 copy-done.7
  332.2 0.9 copy-done.9
  333.1 0.9 copy-done.11
  334.1 0.9 copy-done.13
  335.0 0.9 copy-done.15
  336.0 0.9 copy-done.17
  336.9 0.9 copy-done.19
  337.9 0.9 copy-done.21
  338.8 45.0 %attend.1 = bf16[512,2048]{1,0:T(8,128)(2,1)S(1)} custom-call(s32[288,128]{1,0:T(8,128)S(1)} %copy-done.2, s32[1]{0:T(128)} %bitcast.13.me_ref, bf16[512,2048]{1,0:T(8,128)(2,1)} %query.1, bf16[512,2048]{1,0:T(8,128)(2,1)} %own_key.1, bf16[512,2048]{1,0:T(8,128)(2,1)} %own_value.1, bf16[512,2048]{1,0:T(8,128)(2,1)} %copy-done, ...), custom_call_target="tpu_custom_call" | custom-call | tf_op jit(solution)/shard_map/attend/pallas_call | solution.py:415
  383.8 0.0 copy-start.33
  383.9 1.3 copy-done.33
  (49 shorter events, 0.1 us)
Async XLA Ops:
  0.0 26.2 %collective-permute-start = (bf16[512,2048]{1,0:T(8,128)(2,1)}, bf16[512,2048]{1,0:T(8,128)(2,1)S(1)}, u32[]{:S(2)}, u32[]{:S(2)}) collective-permute-start(bf16[512,2048]{1,0:T(8,128)(2,1)} %own_key.1), channel_id=1, source_target_pairs={{0,1},{1,0},{2,3},{3,2},{4,5},{5,4},{6,7},{7,6},{8,9},{9,8},{10,11... | collective-permute-start | bytes 6291464 | tf_op jit(solution)/shard_map/ppermute | solution.py:471
  0.7 25.5 %collective-permute-start.1 = (bf16[512,2048]{1,0:T(8,128)(2,1)}, bf16[512,2048]{1,0:T(8,128)(2,1)}, u32[]{:S(2)}, u32[]{:S(2)}) collective-permute-start(bf16[512,2048]{1,0:T(8,128)(2,1)} %own_value.1), channel_id=1, source_target_pairs={{0,1},{1,0},{2,3},{3,2},{4,5},{5,4},{6,7},{7,6},{8,9},{9,8},{10,11... | collective-permute-start | bytes 6291464 | tf_op jit(solution)/shard_map/ppermute | solution.py:472
  2.2 18.5 %all-to-all-start.2 = ((s32[128,1,48]{2,1,0:T(1,128)}), s32[128,1,48]{2,1,0:T(1,128)S(1)}, u32[]{:S(2)}, u32[]{:S(2)}) async-start(s32[128,1,48]{2,1,0:T(1,128)} %broadcast_in_dim.56), calls=%async_computation.2 | async-start | bytes 131072 | tf_op jit(solution)/shard_map/all_to_all | solution.py:474
  20.8 16.0 %copy-start.34 = (s32[128,1,48]{0,2,1:T(8,128)}, s32[128,1,48]{0,2,1:T(8,128)S(1)}, u32[]{:S(2)}) copy-start(s32[128,1,48]{0,2,1:T(8,128)S(1)} %copy.28) | copy-start | bytes 73732
  26.2 10.6 %copy-start = (bf16[512,2048]{1,0:T(8,128)(2,1)}, bf16[512,2048]{1,0:T(8,128)(2,1)S(1)}, u32[]{:S(2)}) copy-start(bf16[512,2048]{1,0:T(8,128)(2,1)S(1)} %collective-permute-done.other_keys) | copy-start | bytes 6291460
  26.2 1.1 copy-start.1
  239.8 82.1 %copy-start.2 = (s32[288,128]{1,0:T(8,128)S(1)}, s32[288,128]{1,0:T(8,128)}, u32[]{:S(2)}) copy-start(s32[288,128]{1,0:T(8,128)} %plan.1) | copy-start | bytes 442372
  255.4 1.0 copy-start.3
  256.4 0.7 copy-start.22
  257.1 0.7 copy-start.23
  257.8 0.7 copy-start.24
  258.6 0.7 copy-start.25
  259.3 0.7 copy-start.26
  260.0 0.7 copy-start.27
  260.7 0.7 copy-start.28
  261.4 0.7 copy-start.29
  262.1 0.7 copy-start.30
  262.8 0.7 copy-start.31
  263.5 66.8 %collective-permute-start.2 = (bf16[6,1024,128]{2,1,0:T(8,128)(2,1)}, bf16[6,1024,128]{2,1,0:T(8,128)(2,1)S(1)}, u32[]{:S(2)}, u32[]{:S(2)}) collective-permute-start(bf16[6,1024,128]{2,1,0:T(8,128)(2,1)} %get-tuple-element.164), channel_id=1, source_target_pairs={{1,0},{0,1},{3,2},{2,3},{5,4},{4,5},{7,6},{6,7},{9,8},{8,9},{11,10... | collective-permute-start | bytes 4718600 | tf_op jit(solution)/shard_map/ppermute | solution.py:481
  264.7 65.5 %all-to-all-start.4 = ((bf16[64,64,128]{2,1,0:T(8,128)(2,1)}), bf16[64,64,128]{2,1,0:T(8,128)(2,1)S(1)}, u32[]{:S(2)}, u32[]{:S(2)}) async-start(bf16[64,64,128]{2,1,0:T(8,128)(2,1)} %copy-done.3), calls=%async_computation.4 | async-start | bytes 2097152 | tf_op jit(solution)/shard_map/all_to_all | solution.py:438
  283.6 18.5 %collective-permute-start.10 = (bf16[1,1024,128]{2,1,0:T(8,128)(2,1)}, bf16[1,1024,128]{2,1,0:T(8,128)(2,1)S(1)}, u32[]{:S(2)}, u32[]{:S(2)}) collective-permute-start(bf16[1,1024,128]{2,1,0:T(8,128)(2,1)} %get-tuple-element.172), channel_id=1, source_target_pairs={{25,0},{24,1},{27,2},{26,3},{29,4},{28,5},{31,6},{30,7},{1,8},{0,9... | collective-permute-start | bytes 786440 | tf_op jit(solution)/shard_map/ppermute | solution.py:481
  284.3 18.6 %collective-permute-start.11 = (bf16[1,1024,128]{2,1,0:T(8,128)(2,1)}, bf16[1,1024,128]{2,1,0:T(8,128)(2,1)S(1)}, u32[]{:S(2)}, u32[]{:S(2)}) collective-permute-start(bf16[1,1024,128]{2,1,0:T(8,128)(2,1)} %get-tuple-element.173), channel_id=1, source_target_pairs={{2,0},{3,1},{4,2},{5,3},{6,4},{7,5},{0,6},{1,7},{10,8},{11,9},{12,... | collective-permute-start | bytes 786440 | tf_op jit(solution)/shard_map/ppermute | solution.py:481
  286.8 21.6 %collective-permute-start.12 = (bf16[1,1024,128]{2,1,0:T(8,128)(2,1)}, bf16[1,1024,128]{2,1,0:T(8,128)(2,1)S(1)}, u32[]{:S(2)}, u32[]{:S(2)}) collective-permute-start(bf16[1,1024,128]{2,1,0:T(8,128)(2,1)} %copy-done.31), channel_id=1, source_target_pairs={{3,0},{2,1},{5,2},{4,3},{7,4},{6,5},{1,6},{0,7},{11,8},{10,9},{13,... | collective-permute-start | bytes 786440 | tf_op jit(solution)/shard_map/ppermute | solution.py:481
  287.5 23.5 %collective-permute-start.13 = (bf16[1,1024,128]{2,1,0:T(8,128)(2,1)}, bf16[1,1024,128]{2,1,0:T(8,128)(2,1)S(1)}, u32[]{:S(2)}, u32[]{:S(2)}) collective-permute-start(bf16[1,1024,128]{2,1,0:T(8,128)(2,1)} %copy-done.30), channel_id=1, source_target_pairs={{6,0},{7,1},{0,2},{1,3},{2,4},{3,5},{4,6},{5,7},{14,8},{15,9},{8,1... | collective-permute-start | bytes 786440 | tf_op jit(solution)/shard_map/ppermute | solution.py:481
  302.1 9.6 %collective-permute-start.14 = (bf16[1,1024,128]{2,1,0:T(8,128)(2,1)}, bf16[1,1024,128]{2,1,0:T(8,128)(2,1)S(1)}, u32[]{:S(2)}, u32[]{:S(2)}) collective-permute-start(bf16[1,1024,128]{2,1,0:T(8,128)(2,1)} %copy-done.29), channel_id=1, source_target_pairs={{7,0},{6,1},{1,2},{0,3},{3,4},{2,5},{5,6},{4,7},{15,8},{14,9},{9,1... | collective-permute-start | bytes 786440 | tf_op jit(solution)/shard_map/ppermute | solution.py:481
  302.9 10.2 %collective-permute-start.3 = (bf16[1,1024,128]{2,1,0:T(8,128)(2,1)}, bf16[1,1024,128]{2,1,0:T(8,128)(2,1)S(1)}, u32[]{:S(2)}, u32[]{:S(2)}) collective-permute-start(bf16[1,1024,128]{2,1,0:T(8,128)(2,1)} %copy-done.28), channel_id=1, source_target_pairs={{32,0},{33,1},{34,2},{35,3},{36,4},{37,5},{38,6},{39,7},{40,8},{41... | collective-permute-start | bytes 786440 | tf_op jit(solution)/shard_map/ppermute | solution.py:481
  308.4 8.8 %collective-permute-start.4 = (bf16[1,1024,128]{2,1,0:T(8,128)(2,1)}, bf16[1,1024,128]{2,1,0:T(8,128)(2,1)S(1)}, u32[]{:S(2)}, u32[]{:S(2)}) collective-permute-start(bf16[1,1024,128]{2,1,0:T(8,128)(2,1)} %copy-done.27), channel_id=1, source_target_pairs={{33,0},{32,1},{35,2},{34,3},{37,4},{36,5},{39,6},{38,7},{41,8},{40... | collective-permute-start | bytes 786440 | tf_op jit(solution)/shard_map/ppermute | solution.py:481
  311.0 0.7 copy-start.4
  311.7 8.8 %collective-permute-start.5 = (bf16[1,1024,128]{2,1,0:T(8,128)(2,1)}, bf16[1,1024,128]{2,1,0:T(8,128)(2,1)S(1)}, u32[]{:S(2)}, u32[]{:S(2)}) collective-permute-start(bf16[1,1024,128]{2,1,0:T(8,128)(2,1)} %copy-done.26), channel_id=1, source_target_pairs={{96,0},{97,1},{98,2},{99,3},{100,4},{101,5},{102,6},{103,7},{104,8... | collective-permute-start | bytes 786440 | tf_op jit(solution)/shard_map/ppermute | solution.py:481
  311.7 0.7 copy-start.6
  312.4 14.7 %collective-permute-start.6 = (bf16[1,1024,128]{2,1,0:T(8,128)(2,1)}, bf16[1,1024,128]{2,1,0:T(8,128)(2,1)S(1)}, u32[]{:S(2)}, u32[]{:S(2)}) collective-permute-start(bf16[1,1024,128]{2,1,0:T(8,128)(2,1)} %copy-done.25), channel_id=1, source_target_pairs={{97,0},{96,1},{99,2},{98,3},{101,4},{100,5},{103,6},{102,7},{105,8... | collective-permute-start | bytes 786440 | tf_op jit(solution)/shard_map/ppermute | solution.py:481
  313.1 0.7 copy-start.8
  313.8 14.0 %collective-permute-start.7 = (bf16[1,1024,128]{2,1,0:T(8,128)(2,1)}, bf16[1,1024,128]{2,1,0:T(8,128)(2,1)S(1)}, u32[]{:S(2)}, u32[]{:S(2)}) collective-permute-start(bf16[1,1024,128]{2,1,0:T(8,128)(2,1)} %copy-done.24), channel_id=1, source_target_pairs={{8,0},{9,1},{10,2},{11,3},{12,4},{13,5},{14,6},{15,7},{16,8},{17,9... | collective-permute-start | bytes 786440 | tf_op jit(solution)/shard_map/ppermute | solution.py:481
  317.2 0.7 copy-start.10
  317.9 10.9 %collective-permute-start.8 = (bf16[1,1024,128]{2,1,0:T(8,128)(2,1)}, bf16[1,1024,128]{2,1,0:T(8,128)(2,1)S(1)}, u32[]{:S(2)}, u32[]{:S(2)}) collective-permute-start(bf16[1,1024,128]{2,1,0:T(8,128)(2,1)} %copy-done.23), channel_id=1, source_target_pairs={{9,0},{8,1},{11,2},{10,3},{13,4},{12,5},{15,6},{14,7},{17,8},{16,9... | collective-permute-start | bytes 786440 | tf_op jit(solution)/shard_map/ppermute | solution.py:481
  320.5 0.7 copy-start.12
  321.2 8.3 %collective-permute-start.9 = (bf16[1,1024,128]{2,1,0:T(8,128)(2,1)}, bf16[1,1024,128]{2,1,0:T(8,128)(2,1)S(1)}, u32[]{:S(2)}, u32[]{:S(2)}) collective-permute-start(bf16[1,1024,128]{2,1,0:T(8,128)(2,1)} %copy-done.22), channel_id=1, source_target_pairs={{24,0},{25,1},{26,2},{27,3},{28,4},{29,5},{30,6},{31,7},{0,8},{1,9... | collective-permute-start | bytes 786440 | tf_op jit(solution)/shard_map/ppermute | solution.py:481
  327.0 0.7 copy-start.14
  327.8 0.7 copy-start.16
  328.8 0.7 copy-start.18
  329.6 0.7 copy-start.20
  330.3 1.0 copy-start.5
  331.2 0.9 copy-start.7
  332.2 0.9 copy-start.9
  333.1 0.9 copy-start.11
  334.1 0.9 copy-start.13
  335.0 0.9 copy-start.15
  336.0 0.9 copy-start.17
  336.9 0.9 copy-start.19
  337.9 0.9 copy-start.21
  383.8 1.3 copy-start.33

commit v3 on v2

--- a/solution.py
+++ b/solution.py
@@ -21,18 +21,19 @@
 KINDS = len(SHIFTS)
 SPARE = 4
 PIECE = 16
+PARTS = 4
 SLOT_ROWS = 2 * BLOCK + SPARE * PIECE
 
 ROW_DIRECT = CHIPS
 ROW_SPARE = ROW_DIRECT + CHIPS
 ROW_FORWARD = ROW_SPARE + CHIPS
-ROW_FORWARD_HEAD = ROW_FORWARD + 32
-ROW_FROM = ROW_FORWARD_HEAD + 32
-ROW_FROM_RANK = ROW_FROM + 8
-ROW_FROM_HEAD = ROW_FROM_RANK + 8
-ROW_PARTNER = ROW_FROM_HEAD + 8
+ROW_FORWARD_HEAD = ROW_FORWARD + KINDS
+ROW_FROM_HEAD = ROW_FORWARD_HEAD + KINDS
+ROW_FROM = ROW_FROM_HEAD + SPARE
+ROW_FROM_RANK = ROW_FROM + SPARE
+ROW_PARTNER = ROW_FROM_RANK + SPARE
 ROW_LEFT = ROW_PARTNER + 1
-ROWS = ROW_PARTNER + 8
+ROWS = -(-(ROW_LEFT + 1) // 8) * 8
 
 
 def through(device, shift):
@@ -206,7 +207,7 @@
 ANY = pl.BlockSpec(memory_space=pl.ANY)
 SMEM = pl.BlockSpec(memory_space=pltpu.SMEM)
 VMEM = pl.BlockSpec(memory_space=pltpu.VMEM)
-BIG = pltpu.CompilerParams(vmem_limit_bytes=48 * 1024 * 1024)
+BIG = pltpu.CompilerParams(vmem_limit_bytes=60 * 1024 * 1024)
 
 
 def tiles(count):
@@ -225,15 +226,18 @@
     )(plan, me, keys, values, other_keys, other_values)
 
 
-def forward_kernel(plan, me_ref, arrived, pieces, *rest):
-    outs, sems = rest[:-1], rest[-1]
+def forward_kernel(plan, me_ref, arrived, *rest):
+    outs, (moving, gathered, sems, out_sems) = rest[:-4], rest[-4:]
     me = me_ref[0]
     core = me % 2
+    loads, stores = [], []
     for kind in range(KINDS):
-        out = outs[0].at[kind] if kind < PARTNER else outs[kind - PARTNER + 1].at[0]
-        pltpu.make_async_copy(
-            arrived.at[plan[ROW_FORWARD + kind, me], pl.ds(0, 2 * BLOCK)], out, sems.at[kind]
-        ).start()
+        out = outs[1].at[kind] if kind < PARTNER else outs[kind - PARTNER + 2].at[0]
+        source = arrived.at[plan[ROW_FORWARD + kind, me], pl.ds(0, 2 * BLOCK)]
+        loads.append(pltpu.make_async_copy(source, moving.at[kind], sems.at[kind]))
+        stores.append(pltpu.make_async_copy(moving.at[kind], out, out_sems.at[kind]))
+    for load in loads:
+        load.start()
 
     def one_dest(dest, carry):
         for index in range(SPARE):
@@ -242,27 +246,37 @@
             row = pl.multiple_of(2 * BLOCK + rank * PIECE, PIECE)
             pltpu.make_async_copy(
                 arrived.at[chip, pl.ds(row, PIECE)],
-                pieces.at[dest, pl.ds(index * PIECE, PIECE)],
+                gathered.at[dest, pl.ds(index * PIECE, PIECE)],
                 sems.at[KINDS],
             ).start()
         return carry
 
     lax.fori_loop(0, CHIPS, one_dest, 0)
-    pltpu.make_async_copy(pieces, pieces, sems.at[KINDS]).wait()
-    for kind in range(KINDS):
-        out = outs[0].at[kind] if kind < PARTNER else outs[kind - PARTNER + 1].at[0]
-        pltpu.make_async_copy(arrived.at[0, pl.ds(0, 2 * BLOCK)], out, sems.at[kind]).wait()
+    for load, store in zip(loads, stores):
+        load.wait()
+        store.start()
+    pltpu.make_async_copy(gathered, gathered, sems.at[KINDS]).wait()
+    last = pltpu.make_async_copy(gathered, outs[0], out_sems.at[KINDS])
+    last.start()
+    for store in stores:
+        store.wait()
+    last.wait()
 
 
 def forward(plan, me, arrived):
     return pl.pallas_call(
         forward_kernel,
         in_specs=[SMEM, SMEM, ANY],
-        out_specs=[VMEM] * (KINDS - PARTNER + 2),
+        out_specs=[ANY] * (KINDS - PARTNER + 2),
         out_shape=[jax.ShapeDtypeStruct((CHIPS, SPARE * PIECE, HEAD), jnp.bfloat16)]
         + [tiles(PARTNER)]
         + [tiles(1)] * (KINDS - PARTNER),
-        scratch_shapes=[pltpu.SemaphoreType.DMA((KINDS + 1,))],
+        scratch_shapes=[
+            pltpu.VMEM((KINDS, 2 * BLOCK, HEAD), jnp.bfloat16),
+            pltpu.VMEM((CHIPS, SPARE * PIECE, HEAD), jnp.bfloat16),
+            pltpu.SemaphoreType.DMA((KINDS + 1,)),
+            pltpu.SemaphoreType.DMA((KINDS + 1,)),
+        ],
         compiler_params=BIG,
         name="forward",
     )(plan, me, arrived)
@@ -274,15 +288,12 @@
     )
 
 
-def attend_kernel(
-    plan, me_ref, query, own_key, own_value, other_keys, other_values, arrived, *rest
-):
-    count = KINDS - PARTNER + 1
-    forwarded, pieces = rest[:count], rest[count]
-    out = rest[count + 1]
-    where, filled, key_buf, value_buf, sems = rest[count + 2 :]
+def attend_kernel(first, last, plan, me_ref, query, own_key, own_value, *rest):
+    other_keys, other_values, arrived = rest[:3]
+    out, state, where, filled, key_buf, value_buf, sems = rest[-7:]
     me = me_ref[0]
     step = pl.program_id(0)
+    head = step + first
 
     def note(head_plus, code):
         @pl.when(head_plus > 0)
@@ -301,41 +312,11 @@
                 pltpu.make_async_copy(source_key, into_key, sems.at[slot, j, 0]).start()
                 pltpu.make_async_copy(source_value, into_value, sems.at[slot, j, 1]).start()
 
-            @pl.when(code < CHIPS)
+            @pl.when((code >= 0) & (code < CHIPS))
             def _():
                 start(arrived.at[code, pl.ds(0, BLOCK)], arrived.at[code, pl.ds(BLOCK, BLOCK)])
 
-            @pl.when((code >= 64) & (code < 64 + PARTNER))
-            def _():
-                ref = forwarded[0].at[code - 64]
-                start(ref.at[pl.ds(0, BLOCK)], ref.at[pl.ds(BLOCK, BLOCK)])
-
-            for kind in range(PARTNER, KINDS):
-
-                @pl.when(code == 64 + kind)
-                def _():
-                    ref = forwarded[kind - PARTNER + 1]
-                    start(ref.at[0, pl.ds(0, BLOCK)], ref.at[0, pl.ds(BLOCK, BLOCK)])
-
-            @pl.when((code >= 96) & (code < 128))
-            def _():
-                from_row = pl.ds(pl.multiple_of((code - 96) * PIECE, PIECE), PIECE)
-
-                def one_piece(piece, carry):
-                    rows = pl.ds(pl.multiple_of(piece * PIECE, PIECE), PIECE)
-                    pltpu.make_async_copy(
-                        pieces.at[2 * piece, from_row], into_key.at[rows], sems.at[slot, j, 0]
-                    ).start()
-                    pltpu.make_async_copy(
-                        pieces.at[2 * piece + 1, from_row],
-                        into_value.at[rows],
-                        sems.at[slot, j, 1],
-                    ).start()
-                    return carry
-
-                lax.fori_loop(0, BLOCK // PIECE, one_piece, 0)
-
-            @pl.when(code == 128)
+            @pl.when(code == CHIPS)
             def _():
                 start(other_keys.at[:, columns(head)], other_values.at[:, columns(head)])
 
@@ -344,7 +325,7 @@
         for h in range(HEADS):
             filled[h] = 0
             for j in range(3):
-                where[h * 3 + j] = 0
+                where[h * 3 + j] = -1
         value_buf[...] = jnp.ones(value_buf.shape, value_buf.dtype)
 
         def direct(chip, carry):
@@ -352,72 +333,81 @@
             return carry
 
         lax.fori_loop(0, CHIPS, direct, 0)
-
-        def moved(kind, carry):
-            note(plan[ROW_FORWARD_HEAD + kind, me], 64 + kind)
-            return carry
-
-        lax.fori_loop(0, KINDS, moved, 0)
-
-        def shared(index, carry):
-            note(plan[ROW_FROM_HEAD + index, me], 96 + index)
-            return carry
-
-        lax.fori_loop(0, SPARE, shared, 0)
-        note(plan[ROW_PARTNER, me], 128)
-        fetch(0, 0)
+        note(plan[ROW_PARTNER, me], CHIPS)
+        fetch(first, 0)
 
     slot = step % 2
 
-    @pl.when(step + 1 < HEADS)
+    @pl.when(head + 1 < last)
     def _():
-        fetch(step + 1, 1 - slot)
-
+        fetch(head + 1, 1 - slot)
+
+    present = jnp.minimum(filled[head], 3)
     for j in range(3):
-        pltpu.make_async_copy(
-            arrived.at[0, pl.ds(0, BLOCK)], key_buf.at[slot, j], sems.at[slot, j, 0]
-        ).wait()
-        pltpu.make_async_copy(
-            arrived.at[0, pl.ds(BLOCK, BLOCK)],
-            value_buf.at[slot, j, :, pl.ds(0, HEAD)],
-            sems.at[slot, j, 1],
-        ).wait()
-
-    rows = 256
-    for part in range(BLOCK // rows):
-        length = (part + 1) * rows
-        q = query[part * rows : length, :]
-        own = scores_of(q, own_key[0:length, :])
-        row_iota = lax.broadcasted_iota(jnp.int32, (rows, length), 0) + part * rows
-        col_iota = lax.broadcasted_iota(jnp.int32, (rows, length), 1)
-        own = jnp.where(col_iota <= row_iota, own, -jnp.inf)
-        others = [scores_of(q, key_buf[slot, j]) for j in range(3)]
-        highest = jnp.max(own, axis=1, keepdims=True)
-        for other in others:
-            highest = jnp.maximum(highest, jnp.max(other, axis=1, keepdims=True))
-        weight = jnp.exp2((own - highest) * SCALE).astype(jnp.bfloat16)
-        ones = jnp.ones((length, HEAD), jnp.bfloat16)
-        total = jnp.dot(
-            weight,
-            jnp.concatenate([own_value[0:length, :], ones], axis=1),
-            preferred_element_type=jnp.float32,
-        )
-        for j, other in enumerate(others):
-            weight = jnp.exp2((other - highest) * SCALE).astype(jnp.bfloat16)
-            total = total + jnp.dot(
-                weight, value_buf[slot, j], preferred_element_type=jnp.float32
+
+        @pl.when(j < present)
+        def _():
+            pltpu.make_async_copy(
+                arrived.at[0, pl.ds(0, BLOCK)], key_buf.at[slot, j], sems.at[slot, j, 0]
+            ).wait()
+            pltpu.make_async_copy(
+                arrived.at[0, pl.ds(BLOCK, BLOCK)],
+                value_buf.at[slot, j, :, pl.ds(0, HEAD)],
+                sems.at[slot, j, 1],
+            ).wait()
+
+    def work(count):
+        rows = 256
+        for part in range(BLOCK // rows):
+            length = (part + 1) * rows
+            span = pl.ds(part * rows, rows)
+            q = query[span, :]
+            own = scores_of(q, own_key[0:length, :])
+            row_iota = lax.broadcasted_iota(jnp.int32, (rows, length), 0) + part * rows
+            col_iota = lax.broadcasted_iota(jnp.int32, (rows, length), 1)
+            own = jnp.where(col_iota <= row_iota, own, -jnp.inf)
+            others = [scores_of(q, key_buf[slot, j]) for j in range(count)]
+            highest = jnp.max(own, axis=1, keepdims=True)
+            for other in others:
+                highest = jnp.maximum(highest, jnp.max(other, axis=1, keepdims=True))
+            weight = jnp.exp2((own - highest) * SCALE).astype(jnp.bfloat16)
+            ones = jnp.ones((length, HEAD), jnp.bfloat16)
+            total = jnp.dot(
+                weight,
+                jnp.concatenate([own_value[0:length, :], ones], axis=1),
+                preferred_element_type=jnp.float32,
             )
-        out[part * rows : length, :] = (total[:, :HEAD] / total[:, HEAD:]).astype(jnp.bfloat16)
-
-
-def attend(plan, me, queries, keys, values, other_keys, other_values, arrived, forwarded, pieces):
-    block = pl.BlockSpec((BLOCK, HEAD), lambda h: (0, h))
+            for j, other in enumerate(others):
+                weight = jnp.exp2((other - highest) * SCALE).astype(jnp.bfloat16)
+                total = total + jnp.dot(
+                    weight, value_buf[slot, j], preferred_element_type=jnp.float32
+                )
+            out[span, :] = (total[:, :HEAD] / total[:, HEAD:]).astype(jnp.bfloat16)
+            if count < 3:
+                state[0, span, 0 : 2 * HEAD] = total
+                state[0, span, 2 * HEAD :] = jnp.broadcast_to(highest, (rows, HEAD))
+
+    for count in range(4):
+
+        @pl.when(present == count)
+        def _():
+            work(count)
+
+
+def attend(first, last, before, plan, me, queries, keys, values, others, arrived):
+    block = pl.BlockSpec((BLOCK, HEAD), lambda h: (0, h + first))
+    count = last - first
+    size = count * BLOCK * 4 * BLOCK * HEAD
     return pl.pallas_call(
-        attend_kernel,
-        grid=(HEADS,),
-        in_specs=[SMEM, SMEM, block, block, block] + [ANY] * (4 + len(forwarded)),
-        out_specs=block,
-        out_shape=jax.ShapeDtypeStruct((BLOCK, HEADS * HEAD), jnp.bfloat16),
+        lambda *refs: attend_kernel(first, last, *refs),
+        grid=(count,),
+        in_specs=[SMEM, SMEM, block, block, block, ANY, ANY, ANY] + [ANY] * len(before),
+        out_specs=[block, pl.BlockSpec((1, BLOCK, 3 * HEAD), lambda h: (h + first, 0, 0))],
+        out_shape=[
+            jax.ShapeDtypeStruct((BLOCK, HEADS * HEAD), jnp.bfloat16),
+            jax.ShapeDtypeStruct((HEADS, BLOCK, 3 * HEAD), jnp.float32),
+        ],
+        input_output_aliases={8: 0, 9: 1} if before else {},
         scratch_shapes=[
             pltpu.SMEM((3 * HEADS,), jnp.int32),
             pltpu.SMEM((HEADS,), jnp.int32),
@@ -425,9 +415,134 @@
             pltpu.VMEM((2, 3, BLOCK, 2 * HEAD), jnp.bfloat16),
             pltpu.SemaphoreType.DMA((2, 3, 2)),
         ],
+        cost_estimate=pl.CostEstimate(
+            flops=16 * size, bytes_accessed=count * 3 * 2**20, transcendentals=size // HEAD
+        ),
         compiler_params=BIG,
         name="attend",
-    )(plan, me, queries, keys, values, other_keys, other_values, arrived, *forwarded, pieces)
+    )(plan, me, queries, keys, values, *others, arrived, *before)
+
+
+PENDING = KINDS + SPARE
+
+
+def merge_kernel(plan, me_ref, query, state, out_before, pieces, *rest):
+    count = KINDS - PARTNER + 1
+    forwarded = rest[:count]
+    out, waiting, carried, tile_buf, done_buf, state_sems, sems, done_sems = rest[count:]
+    me = me_ref[0]
+
+    def head_of(index):
+        return plan[ROW_FORWARD_HEAD + index, me]
+
+    for h in range(HEADS):
+        waiting[h] = 0
+
+    def count_one(index, carry):
+        @pl.when(head_of(index) > 0)
+        def _():
+            waiting[head_of(index) - 1] = 1
+
+        return carry
+
+    lax.fori_loop(0, PENDING, count_one, 0)
+
+    def load_state(h):
+        return pltpu.make_async_copy(state.at[h], carried.at[h], state_sems.at[h])
+
+    def store_out(h):
+        return pltpu.make_async_copy(done_buf.at[h], out.at[:, columns(h)], done_sems.at[h])
+
+    def each_waiting(action):
+        def one(h, carry):
+            @pl.when(waiting[h] > 0)
+            def _():
+                action(h)
+
+            return carry
+
+        lax.fori_loop(0, HEADS, one, 0)
+
+    each_waiting(lambda h: load_state(h).start())
+    for kind in range(KINDS):
+        source = forwarded[0].at[kind] if kind < PARTNER else forwarded[kind - PARTNER + 1].at[0]
+
+        @pl.when(head_of(kind) > 0)
+        def _():
+            pltpu.make_async_copy(source, tile_buf.at[kind], sems.at[kind]).start()
+
+    def one_spare(index, carry):
+        @pl.when(head_of(KINDS + index) > 0)
+        def _():
+            from_row = pl.ds(pl.multiple_of(index * PIECE, PIECE), PIECE)
+
+            def one_piece(piece, carry):
+                for half in range(2):
+                    row = pl.multiple_of(half * BLOCK + piece * PIECE, PIECE)
+                    pltpu.make_async_copy(
+                        pieces.at[2 * piece + half, from_row],
+                        tile_buf.at[KINDS + index, pl.ds(row, PIECE)],
+                        sems.at[KINDS + index],
+                    ).start()
+                return carry
+
+            lax.fori_loop(0, BLOCK // PIECE, one_piece, 0)
+
+        return carry
+
+    lax.fori_loop(0, SPARE, one_spare, 0)
+    each_waiting(lambda h: load_state(h).wait())
+
+    def one_tile(index, carry):
+        @pl.when(head_of(index) > 0)
+        def _():
+            h = head_of(index) - 1
+            pltpu.make_async_copy(tile_buf.at[0], tile_buf.at[index], sems.at[index]).wait()
+            key = tile_buf[index, 0:BLOCK, :]
+            ones = jnp.ones((BLOCK, HEAD), jnp.bfloat16)
+            value = jnp.concatenate([tile_buf[index, BLOCK:, :], ones], axis=1)
+            rows = 256
+            for part in range(BLOCK // rows):
+                span = pl.ds(part * rows, rows)
+                scores = scores_of(query[span, columns(h)], key)
+                old = carried[h, span, 2 * HEAD :]
+                highest = jnp.maximum(old, jnp.max(scores, axis=1, keepdims=True))
+                keep = jnp.exp2((old - highest) * SCALE)
+                weight = jnp.exp2((scores - highest[:, :1]) * SCALE).astype(jnp.bfloat16)
+                added = jnp.dot(weight, value, preferred_element_type=jnp.float32)
+                total = carried[h, span, 0:HEAD] * keep + added[:, :HEAD]
+                norm = carried[h, span, HEAD : 2 * HEAD] * keep + added[:, HEAD:]
+                carried[h, span, 0:HEAD] = total
+                carried[h, span, HEAD : 2 * HEAD] = norm
+                carried[h, span, 2 * HEAD :] = highest
+                done_buf[h, span, :] = (total / norm).astype(jnp.bfloat16)
+
+        return carry
+
+    lax.fori_loop(0, PENDING, one_tile, 0)
+    each_waiting(lambda h: store_out(h).start())
+    each_waiting(lambda h: store_out(h).wait())
+
+
+def merge(plan, me, queries, state, out, pieces, forwarded):
+    return pl.pallas_call(
+        merge_kernel,
+        in_specs=[SMEM, SMEM, VMEM, ANY, ANY, ANY] + [ANY] * len(forwarded),
+        out_specs=ANY,
+        out_shape=jax.ShapeDtypeStruct((BLOCK, HEADS * HEAD), jnp.bfloat16),
+        input_output_aliases={4: 0},
+        scratch_shapes=[
+            pltpu.SMEM((HEADS,), jnp.int32),
+            pltpu.VMEM((HEADS, BLOCK, 3 * HEAD), jnp.float32),
+            pltpu.VMEM((PENDING, 2 * BLOCK, HEAD), jnp.bfloat16),
+            pltpu.VMEM((HEADS, BLOCK, HEAD), jnp.bfloat16),
+            pltpu.SemaphoreType.DMA((HEADS,)),
+            pltpu.SemaphoreType.DMA((PENDING,)),
+            pltpu.SemaphoreType.DMA((HEADS,)),
+        ],
+        compiler_params=BIG,
+        name="merge",
+    )(plan, me, queries, state, out, pieces, *forwarded)
 
 
 LANES = [[2 * chip + core for chip in range(CHIPS)] for core in range(2)]
@@ -481,9 +596,22 @@
         lax.ppermute(array, "ctx", shift_pairs(SHIFTS[0] if n == 0 else SHIFTS[PARTNER + n - 1]))
         for n, array in enumerate(outgoing)
     ]
-    out = attend(
-        plan, me_ref, queries, keys, values, other_keys, other_values, arrived, forwarded, pieces
-    )
+    parts = ()
+    step = HEADS // PARTS
+    for first in range(0, HEADS, step):
+        parts = attend(
+            first,
+            first + step,
+            parts,
+            plan,
+            me_ref,
+            queries,
+            keys,
+            values,
+            (other_keys, other_values),
+            arrived,
+        )
+    out = merge(plan, me_ref, queries, parts[1], parts[0], pieces, forwarded)
     return lax.cond(
         plan[ROW_LEFT, 0] > 0,
         lambda: full_attention(queries, keys, values, chosen_all, me),

time: 388 us -> 490 us (1.26)
  waiting for transfers between devices: 32.8 us -> 307 us
  blocking collectives: 203 us -> 0 us
  Pallas kernels: 75.5 us -> 115 us
  local copies, waits for them, and re-layouts: 27.5 us -> 5.06 us
  starting transfers between devices: 45.6 us -> 61 us
    all_to_all x1 -> x2, waiting for transfers between devices: 0.01 us -> 299 us  [exchange(): lax.all_to_all(array, 'ctx', 0, 0, axis_index_groups=LANES, tiled=True)]
    all_to_all x1 -> x0, blocking collectives: 203 us -> none  [exchange(): lax.all_to_all(array, 'ctx', 0, 0, axis_index_groups=LANES, tiled=True)]
    pallas_call x2 -> x6, Pallas kernels: 60.5 us -> 99.3 us  [the longest x4 56.5 us: attend(): pl.pallas_call(lambda *refs: attend_kernel(first, last, *refs), grid=(cou...]
    ppermute x13, waiting for transfers between devices: 24.9 us -> 0.03 us  [body(): lax.ppermute(array, 'ctx', shift_pairs(SHIFTS[0] if n == 0 else SHIFTS[PA...]
    unnamed x69 -> x15, local copies, waits for them, and re-layouts: 26.1 us -> 3.05 us
    ppermute x13, starting transfers between devices: 15.4 us -> 32 us  [body(): lax.ppermute(array, 'ctx', shift_pairs(SHIFTS[0] if n == 0 else SHIFTS[PA...]
    all_to_all x1 -> x2, starting transfers between devices: 18.9 us -> 17.7 us  [exchange(): lax.all_to_all(array, 'ctx', 0, 0, axis_index_groups=LANES, tiled=True)]
  transfers between devices with their start and end apart: 17 -> 18, of which waited for: 7 -> 2; matrix products, arithmetic and copies ran while one was open for 1% -> 1% of each run, Pallas kernels for 1% -> 13%
where the time goes in v3:
time: 490 us; the launch traced here: 489 us
  waiting for transfers between devices  307 us (63%)
  Pallas kernels  115 us (23%)
  starting transfers between devices  61 us (12%)
  local copies, waits for them, and re-layouts  5.06 us (1%)
    all_to_all x2, waiting for transfers between devices, exchange(): lax.all_to_all(array, 'ctx', 0, 0, axis_index_groups=LANES, tiled=True)  299 us
    pallas_call x4, Pallas kernels, attend(): pl.pallas_call(lambda *refs: attend_kernel(first, last, *refs), grid=(cou...  56.5 us
    ppermute x13, starting transfers between devices, body(): lax.ppermute(array, 'ctx', shift_pairs(SHIFTS[0] if n == 0 else SHIFTS[PA...  32 us
    pallas_call x1, Pallas kernels, forward(): pl.pallas_call(forward_kernel, in_specs=[SMEM, SMEM, ANY], out_specs=[ANY...  24.6 us
    pallas_call x1, Pallas kernels, merge(): pl.pallas_call(merge_kernel, in_specs=[SMEM, SMEM, VMEM, ANY, ANY, ANY] +...  18.2 us
    all_to_all x2, starting transfers between devices, exchange(): lax.all_to_all(array, 'ctx', 0, 0, axis_index_groups=LANES, tiled=True)  17.7 us
    all_to_all x1, starting transfers between devices, body(): chosen_all = lax.all_to_all(spread, 'ctx', 0, 0, tiled=True)  10.6 us
    pallas_call x1, Pallas kernels, pack(): pl.pallas_call(pack_kernel, in_specs=[SMEM, SMEM, VMEM, VMEM, VMEM, VMEM]...  10.1 us
  transfers between devices with their start and end apart: 18, of which 2 were waited for; matrix products, arithmetic and copies ran while one was open for 1% of the time, Pallas kernels for 13%

profile of v3, /device:TPU:7, one launch (start us, length us, event | category | flops | bytes accessed | tf_op | source)
XLA Modules:
  0.0 489.0 jit_solution(7520223818426000497)
XLA Ops:
  0.0 0.7 collective-permute-start
  0.7 0.0 collective-permute-start.1
  0.7 0.8 copy.34
  1.4 0.1 broadcast_in_dim.55
  1.5 0.7 broadcast_in_dim.56
  2.2 10.6 %all-to-all-start.2 = ((s32[128,1,48]{2,1,0:T(1,128)}), s32[128,1,48]{2,1,0:T(1,128)S(1)}, u32[]{:S(2)}, u32[]{:S(2)}) async-start(s32[128,1,48]{2,1,0:T(1,128)} %broadcast_in_dim.56), calls=%async_computation.2 | async-start | bytes 131072 | tf_op jit(solution)/shard_map/all_to_all | solution.py:589
  12.8 7.9 %all-to-all-done.2 = s32[128,1,48]{2,1,0:T(1,128)S(1)} async-done(((s32[128,1,48]{2,1,0:T(1,128)}), s32[128,1,48]{2,1,0:T(1,128)S(1)}, u32[]{:S(2)}, u32[]{:S(2)}) %all-to-all-start.2) | async-done | bytes 24608 | tf_op jit(solution)/shard_map/all_to_all | solution.py:589
  20.7 0.1 copy.35
  20.8 5.4 %plan.1.refs_0_ = s32[248,128]{1,0:T(8,128)} custom-call(s32[48,128]{1,0:T(8,128)S(1)} %bitcast.60), custom_call_target="tpu_custom_call" | custom-call | tf_op jit(solution)/shard_map/plan/pallas_call | solution.py:141
  26.2 0.0 collective-permute-done.other_keys.refs_5_
  26.2 0.0 copy-start.3
  26.2 0.0 collective-permute-done.1.other_values.refs_6_
  26.2 1.3 copy-done.3
  27.4 10.1 %pack.1 = bf16[64,1088,128]{2,1,0:T(8,128)(2,1)} custom-call(s32[248,128]{1,0:T(8,128)} %plan.1.refs_0_, s32[1]{0:T(128)} %bitcast.13.me_ref.refs_1_, bf16[512,2048]{1,0:T(8,128)(2,1)} %refs_3_.7, bf16[512,2048]{1,0:T(8,128)(2,1)} %refs_4_.7, bf16[512,2048]{1,0:T(8,128)(2,1)} %copy-done.3, bf16[512,2048]{1,0:T(8,128)(2,1)} %collective-permute-done.1.other_values.refs_6_), custom_call_target="tpu_custom_call" | custom-call | tf_op jit(solution)/shard_map/pack/pallas_call | solution.py:218
  37.5 7.0 %all-to-all-start.3 = ((bf16[64,1088,128]{2,1,0:T(8,128)(2,1)}), bf16[64,1088,128]{2,1,0:T(8,128)(2,1)}, u32[]{:S(2)}, u32[]{:S(2)}) async-start(bf16[64,1088,128]{2,1,0:T(8,128)(2,1)} %pack.1), calls=%async_computation.3 | async-start | bytes 35651584 | tf_op jit(solution)/shard_map/all_to_all | solution.py:553
  44.6 1.2 slice.12
  46.4 0.0 copy-start.1
  46.4 299.1 %all-to-all-done.3.refs_7_.arrived = bf16[64,1088,128]{2,1,0:T(8,128)(2,1)} async-done(((bf16[64,1088,128]{2,1,0:T(8,128)(2,1)}), bf16[64,1088,128]{2,1,0:T(8,128)(2,1)}, u32[]{:S(2)}, u32[]{:S(2)}) %all-to-all-start.3) | async-done | bytes 17825824 | tf_op jit(solution)/shard_map/all_to_all | solution.py:553
  345.6 24.6 %forward.1 = (bf16[64,64,128]{2,1,0:T(8,128)(2,1)}, bf16[6,1024,128]{2,1,0:T(8,128)(2,1)}, bf16[1,1024,128]{2,1,0:T(8,128)(2,1)}, bf16[1,1024,128]{2,1,0:T(8,128...) custom-call(s32[248,128]{1,0:T(8,128)} %plan.1.refs_0_, ...), custom_call_target="tpu_custom_call" | custom-call | tf_op jit(solution)/shard_map/forward/pallas_call | solution.py:267
  370.2 0.8 collective-permute-start.2
  371.0 3.1 collective-permute-start.10
  374.0 0.0 collective-permute-start.11
  374.1 0.0 collective-permute-start.12
  374.1 1.7 collective-permute-start.13
  375.8 10.7 %all-to-all-start.4 = ((bf16[64,64,128]{2,1,0:T(8,128)(2,1)}), bf16[64,64,128]{2,1,0:T(8,128)(2,1)S(1)}, u32[]{:S(2)}, u32[]{:S(2)}) async-start(bf16[64,64,128]{2,1,0:T(8,128)(2,1)} %get-tuple-element.180), calls=%async_computation.4 | async-start | bytes 2097152 | tf_op jit(solution)/shard_map/all_to_all | solution.py:553
  386.5 0.0 copy-done.1
  386.5 13.7 %attend.4 = (bf16[512,2048]{1,0:T(8,128)(2,1)}, f32[16,512,384]{2,1,0:T(8,128)}) custom-call(s32[248,128]{1,0:T(8,128)} %plan.1.refs_0_, s32[1]{0:T(128)} %bitcast.13.me_ref.refs_1_, bf16[512,2048]{1,0:T(8,128)(2,1)S(1)} %copy-done.1, bf16[512,2048]{1,0:T(8,128)(2,1)} %refs_3_.7, bf16[512,2048]{1,0:T(8,128)(2,1)} %refs_4_.7, bf16[512,2048]{1,0:T(8,128)(2,1)} %copy-done.3, ...), custom_call_target="tpu_custom_call" | custom-call | flops 8589934592 | bytes 12582912 | tf_op jit(solution)/shard_map/attend/pallas_call | solution.py:401
  400.2 15.0 %attend.5 = (bf16[512,2048]{1,0:T(8,128)(2,1)}, f32[16,512,384]{2,1,0:T(8,128)}) custom-call(s32[248,128]{1,0:T(8,128)} %plan.1.refs_0_, s32[1]{0:T(128)} %bitcast.13.me_ref.refs_1_, bf16[512,2048]{1,0:T(8,128)(2,1)S(1)} %copy-done.1, bf16[512,2048]{1,0:T(8,128)(2,1)} %refs_3_.7, ...), custom_call_target="tpu_custom_call", output_to_operand_aliasing={{0}: (8, {}), {1}: (9, {})} | custom-call | flops 8589934592 | bytes 12582912 | tf_op jit(solution)/shard_map/attend/pallas_call | solution.py:401
  415.2 0.0 collective-permute-done.10.rest_8_
  415.2 0.0 copy-start.5
  415.2 2.4 collective-permute-start.14
  417.6 0.0 collective-permute-done.11.rest_9_
  417.6 3.0 collective-permute-start.3
  420.6 0.0 collective-permute-done.12.rest_10_
  420.6 0.1 collective-permute-start.4
  420.7 0.0 collective-permute-done.13.rest_11_
  420.7 15.8 %collective-permute-start.5 = (bf16[1,1024,128]{2,1,0:T(8,128)(2,1)}, bf16[1,1024,128]{2,1,0:T(8,128)(2,1)}, u32[]{:S(2)}, u32[]{:S(2)}) collective-permute-start(bf16[1,1024,128]{2,1,0:T(8,128)(2,1)} %get-tuple-element.184), channel_id=1, source_target_pairs={{96,0},{97,1},{98,2},{99,3},{100,4},{101,5},{102,6},{103,7},{104,8... | collective-permute-start | bytes 786440 | tf_op jit(solution)/shard_map/ppermute | solution.py:596
  436.6 13.0 %attend.6 = (bf16[512,2048]{1,0:T(8,128)(2,1)}, f32[16,512,384]{2,1,0:T(8,128)}) custom-call(s32[248,128]{1,0:T(8,128)} %plan.1.refs_0_, s32[1]{0:T(128)} %bitcast.13.me_ref.refs_1_, bf16[512,2048]{1,0:T(8,128)(2,1)S(1)} %copy-done.1, bf16[512,2048]{1,0:T(8,128)(2,1)} %refs_3_.7, ...), custom_call_target="tpu_custom_call", output_to_operand_aliasing={{0}: (8, {}), {1}: (9, {})} | custom-call | flops 8589934592 | bytes 12582912 | tf_op jit(solution)/shard_map/attend/pallas_call | solution.py:401
  449.5 0.0 copy-done.5
  449.6 0.0 collective-permute-done.14.rest_12_
  449.6 0.0 copy-start.6
  449.6 1.4 collective-permute-start.6
  451.0 0.0 collective-permute-done.3.rest_1_
  451.0 0.0 copy-start.7
  451.0 0.0 collective-permute-start.7
  451.0 0.0 collective-permute-done.4.rest_2_
  451.0 1.0 collective-permute-start.8
  452.0 0.0 collective-permute-done.5.rest_3_
  452.0 2.6 collective-permute-start.9
  454.7 14.9 %attend.7 = (bf16[512,2048]{1,0:T(8,128)(2,1)}, f32[16,512,384]{2,1,0:T(8,128)}) custom-call(s32[248,128]{1,0:T(8,128)} %plan.1.refs_0_, s32[1]{0:T(128)} %bitcast.13.me_ref.refs_1_, bf16[512,2048]{1,0:T(8,128)(2,1)S(1)} %copy-done.1, bf16[512,2048]{1,0:T(8,128)(2,1)} %refs_3_.7, ...), custom_call_target="tpu_custom_call", output_to_operand_aliasing={{0}: (8, {}), {1}: (9, {})} | custom-call | flops 8589934592 | bytes 12582912 | tf_op jit(solution)/shard_map/attend/pallas_call | solution.py:401
  469.5 0.0 copy-done.6
  469.5 0.0 copy-done.7
  469.6 0.0 collective-permute-done.6.rest_4_
  469.6 0.0 copy-start.8
  469.6 0.0 collective-permute-done.7.rest_5_
  469.6 0.0 collective-permute-done.8.rest_6_
  469.6 0.0 collective-permute-done.9.rest_7_
  469.6 0.0 all-to-all-done.4.pieces
  469.6 0.0 copy-start.4
  469.6 0.0 collective-permute-done.2.rest_0_
  469.6 0.6 copy-done.8
  470.3 0.4 copy-done.4
  470.6 18.2 %merge.1 = bf16[512,2048]{1,0:T(8,128)(2,1)} custom-call(s32[248,128]{1,0:T(8,128)} %plan.1.refs_0_, s32[1]{0:T(128)} %bitcast.13.me_ref.refs_1_, bf16[512,2048]{1,0:T(8,128)(2,1)S(1)} %copy-done.1, f32[16,512,384]{2,1,0:T(8,128)} %get-tuple-element.178.state, bf16[512,2048]{1,0:T(8,128)(2,1)} %get-tuple-element.179.out_before, ...), custom_call_target="tpu_custom_call", output_to_operand_aliasing={{}: (4, {})} | custom-call | tf_op jit(solution)/shard_map/merge/pallas_call | solution.py:528
  (1 shorter events, 0.0 us)
Async XLA Ops:
  0.0 26.2 %collective-permute-start = (bf16[512,2048]{1,0:T(8,128)(2,1)}, bf16[512,2048]{1,0:T(8,128)(2,1)S(1)}, u32[]{:S(2)}, u32[]{:S(2)}) collective-permute-start(bf16[512,2048]{1,0:T(8,128)(2,1)} %refs_3_.7), channel_id=1, source_target_pairs={{0,1},{1,0},{2,3},{3,2},{4,5},{5,4},{6,7},{7,6},{8,9},{9,8},{10,11... | collective-permute-start | bytes 6291464 | tf_op jit(solution)/shard_map/ppermute | solution.py:586
  0.7 25.5 %collective-permute-start.1 = (bf16[512,2048]{1,0:T(8,128)(2,1)}, bf16[512,2048]{1,0:T(8,128)(2,1)}, u32[]{:S(2)}, u32[]{:S(2)}) collective-permute-start(bf16[512,2048]{1,0:T(8,128)(2,1)} %refs_4_.7), channel_id=1, source_target_pairs={{0,1},{1,0},{2,3},{3,2},{4,5},{5,4},{6,7},{7,6},{8,9},{9,8},{10,11... | collective-permute-start | bytes 6291464 | tf_op jit(solution)/shard_map/ppermute | solution.py:587
  2.2 18.5 %all-to-all-start.2 = ((s32[128,1,48]{2,1,0:T(1,128)}), s32[128,1,48]{2,1,0:T(1,128)S(1)}, u32[]{:S(2)}, u32[]{:S(2)}) async-start(s32[128,1,48]{2,1,0:T(1,128)} %broadcast_in_dim.56), calls=%async_computation.2 | async-start | bytes 131072 | tf_op jit(solution)/shard_map/all_to_all | solution.py:589
  26.2 1.3 copy-start.3
  37.5 308.1 %all-to-all-start.3 = ((bf16[64,1088,128]{2,1,0:T(8,128)(2,1)}), bf16[64,1088,128]{2,1,0:T(8,128)(2,1)}, u32[]{:S(2)}, u32[]{:S(2)}) async-start(bf16[64,1088,128]{2,1,0:T(8,128)(2,1)} %pack.1), calls=%async_computation.3 | async-start | bytes 35651584 | tf_op jit(solution)/shard_map/all_to_all | solution.py:553
  46.4 340.1 %copy-start.1 = (bf16[512,2048]{1,0:T(8,128)(2,1)S(1)}, bf16[512,2048]{1,0:T(8,128)(2,1)}, u32[]{:S(2)}) copy-start(bf16[512,2048]{1,0:T(8,128)(2,1)} %query.1) | copy-start | bytes 6291460
  370.2 99.4 %collective-permute-start.2 = (bf16[6,1024,128]{2,1,0:T(8,128)(2,1)}, bf16[6,1024,128]{2,1,0:T(8,128)(2,1)}, u32[]{:S(2)}, u32[]{:S(2)}) collective-permute-start(bf16[6,1024,128]{2,1,0:T(8,128)(2,1)} %get-tuple-element.181), channel_id=1, source_target_pairs={{1,0},{0,1},{3,2},{2,3},{5,4},{4,5},{7,6},{6,7},{9,8},{8,9},{11,10... | collective-permute-start | bytes 4718600 | tf_op jit(solution)/shard_map/ppermute | solution.py:596
  371.0 44.2 %collective-permute-start.10 = (bf16[1,1024,128]{2,1,0:T(8,128)(2,1)}, bf16[1,1024,128]{2,1,0:T(8,128)(2,1)S(1)}, u32[]{:S(2)}, u32[]{:S(2)}) collective-permute-start(bf16[1,1024,128]{2,1,0:T(8,128)(2,1)} %get-tuple-element.189), channel_id=1, source_target_pairs={{25,0},{24,1},{27,2},{26,3},{29,4},{28,5},{31,6},{30,7},{1,8},{0,9... | collective-permute-start | bytes 786440 | tf_op jit(solution)/shard_map/ppermute | solution.py:596
  374.0 43.6 %collective-permute-start.11 = (bf16[1,1024,128]{2,1,0:T(8,128)(2,1)}, bf16[1,1024,128]{2,1,0:T(8,128)(2,1)}, u32[]{:S(2)}, u32[]{:S(2)}) collective-permute-start(bf16[1,1024,128]{2,1,0:T(8,128)(2,1)} %get-tuple-element.190), channel_id=1, source_target_pairs={{2,0},{3,1},{4,2},{5,3},{6,4},{7,5},{0,6},{1,7},{10,8},{11,9},{12,... | collective-permute-start | bytes 786440 | tf_op jit(solution)/shard_map/ppermute | solution.py:596
  374.1 46.6 %collective-permute-start.12 = (bf16[1,1024,128]{2,1,0:T(8,128)(2,1)}, bf16[1,1024,128]{2,1,0:T(8,128)(2,1)}, u32[]{:S(2)}, u32[]{:S(2)}) collective-permute-start(bf16[1,1024,128]{2,1,0:T(8,128)(2,1)} %get-tuple-element.191), channel_id=1, source_target_pairs={{3,0},{2,1},{5,2},{4,3},{7,4},{6,5},{1,6},{0,7},{11,8},{10,9},{13,... | collective-permute-start | bytes 786440 | tf_op jit(solution)/shard_map/ppermute | solution.py:596
  374.1 46.7 %collective-permute-start.13 = (bf16[1,1024,128]{2,1,0:T(8,128)(2,1)}, bf16[1,1024,128]{2,1,0:T(8,128)(2,1)}, u32[]{:S(2)}, u32[]{:S(2)}) collective-permute-start(bf16[1,1024,128]{2,1,0:T(8,128)(2,1)} %get-tuple-element.192), channel_id=1, source_target_pairs={{6,0},{7,1},{0,2},{1,3},{2,4},{3,5},{4,6},{5,7},{14,8},{15,9},{8,1... | collective-permute-start | bytes 786440 | tf_op jit(solution)/shard_map/ppermute | solution.py:596
  375.8 93.8 %all-to-all-start.4 = ((bf16[64,64,128]{2,1,0:T(8,128)(2,1)}), bf16[64,64,128]{2,1,0:T(8,128)(2,1)S(1)}, u32[]{:S(2)}, u32[]{:S(2)}) async-start(bf16[64,64,128]{2,1,0:T(8,128)(2,1)} %get-tuple-element.180), calls=%async_computation.4 | async-start | bytes 2097152 | tf_op jit(solution)/shard_map/all_to_all | solution.py:553
  415.2 34.4 %copy-start.5 = (bf16[1,1024,128]{2,1,0:T(8,128)(2,1)}, bf16[1,1024,128]{2,1,0:T(8,128)(2,1)S(1)}, u32[]{:S(2)}) copy-start(bf16[1,1024,128]{2,1,0:T(8,128)(2,1)S(1)} %collective-permute-done.10.rest_8_) | copy-start | bytes 786436
  415.2 34.4 %collective-permute-start.14 = (bf16[1,1024,128]{2,1,0:T(8,128)(2,1)}, bf16[1,1024,128]{2,1,0:T(8,128)(2,1)S(1)}, u32[]{:S(2)}, u32[]{:S(2)}) collective-permute-start(bf16[1,1024,128]{2,1,0:T(8,128)(2,1)} %get-tuple-element.193), channel_id=1, source_target_pairs={{7,0},{6,1},{1,2},{0,3},{3,4},{2,5},{5,6},{4,7},{15,8},{14,9},{9,1... | collective-permute-start | bytes 786440 | tf_op jit(solution)/shard_map/ppermute | solution.py:596
  417.6 33.4 %collective-permute-start.3 = (bf16[1,1024,128]{2,1,0:T(8,128)(2,1)}, bf16[1,1024,128]{2,1,0:T(8,128)(2,1)S(1)}, u32[]{:S(2)}, u32[]{:S(2)}) collective-permute-start(bf16[1,1024,128]{2,1,0:T(8,128)(2,1)} %get-tuple-element.182), channel_id=1, source_target_pairs={{32,0},{33,1},{34,2},{35,3},{36,4},{37,5},{38,6},{39,7},{40,8},{41... | collective-permute-start | bytes 786440 | tf_op jit(solution)/shard_map/ppermute | solution.py:596
  420.6 30.4 %collective-permute-start.4 = (bf16[1,1024,128]{2,1,0:T(8,128)(2,1)}, bf16[1,1024,128]{2,1,0:T(8,128)(2,1)}, u32[]{:S(2)}, u32[]{:S(2)}) collective-permute-start(bf16[1,1024,128]{2,1,0:T(8,128)(2,1)} %get-tuple-element.183), channel_id=1, source_target_pairs={{33,0},{32,1},{35,2},{34,3},{37,4},{36,5},{39,6},{38,7},{41,8},{40... | collective-permute-start | bytes 786440 | tf_op jit(solution)/shard_map/ppermute | solution.py:596
  420.7 31.3 %collective-permute-start.5 = (bf16[1,1024,128]{2,1,0:T(8,128)(2,1)}, bf16[1,1024,128]{2,1,0:T(8,128)(2,1)}, u32[]{:S(2)}, u32[]{:S(2)}) collective-permute-start(bf16[1,1024,128]{2,1,0:T(8,128)(2,1)} %get-tuple-element.184), channel_id=1, source_target_pairs={{96,0},{97,1},{98,2},{99,3},{100,4},{101,5},{102,6},{103,7},{104,8... | collective-permute-start | bytes 786440 | tf_op jit(solution)/shard_map/ppermute | solution.py:596
  449.6 20.0 %copy-start.6 = (bf16[1,1024,128]{2,1,0:T(8,128)(2,1)}, bf16[1,1024,128]{2,1,0:T(8,128)(2,1)S(1)}, u32[]{:S(2)}) copy-start(bf16[1,1024,128]{2,1,0:T(8,128)(2,1)S(1)} %collective-permute-done.14.rest_12_) | copy-start | bytes 786436
  449.6 20.0 %collective-permute-start.6 = (bf16[1,1024,128]{2,1,0:T(8,128)(2,1)}, bf16[1,1024,128]{2,1,0:T(8,128)(2,1)S(1)}, u32[]{:S(2)}, u32[]{:S(2)}) collective-permute-start(bf16[1,1024,128]{2,1,0:T(8,128)(2,1)} %get-tuple-element.185), channel_id=1, source_target_pairs={{97,0},{96,1},{99,2},{98,3},{101,4},{100,5},{103,6},{102,7},{105,8... | collective-permute-start | bytes 786440 | tf_op jit(solution)/shard_map/ppermute | solution.py:596
  451.0 18.5 %copy-start.7 = (bf16[1,1024,128]{2,1,0:T(8,128)(2,1)}, bf16[1,1024,128]{2,1,0:T(8,128)(2,1)S(1)}, u32[]{:S(2)}) copy-start(bf16[1,1024,128]{2,1,0:T(8,128)(2,1)S(1)} %collective-permute-done.3.rest_1_) | copy-start | bytes 786436
  451.0 18.6 %collective-permute-start.7 = (bf16[1,1024,128]{2,1,0:T(8,128)(2,1)}, bf16[1,1024,128]{2,1,0:T(8,128)(2,1)}, u32[]{:S(2)}, u32[]{:S(2)}) collective-permute-start(bf16[1,1024,128]{2,1,0:T(8,128)(2,1)} %get-tuple-element.186), channel_id=1, source_target_pairs={{8,0},{9,1},{10,2},{11,3},{12,4},{13,5},{14,6},{15,7},{16,8},{17,9... | collective-permute-start | bytes 786440 | tf_op jit(solution)/shard_map/ppermute | solution.py:596
  451.0 18.5 %collective-permute-start.8 = (bf16[1,1024,128]{2,1,0:T(8,128)(2,1)}, bf16[1,1024,128]{2,1,0:T(8,128)(2,1)}, u32[]{:S(2)}, u32[]{:S(2)}) collective-permute-start(bf16[1,1024,128]{2,1,0:T(8,128)(2,1)} %get-tuple-element.187), channel_id=1, source_target_pairs={{9,0},{8,1},{11,2},{10,3},{13,4},{12,5},{15,6},{14,7},{17,8},{16,9... | collective-permute-start | bytes 786440 | tf_op jit(solution)/shard_map/ppermute | solution.py:596
  452.0 17.6 %collective-permute-start.9 = (bf16[1,1024,128]{2,1,0:T(8,128)(2,1)}, bf16[1,1024,128]{2,1,0:T(8,128)(2,1)}, u32[]{:S(2)}, u32[]{:S(2)}) collective-permute-start(bf16[1,1024,128]{2,1,0:T(8,128)(2,1)} %get-tuple-element.188), channel_id=1, source_target_pairs={{24,0},{25,1},{26,2},{27,3},{28,4},{29,5},{30,6},{31,7},{0,8},{1,9... | collective-permute-start | bytes 786440 | tf_op jit(solution)/shard_map/ppermute | solution.py:596
  469.6 0.7 copy-start.8
  469.6 1.0 copy-start.4

commit v4 on v3

--- a/solution.py
+++ b/solution.py
@@ -589,7 +589,9 @@
     chosen_all = lax.all_to_all(spread, "ctx", 0, 0, tiled=True)
     plan = make_plan(chosen_all.T)
     send = pack(plan, me_ref, keys, values, other_keys, other_values)
-    arrived = exchange(send)
+    held = (exchange(send), plan, queries, keys, values, other_keys, other_values, me_ref)
+    held = lax.optimization_barrier(held)
+    arrived, plan, queries, keys, values, other_keys, other_values, me_ref = held
     pieces, *outgoing = forward(plan, me_ref, arrived)
     pieces = exchange(pieces)
     forwarded = [

time: 490 us -> 387 us (0.79)
  waiting for transfers between devices: 307 us -> 7.91 us
  blocking collectives: 0 us -> 203 us
  Pallas kernels: 115 us -> 106 us
    all_to_all x2 -> x1, waiting for transfers between devices: 299 us -> 0.01 us  [exchange(): lax.all_to_all(array, 'ctx', 0, 0, axis_index_groups=LANES, tiled=True)]
    all_to_all x0 -> x1, blocking collectives: none -> 203 us  [exchange(): lax.all_to_all(array, 'ctx', 0, 0, axis_index_groups=LANES, tiled=True)]
    pallas_call x1, Pallas kernels: 24.6 us -> 16.5 us  [forward(): pl.pallas_call(forward_kernel, in_specs=[SMEM, SMEM, ANY], out_specs=[ANY...]
    all_to_all x2 -> x1, starting transfers between devices: 17.7 us -> 17.6 us  [exchange(): lax.all_to_all(array, 'ctx', 0, 0, axis_index_groups=LANES, tiled=True)]
  transfers between devices with their start and end apart: 18 -> 17, of which waited for: 2 -> 1; matrix products, arithmetic and copies ran while one was open for 1% -> 1% of each run, Pallas kernels for 13% -> 16%
where the time goes in v4:
time: 387 us; the launch traced here: 383 us
  blocking collectives  203 us (52%)
  Pallas kernels  106 us (27%)
  starting transfers between devices  59.6 us (15%)
  waiting for transfers between devices  7.91 us (2%)
  local copies, waits for them, and re-layouts  5.13 us (1%)
    all_to_all x1, blocking collectives, exchange(): lax.all_to_all(array, 'ctx', 0, 0, axis_index_groups=LANES, tiled=True)  203 us
    pallas_call x4, Pallas kernels, attend(): pl.pallas_call(lambda *refs: attend_kernel(first, last, *refs), grid=(cou...  57 us
    ppermute x13, starting transfers between devices, body(): lax.ppermute(array, 'ctx', shift_pairs(SHIFTS[0] if n == 0 else SHIFTS[PA...  30.7 us
    all_to_all x1, starting transfers between devices, exchange(): lax.all_to_all(array, 'ctx', 0, 0, axis_index_groups=LANES, tiled=True)  17.6 us
    pallas_call x1, Pallas kernels, merge(): pl.pallas_call(merge_kernel, in_specs=[SMEM, SMEM, VMEM, ANY, ANY, ANY] +...  16.8 us
    pallas_call x1, Pallas kernels, forward(): pl.pallas_call(forward_kernel, in_specs=[SMEM, SMEM, ANY], out_specs=[ANY...  16.5 us
    all_to_all x1, starting transfers between devices, body(): chosen_all = lax.all_to_all(spread, 'ctx', 0, 0, tiled=True)  10.6 us
    pallas_call x1, Pallas kernels, pack(): pl.pallas_call(pack_kernel, in_specs=[SMEM, SMEM, VMEM, VMEM, VMEM, VMEM]...  10 us
  transfers between devices with their start and end apart: 17, of which 1 were waited for; matrix products, arithmetic and copies ran while one was open for 1% of the time, Pallas kernels for 16%

profile of v4, /device:TPU:7, one launch (start us, length us, event | category | flops | bytes accessed | tf_op | source)
XLA Modules:
  0.0 382.5 jit_solution(13613848187261054003)
XLA Ops:
  0.0 0.7 collective-permute-start
  0.7 0.0 collective-permute-start.1
  0.7 0.8 copy.34
  1.4 0.1 broadcast_in_dim.55
  1.5 0.7 broadcast_in_dim.56
  2.2 10.6 %all-to-all-start.2 = ((s32[128,1,48]{2,1,0:T(1,128)}), s32[128,1,48]{2,1,0:T(1,128)S(1)}, u32[]{:S(2)}, u32[]{:S(2)}) async-start(s32[128,1,48]{2,1,0:T(1,128)} %broadcast_in_dim.56), calls=%async_computation.2 | async-start | bytes 131072 | tf_op jit(solution)/shard_map/all_to_all | solution.py:589
  12.8 7.9 %all-to-all-done.2 = s32[128,1,48]{2,1,0:T(1,128)S(1)} async-done(((s32[128,1,48]{2,1,0:T(1,128)}), s32[128,1,48]{2,1,0:T(1,128)S(1)}, u32[]{:S(2)}, u32[]{:S(2)}) %all-to-all-start.2) | async-done | bytes 24608 | tf_op jit(solution)/shard_map/all_to_all | solution.py:589
  20.7 0.1 copy.35
  20.8 5.4 %plan.1.refs_0_ = s32[248,128]{1,0:T(8,128)} custom-call(s32[48,128]{1,0:T(8,128)S(1)} %bitcast.60), custom_call_target="tpu_custom_call" | custom-call | tf_op jit(solution)/shard_map/plan/pallas_call | solution.py:141
  26.1 0.0 collective-permute-done.other_keys.refs_5_
  26.2 0.0 copy-start.3
  26.2 0.0 collective-permute-done.1.other_values.refs_6_
  26.2 1.3 copy-done.3
  27.5 10.0 %pack.1 = bf16[64,1088,128]{2,1,0:T(8,128)(2,1)} custom-call(s32[248,128]{1,0:T(8,128)} %plan.1.refs_0_, s32[1]{0:T(128)} %bitcast.12.me_ref.refs_1_, bf16[512,2048]{1,0:T(8,128)(2,1)} %refs_3_.3, bf16[512,2048]{1,0:T(8,128)(2,1)} %refs_4_.3, bf16[512,2048]{1,0:T(8,128)(2,1)} %copy-done.3, bf16[512,2048]{1,0:T(8,128)(2,1)} %collective-permute-done.1.other_values.refs_6_), custom_call_target="tpu_custom_call" | custom-call | tf_op jit(solution)/shard_map/pack/pallas_call | solution.py:218
  37.5 203.1 %all_to_all.28.refs_7_.arrived = bf16[64,1088,128]{2,1,0:T(8,128)(2,1)} all-to-all(bf16[64,1088,128]{2,1,0:T(8,128)(2,1)} %pack.1), channel_id=1, replica_groups={{0,2,4,6,8,10,12,14,16,18,20,22,24,26,28,30,32,34,36,38,40,42,44,46,48,..., dimensions={0} | all-to-all | bytes 35651584 | tf_op jit(solution)/shard_map/all_to_all | solution.py:553
  240.6 0.0 copy-start.1
  240.6 16.5 %forward.1 = (bf16[64,64,128]{2,1,0:T(8,128)(2,1)}, bf16[6,1024,128]{2,1,0:T(8,128)(2,1)}, bf16[1,1024,128]{2,1,0:T(8,128)(2,1)}, bf16[1,1024,128]{2,1,0:T(8,128...) custom-call(s32[248,128]{1,0:T(8,128)} %plan.1.refs_0_, ...), custom_call_target="tpu_custom_call" | custom-call | tf_op jit(solution)/shard_map/forward/pallas_call | solution.py:267
  257.1 1.4 collective-permute-start.2
  258.5 2.2 collective-permute-start.10
  260.7 1.0 collective-permute-start.11
  261.6 1.2 collective-permute-start.12
  262.8 0.8 collective-permute-start.13
  263.7 17.6 %all-to-all-start.4 = ((bf16[64,64,128]{2,1,0:T(8,128)(2,1)}), bf16[64,64,128]{2,1,0:T(8,128)(2,1)S(1)}, u32[]{:S(2)}, u32[]{:S(2)}) async-start(bf16[64,64,128]{2,1,0:T(8,128)(2,1)} %get-tuple-element.196), calls=%async_computation.4 | async-start | bytes 2097152 | tf_op jit(solution)/shard_map/all_to_all | solution.py:553
  281.3 0.0 copy-done.1
  281.3 14.9 %attend.4 = (bf16[512,2048]{1,0:T(8,128)(2,1)}, f32[16,512,384]{2,1,0:T(8,128)}) custom-call(s32[248,128]{1,0:T(8,128)} %plan.1.refs_0_, s32[1]{0:T(128)} %bitcast.12.me_ref.refs_1_, bf16[512,2048]{1,0:T(8,128)(2,1)S(1)} %copy-done.1, bf16[512,2048]{1,0:T(8,128)(2,1)} %refs_3_.3, bf16[512,2048]{1,0:T(8,128)(2,1)} %refs_4_.3, bf16[512,2048]{1,0:T(8,128)(2,1)} %copy-done.3, ...), custom_call_target="tpu_custom_call" | custom-call | flops 8589934592 | bytes 12582912 | tf_op jit(solution)/shard_map/attend/pallas_call | solution.py:401
  296.2 13.8 %attend.5 = (bf16[512,2048]{1,0:T(8,128)(2,1)}, f32[16,512,384]{2,1,0:T(8,128)}) custom-call(s32[248,128]{1,0:T(8,128)} %plan.1.refs_0_, s32[1]{0:T(128)} %bitcast.12.me_ref.refs_1_, bf16[512,2048]{1,0:T(8,128)(2,1)S(1)} %copy-done.1, bf16[512,2048]{1,0:T(8,128)(2,1)} %refs_3_.3, ...), custom_call_target="tpu_custom_call", output_to_operand_aliasing={{0}: (8, {}), {1}: (9, {})} | custom-call | flops 8589934592 | bytes 12582912 | tf_op jit(solution)/shard_map/attend/pallas_call | solution.py:401
  310.0 0.0 collective-permute-done.10.rest_8_
  310.1 0.0 copy-start.5
  310.1 1.8 collective-permute-start.14
  311.9 0.0 collective-permute-done.11.rest_9_
  311.9 3.0 collective-permute-start.3
  314.8 0.0 collective-permute-done.12.rest_10_
  314.8 1.2 collective-permute-start.4
  316.0 0.0 collective-permute-done.13.rest_11_
  316.0 14.2 %collective-permute-start.5 = (bf16[1,1024,128]{2,1,0:T(8,128)(2,1)}, bf16[1,1024,128]{2,1,0:T(8,128)(2,1)}, u32[]{:S(2)}, u32[]{:S(2)}) collective-permute-start(bf16[1,1024,128]{2,1,0:T(8,128)(2,1)} %get-tuple-element.200), channel_id=1, source_target_pairs={{96,0},{97,1},{98,2},{99,3},{100,4},{101,5},{102,6},{103,7},{104,8... | collective-permute-start | bytes 786440 | tf_op jit(solution)/shard_map/ppermute | solution.py:598
  330.2 14.2 %attend.6 = (bf16[512,2048]{1,0:T(8,128)(2,1)}, f32[16,512,384]{2,1,0:T(8,128)}) custom-call(s32[248,128]{1,0:T(8,128)} %plan.1.refs_0_, s32[1]{0:T(128)} %bitcast.12.me_ref.refs_1_, bf16[512,2048]{1,0:T(8,128)(2,1)S(1)} %copy-done.1, bf16[512,2048]{1,0:T(8,128)(2,1)} %refs_3_.3, ...), custom_call_target="tpu_custom_call", output_to_operand_aliasing={{0}: (8, {}), {1}: (9, {})} | custom-call | flops 8589934592 | bytes 12582912 | tf_op jit(solution)/shard_map/attend/pallas_call | solution.py:401
  344.3 0.0 copy-done.5
  344.4 0.0 collective-permute-done.14.rest_12_
  344.4 0.0 copy-start.6
  344.4 0.9 collective-permute-start.6
  345.3 0.0 collective-permute-done.3.rest_1_
  345.3 0.0 copy-start.7
  345.3 0.3 collective-permute-start.7
  345.6 0.0 collective-permute-done.4.rest_2_
  345.6 1.8 collective-permute-start.8
  347.4 0.0 collective-permute-done.5.rest_3_
  347.4 1.0 collective-permute-start.9
  348.4 14.1 %attend.7 = (bf16[512,2048]{1,0:T(8,128)(2,1)}, f32[16,512,384]{2,1,0:T(8,128)}) custom-call(s32[248,128]{1,0:T(8,128)} %plan.1.refs_0_, s32[1]{0:T(128)} %bitcast.12.me_ref.refs_1_, bf16[512,2048]{1,0:T(8,128)(2,1)S(1)} %copy-done.1, bf16[512,2048]{1,0:T(8,128)(2,1)} %refs_3_.3, ...), custom_call_target="tpu_custom_call", output_to_operand_aliasing={{0}: (8, {}), {1}: (9, {})} | custom-call | flops 8589934592 | bytes 12582912 | tf_op jit(solution)/shard_map/attend/pallas_call | solution.py:401
  362.5 0.0 copy-done.6
  362.6 0.0 copy-done.7
  362.6 1.3 slice.3
  364.5 0.0 collective-permute-done.6.rest_4_
  364.5 0.0 copy-start.8
  364.5 0.0 collective-permute-done.7.rest_5_
  364.5 0.0 collective-permute-done.8.rest_6_
  364.5 0.0 collective-permute-done.9.rest_7_
  364.5 0.0 all-to-all-done.4.pieces
  364.5 0.0 copy-start.4
  364.5 0.0 collective-permute-done.2.rest_0_
  364.6 0.6 copy-done.8
  365.2 0.4 copy-done.4
  365.5 16.8 %merge.1 = bf16[512,2048]{1,0:T(8,128)(2,1)} custom-call(s32[248,128]{1,0:T(8,128)} %plan.1.refs_0_, s32[1]{0:T(128)} %bitcast.12.me_ref.refs_1_, bf16[512,2048]{1,0:T(8,128)(2,1)S(1)} %copy-done.1, f32[16,512,384]{2,1,0:T(8,128)} %get-tuple-element.194.state, bf16[512,2048]{1,0:T(8,128)(2,1)} %get-tuple-element.195.out_before, ...), custom_call_target="tpu_custom_call", output_to_operand_aliasing={{}: (4, {})} | custom-call | tf_op jit(solution)/shard_map/merge/pallas_call | solution.py:528
  (1 shorter events, 0.0 us)
Async XLA Ops:
  0.0 26.2 %collective-permute-start = (bf16[512,2048]{1,0:T(8,128)(2,1)}, bf16[512,2048]{1,0:T(8,128)(2,1)S(1)}, u32[]{:S(2)}, u32[]{:S(2)}) collective-permute-start(bf16[512,2048]{1,0:T(8,128)(2,1)} %refs_3_.3), channel_id=1, source_target_pairs={{0,1},{1,0},{2,3},{3,2},{4,5},{5,4},{6,7},{7,6},{8,9},{9,8},{10,11... | collective-permute-start | bytes 6291464 | tf_op jit(solution)/shard_map/ppermute | solution.py:586
  0.7 25.5 %collective-permute-start.1 = (bf16[512,2048]{1,0:T(8,128)(2,1)}, bf16[512,2048]{1,0:T(8,128)(2,1)}, u32[]{:S(2)}, u32[]{:S(2)}) collective-permute-start(bf16[512,2048]{1,0:T(8,128)(2,1)} %refs_4_.3), channel_id=1, source_target_pairs={{0,1},{1,0},{2,3},{3,2},{4,5},{5,4},{6,7},{7,6},{8,9},{9,8},{10,11... | collective-permute-start | bytes 6291464 | tf_op jit(solution)/shard_map/ppermute | solution.py:587
  2.2 18.5 %all-to-all-start.2 = ((s32[128,1,48]{2,1,0:T(1,128)}), s32[128,1,48]{2,1,0:T(1,128)S(1)}, u32[]{:S(2)}, u32[]{:S(2)}) async-start(s32[128,1,48]{2,1,0:T(1,128)} %broadcast_in_dim.56), calls=%async_computation.2 | async-start | bytes 131072 | tf_op jit(solution)/shard_map/all_to_all | solution.py:589
  26.2 1.3 copy-start.3
  240.6 40.7 %copy-start.1 = (bf16[512,2048]{1,0:T(8,128)(2,1)S(1)}, bf16[512,2048]{1,0:T(8,128)(2,1)}, u32[]{:S(2)}) copy-start(bf16[512,2048]{1,0:T(8,128)(2,1)} %query) | copy-start | bytes 6291460
  257.1 107.5 %collective-permute-start.2 = (bf16[6,1024,128]{2,1,0:T(8,128)(2,1)}, bf16[6,1024,128]{2,1,0:T(8,128)(2,1)}, u32[]{:S(2)}, u32[]{:S(2)}) collective-permute-start(bf16[6,1024,128]{2,1,0:T(8,128)(2,1)} %get-tuple-element.197), channel_id=1, source_target_pairs={{1,0},{0,1},{3,2},{2,3},{5,4},{4,5},{7,6},{6,7},{9,8},{8,9},{11,10... | collective-permute-start | bytes 4718600 | tf_op jit(solution)/shard_map/ppermute | solution.py:598
  258.5 51.5 %collective-permute-start.10 = (bf16[1,1024,128]{2,1,0:T(8,128)(2,1)}, bf16[1,1024,128]{2,1,0:T(8,128)(2,1)S(1)}, u32[]{:S(2)}, u32[]{:S(2)}) collective-permute-start(bf16[1,1024,128]{2,1,0:T(8,128)(2,1)} %get-tuple-element.205), channel_id=1, source_target_pairs={{25,0},{24,1},{27,2},{26,3},{29,4},{28,5},{31,6},{30,7},{1,8},{0,9... | collective-permute-start | bytes 786440 | tf_op jit(solution)/shard_map/ppermute | solution.py:598
  260.7 51.2 %collective-permute-start.11 = (bf16[1,1024,128]{2,1,0:T(8,128)(2,1)}, bf16[1,1024,128]{2,1,0:T(8,128)(2,1)}, u32[]{:S(2)}, u32[]{:S(2)}) collective-permute-start(bf16[1,1024,128]{2,1,0:T(8,128)(2,1)} %get-tuple-element.206), channel_id=1, source_target_pairs={{2,0},{3,1},{4,2},{5,3},{6,4},{7,5},{0,6},{1,7},{10,8},{11,9},{12,... | collective-permute-start | bytes 786440 | tf_op jit(solution)/shard_map/ppermute | solution.py:598
  261.6 53.2 %collective-permute-start.12 = (bf16[1,1024,128]{2,1,0:T(8,128)(2,1)}, bf16[1,1024,128]{2,1,0:T(8,128)(2,1)}, u32[]{:S(2)}, u32[]{:S(2)}) collective-permute-start(bf16[1,1024,128]{2,1,0:T(8,128)(2,1)} %get-tuple-element.207), channel_id=1, source_target_pairs={{3,0},{2,1},{5,2},{4,3},{7,4},{6,5},{1,6},{0,7},{11,8},{10,9},{13,... | collective-permute-start | bytes 786440 | tf_op jit(solution)/shard_map/ppermute | solution.py:598
  262.8 53.2 %collective-permute-start.13 = (bf16[1,1024,128]{2,1,0:T(8,128)(2,1)}, bf16[1,1024,128]{2,1,0:T(8,128)(2,1)}, u32[]{:S(2)}, u32[]{:S(2)}) collective-permute-start(bf16[1,1024,128]{2,1,0:T(8,128)(2,1)} %get-tuple-element.208), channel_id=1, source_target_pairs={{6,0},{7,1},{0,2},{1,3},{2,4},{3,5},{4,6},{5,7},{14,8},{15,9},{8,1... | collective-permute-start | bytes 786440 | tf_op jit(solution)/shard_map/ppermute | solution.py:598
  263.7 100.8 %all-to-all-start.4 = ((bf16[64,64,128]{2,1,0:T(8,128)(2,1)}), bf16[64,64,128]{2,1,0:T(8,128)(2,1)S(1)}, u32[]{:S(2)}, u32[]{:S(2)}) async-start(bf16[64,64,128]{2,1,0:T(8,128)(2,1)} %get-tuple-element.196), calls=%async_computation.4 | async-start | bytes 2097152 | tf_op jit(solution)/shard_map/all_to_all | solution.py:553
  310.1 34.3 %copy-start.5 = (bf16[1,1024,128]{2,1,0:T(8,128)(2,1)}, bf16[1,1024,128]{2,1,0:T(8,128)(2,1)S(1)}, u32[]{:S(2)}) copy-start(bf16[1,1024,128]{2,1,0:T(8,128)(2,1)S(1)} %collective-permute-done.10.rest_8_) | copy-start | bytes 786436
  310.1 34.3 %collective-permute-start.14 = (bf16[1,1024,128]{2,1,0:T(8,128)(2,1)}, bf16[1,1024,128]{2,1,0:T(8,128)(2,1)S(1)}, u32[]{:S(2)}, u32[]{:S(2)}) collective-permute-start(bf16[1,1024,128]{2,1,0:T(8,128)(2,1)} %get-tuple-element.209), channel_id=1, source_target_pairs={{7,0},{6,1},{1,2},{0,3},{3,4},{2,5},{5,6},{4,7},{15,8},{14,9},{9,1... | collective-permute-start | bytes 786440 | tf_op jit(solution)/shard_map/ppermute | solution.py:598
  311.9 33.4 %collective-permute-start.3 = (bf16[1,1024,128]{2,1,0:T(8,128)(2,1)}, bf16[1,1024,128]{2,1,0:T(8,128)(2,1)S(1)}, u32[]{:S(2)}, u32[]{:S(2)}) collective-permute-start(bf16[1,1024,128]{2,1,0:T(8,128)(2,1)} %get-tuple-element.198), channel_id=1, source_target_pairs={{32,0},{33,1},{34,2},{35,3},{36,4},{37,5},{38,6},{39,7},{40,8},{41... | collective-permute-start | bytes 786440 | tf_op jit(solution)/shard_map/ppermute | solution.py:598
  314.8 30.7 %collective-permute-start.4 = (bf16[1,1024,128]{2,1,0:T(8,128)(2,1)}, bf16[1,1024,128]{2,1,0:T(8,128)(2,1)}, u32[]{:S(2)}, u32[]{:S(2)}) collective-permute-start(bf16[1,1024,128]{2,1,0:T(8,128)(2,1)} %get-tuple-element.199), channel_id=1, source_target_pairs={{33,0},{32,1},{35,2},{34,3},{37,4},{36,5},{39,6},{38,7},{41,8},{40... | collective-permute-start | bytes 786440 | tf_op jit(solution)/shard_map/ppermute | solution.py:598
  316.0 31.4 %collective-permute-start.5 = (bf16[1,1024,128]{2,1,0:T(8,128)(2,1)}, bf16[1,1024,128]{2,1,0:T(8,128)(2,1)}, u32[]{:S(2)}, u32[]{:S(2)}) collective-permute-start(bf16[1,1024,128]{2,1,0:T(8,128)(2,1)} %get-tuple-element.200), channel_id=1, source_target_pairs={{96,0},{97,1},{98,2},{99,3},{100,4},{101,5},{102,6},{103,7},{104,8... | collective-permute-start | bytes 786440 | tf_op jit(solution)/shard_map/ppermute | solution.py:598
  344.4 18.2 %copy-start.6 = (bf16[1,1024,128]{2,1,0:T(8,128)(2,1)}, bf16[1,1024,128]{2,1,0:T(8,128)(2,1)S(1)}, u32[]{:S(2)}) copy-start(bf16[1,1024,128]{2,1,0:T(8,128)(2,1)S(1)} %collective-permute-done.14.rest_12_) | copy-start | bytes 786436
  344.4 20.1 %collective-permute-start.6 = (bf16[1,1024,128]{2,1,0:T(8,128)(2,1)}, bf16[1,1024,128]{2,1,0:T(8,128)(2,1)S(1)}, u32[]{:S(2)}, u32[]{:S(2)}) collective-permute-start(bf16[1,1024,128]{2,1,0:T(8,128)(2,1)} %get-tuple-element.201), channel_id=1, source_target_pairs={{97,0},{96,1},{99,2},{98,3},{101,4},{100,5},{103,6},{102,7},{105,8... | collective-permute-start | bytes 786440 | tf_op jit(solution)/shard_map/ppermute | solution.py:598
  345.3 17.3 %copy-start.7 = (bf16[1,1024,128]{2,1,0:T(8,128)(2,1)}, bf16[1,1024,128]{2,1,0:T(8,128)(2,1)S(1)}, u32[]{:S(2)}) copy-start(bf16[1,1024,128]{2,1,0:T(8,128)(2,1)S(1)} %collective-permute-done.3.rest_1_) | copy-start | bytes 786436
  345.3 19.2 %collective-permute-start.7 = (bf16[1,1024,128]{2,1,0:T(8,128)(2,1)}, bf16[1,1024,128]{2,1,0:T(8,128)(2,1)}, u32[]{:S(2)}, u32[]{:S(2)}) collective-permute-start(bf16[1,1024,128]{2,1,0:T(8,128)(2,1)} %get-tuple-element.202), channel_id=1, source_target_pairs={{8,0},{9,1},{10,2},{11,3},{12,4},{13,5},{14,6},{15,7},{16,8},{17,9... | collective-permute-start | bytes 786440 | tf_op jit(solution)/shard_map/ppermute | solution.py:598
  345.6 18.9 %collective-permute-start.8 = (bf16[1,1024,128]{2,1,0:T(8,128)(2,1)}, bf16[1,1024,128]{2,1,0:T(8,128)(2,1)}, u32[]{:S(2)}, u32[]{:S(2)}) collective-permute-start(bf16[1,1024,128]{2,1,0:T(8,128)(2,1)} %get-tuple-element.203), channel_id=1, source_target_pairs={{9,0},{8,1},{11,2},{10,3},{13,4},{12,5},{15,6},{14,7},{17,8},{16,9... | collective-permute-start | bytes 786440 | tf_op jit(solution)/shard_map/ppermute | solution.py:598
  347.4 17.1 %collective-permute-start.9 = (bf16[1,1024,128]{2,1,0:T(8,128)(2,1)}, bf16[1,1024,128]{2,1,0:T(8,128)(2,1)}, u32[]{:S(2)}, u32[]{:S(2)}) collective-permute-start(bf16[1,1024,128]{2,1,0:T(8,128)(2,1)} %get-tuple-element.204), channel_id=1, source_target_pairs={{24,0},{25,1},{26,2},{27,3},{28,4},{29,5},{30,6},{31,7},{0,8},{1,9... | collective-permute-start | bytes 786440 | tf_op jit(solution)/shard_map/ppermute | solution.py:598
  364.5 0.7 copy-start.8
  364.5 1.0 copy-start.4

commit v5 on v4

--- a/solution.py
+++ b/solution.py
@@ -19,10 +19,12 @@
 SHIFTS = [(0, 0, 0, 1)] * PARTNER
 SHIFTS += [(*s, c) for s in ONE for c in (0, 1)]
 KINDS = len(SHIFTS)
-SPARE = 4
+SPARE = 5
 PIECE = 16
-PARTS = 4
-SLOT_ROWS = 2 * BLOCK + SPARE * PIECE
+PARTS = (0, 6, 11, 16)
+HALF = BLOCK // PIECE
+SLOT_PIECES = 2 * HALF + SPARE
+SLOT_ROWS = SLOT_PIECES * PIECE
 
 ROW_DIRECT = CHIPS
 ROW_SPARE = ROW_DIRECT + CHIPS
@@ -155,21 +157,22 @@
 
     def one_slot(dest, carry):
         code = plan[chip, 2 * dest + core]
-        head = code % 16
+
+        def copy(*sources):
+            for half, source in enumerate(sources):
+                pltpu.make_async_copy(
+                    source.at[:, :, columns(code % 16)],
+                    send.at[dest // 2, dest % 2, pl.ds(half * HALF, HALF)],
+                    sem,
+                ).start()
 
         @pl.when(code // 16 == core)
         def _():
-            for half, source in enumerate((keys, values)):
-                pltpu.make_async_copy(
-                    source.at[:, columns(head)], send.at[dest, pl.ds(half * BLOCK, BLOCK)], sem
-                ).start()
+            copy(keys, values)
 
         @pl.when(code // 16 != core)
         def _():
-            for half, source in enumerate((other_keys, other_values)):
-                pltpu.make_async_copy(
-                    source.at[:, columns(head)], send.at[dest, pl.ds(half * BLOCK, BLOCK)], sem
-                ).start()
+            copy(other_keys, other_values)
 
         return carry
 
@@ -177,28 +180,22 @@
 
     def one_spare(index, carry):
         head = jnp.maximum(plan[ROW_SPARE + chip, 2 * index + core] - 1, 0)
-        into = pl.ds(pl.multiple_of(2 * BLOCK + index * PIECE, PIECE), PIECE)
-
-        def one_piece(piece, carry):
-            rows = pl.ds(pl.multiple_of(piece * PIECE, PIECE), PIECE)
-
-            @pl.when(core == 1)
-            def _():
-                for half, source in enumerate((keys, values)):
-                    pltpu.make_async_copy(
-                        source.at[rows, columns(head)], send.at[2 * piece + half, into], sem
-                    ).start()
-
-            @pl.when(core == 0)
-            def _():
-                for half, source in enumerate((other_keys, other_values)):
-                    pltpu.make_async_copy(
-                        source.at[rows, columns(head)], send.at[2 * piece + half, into], sem
-                    ).start()
-
-            return carry
-
-        return lax.fori_loop(0, CHIPS // 2, one_piece, carry)
+
+        def copy(*sources):
+            for half, source in enumerate(sources):
+                pltpu.make_async_copy(
+                    source.at[:, :, columns(head)], send.at[:, half, 2 * HALF + index], sem
+                ).start()
+
+        @pl.when(core == 1)
+        def _():
+            copy(keys, values)
+
+        @pl.when(core == 0)
+        def _():
+            copy(other_keys, other_values)
+
+        return carry
 
     lax.fori_loop(0, SPARE, one_spare, 0)
     pltpu.make_async_copy(send, send, sem).wait()
@@ -211,7 +208,7 @@
 
 
 def tiles(count):
-    return jax.ShapeDtypeStruct((count, 2 * BLOCK, HEAD), jnp.bfloat16)
+    return jax.ShapeDtypeStruct((count, 2 * HALF, PIECE, HEAD), jnp.bfloat16)
 
 
 def pack(plan, me, keys, values, other_keys, other_values):
@@ -219,43 +216,60 @@
         pack_kernel,
         in_specs=[SMEM, SMEM, VMEM, VMEM, VMEM, VMEM],
         out_specs=ANY,
-        out_shape=jax.ShapeDtypeStruct((CHIPS, SLOT_ROWS, HEAD), jnp.bfloat16),
+        out_shape=jax.ShapeDtypeStruct((HALF, 2, SLOT_PIECES, PIECE, HEAD), jnp.bfloat16),
         scratch_shapes=[pltpu.SemaphoreType.DMA],
         compiler_params=BIG,
         name="pack",
-    )(plan, me, keys, values, other_keys, other_values)
+    )(plan, me, *(a.reshape(HALF, PIECE, -1) for a in (keys, values, other_keys, other_values)))
 
 
 def forward_kernel(plan, me_ref, arrived, *rest):
-    outs, (moving, gathered, sems, out_sems) = rest[:-4], rest[-4:]
+    outs, (where, moving, spare, gathered, sems, out_sems) = rest[:-6], rest[-6:]
     me = me_ref[0]
     core = me % 2
     loads, stores = [], []
     for kind in range(KINDS):
         out = outs[1].at[kind] if kind < PARTNER else outs[kind - PARTNER + 2].at[0]
-        source = arrived.at[plan[ROW_FORWARD + kind, me], pl.ds(0, 2 * BLOCK)]
+        source = arrived.at[plan[ROW_FORWARD + kind, me], pl.ds(0, 2 * HALF)]
         loads.append(pltpu.make_async_copy(source, moving.at[kind], sems.at[kind]))
         stores.append(pltpu.make_async_copy(moving.at[kind], out, out_sems.at[kind]))
     for load in loads:
         load.start()
 
+    load_spare = pltpu.make_async_copy(
+        arrived.at[:, pl.ds(2 * HALF, SPARE)], spare, sems.at[KINDS]
+    )
+    load_spare.start()
+
+    def note(head_plus, code):
+        @pl.when(head_plus > 0)
+        def _():
+            at = where[3 * HEADS + head_plus - 1]
+            where[(head_plus - 1) * 3 + jnp.minimum(at, 2)] = code
+            where[3 * HEADS + head_plus - 1] = at + 1
+
+    for entry in range(4 * HEADS):
+        where[entry] = 0
+
+    def direct(chip, carry):
+        note(plan[ROW_DIRECT + chip, me], chip)
+        return carry
+
+    lax.fori_loop(0, CHIPS, direct, 0)
+    note(plan[ROW_PARTNER, me], CHIPS)
+    for load, store in zip(loads, stores):
+        load.wait()
+        store.start()
+    load_spare.wait()
+
     def one_dest(dest, carry):
         for index in range(SPARE):
             chip = plan[ROW_FROM + index, 2 * dest + core]
             rank = plan[ROW_FROM_RANK + index, 2 * dest + core]
-            row = pl.multiple_of(2 * BLOCK + rank * PIECE, PIECE)
-            pltpu.make_async_copy(
-                arrived.at[chip, pl.ds(row, PIECE)],
-                gathered.at[dest, pl.ds(index * PIECE, PIECE)],
-                sems.at[KINDS],
-            ).start()
+            gathered[dest, index] = spare[chip, rank]
         return carry
 
     lax.fori_loop(0, CHIPS, one_dest, 0)
-    for load, store in zip(loads, stores):
-        load.wait()
-        store.start()
-    pltpu.make_async_copy(gathered, gathered, sems.at[KINDS]).wait()
     last = pltpu.make_async_copy(gathered, outs[0], out_sems.at[KINDS])
     last.start()
     for store in stores:
@@ -267,19 +281,21 @@
     return pl.pallas_call(
         forward_kernel,
         in_specs=[SMEM, SMEM, ANY],
-        out_specs=[ANY] * (KINDS - PARTNER + 2),
-        out_shape=[jax.ShapeDtypeStruct((CHIPS, SPARE * PIECE, HEAD), jnp.bfloat16)]
+        out_specs=[ANY] * (KINDS - PARTNER + 2) + [SMEM],
+        out_shape=[jax.ShapeDtypeStruct((CHIPS, SPARE, PIECE, HEAD), jnp.bfloat16)]
         + [tiles(PARTNER)]
-        + [tiles(1)] * (KINDS - PARTNER),
+        + [tiles(1)] * (KINDS - PARTNER)
+        + [jax.ShapeDtypeStruct((4 * HEADS,), jnp.int32)],
         scratch_shapes=[
-            pltpu.VMEM((KINDS, 2 * BLOCK, HEAD), jnp.bfloat16),
-            pltpu.VMEM((CHIPS, SPARE * PIECE, HEAD), jnp.bfloat16),
+            pltpu.VMEM((KINDS, 2 * HALF, PIECE, HEAD), jnp.bfloat16),
+            pltpu.VMEM((CHIPS, SPARE, PIECE, HEAD), jnp.bfloat16),
+            pltpu.VMEM((CHIPS, SPARE, PIECE, HEAD), jnp.bfloat16),
             pltpu.SemaphoreType.DMA((KINDS + 1,)),
             pltpu.SemaphoreType.DMA((KINDS + 1,)),
         ],
         compiler_params=BIG,
         name="forward",
-    )(plan, me, arrived)
+    )(plan, me, arrived.reshape(CHIPS, SLOT_PIECES, PIECE, HEAD))
 
 
 def scores_of(query, key):
@@ -288,19 +304,33 @@
     )
 
 
-def attend_kernel(first, last, plan, me_ref, query, own_key, own_value, *rest):
+ROWS_AT_ONCE = 256
+
+
+def add_tile(query, key, value, state):
+    results = []
+    for start in range(0, BLOCK, ROWS_AT_ONCE):
+        rows = slice(start, start + ROWS_AT_ONCE)
+        scores = scores_of(query[rows, :], key)
+        old = state[rows, 2 * HEAD :]
+        highest = jnp.maximum(old, jnp.max(scores, axis=1, keepdims=True))
+        keep = jnp.exp2((old - highest) * SCALE)
+        weight = jnp.exp2((scores - highest[:, :1]) * SCALE).astype(jnp.bfloat16)
+        added = jnp.dot(weight, value, preferred_element_type=jnp.float32)
+        total = state[rows, 0:HEAD] * keep + added[:, :HEAD]
+        norm = state[rows, HEAD : 2 * HEAD] * keep + added[:, HEAD:]
+        results.append((rows, total, norm, highest))
+    for rows, total, norm, highest in results:
+        state[rows, 0:HEAD] = total
+        state[rows, HEAD : 2 * HEAD] = norm
+        state[rows, 2 * HEAD :] = highest
+
+
+def attend_kernel(first, last, where, query, own_key, own_value, *rest):
     other_keys, other_values, arrived = rest[:3]
-    out, state, where, filled, key_buf, value_buf, sems = rest[-7:]
-    me = me_ref[0]
+    out, state, key_buf, value_buf, sems = rest[-5:]
     step = pl.program_id(0)
     head = step + first
-
-    def note(head_plus, code):
-        @pl.when(head_plus > 0)
-        def _():
-            at = filled[head_plus - 1]
-            where[(head_plus - 1) * 3 + jnp.minimum(at, 2)] = code
-            filled[head_plus - 1] = at + 1
 
     def fetch(head, slot):
         for j in range(3):
@@ -312,7 +342,7 @@
                 pltpu.make_async_copy(source_key, into_key, sems.at[slot, j, 0]).start()
                 pltpu.make_async_copy(source_value, into_value, sems.at[slot, j, 1]).start()
 
-            @pl.when((code >= 0) & (code < CHIPS))
+            @pl.when(code < CHIPS)
             def _():
                 start(arrived.at[code, pl.ds(0, BLOCK)], arrived.at[code, pl.ds(BLOCK, BLOCK)])
 
@@ -322,19 +352,11 @@
 
     @pl.when(step == 0)
     def _():
-        for h in range(HEADS):
-            filled[h] = 0
+        fetch(first, 0)
+        ones = jnp.ones((BLOCK, HEAD), jnp.bfloat16)
+        for pair in range(2):
             for j in range(3):
-                where[h * 3 + j] = -1
-        value_buf[...] = jnp.ones(value_buf.shape, value_buf.dtype)
-
-        def direct(chip, carry):
-            note(plan[ROW_DIRECT + chip, me], chip)
-            return carry
-
-        lax.fori_loop(0, CHIPS, direct, 0)
-        note(plan[ROW_PARTNER, me], CHIPS)
-        fetch(first, 0)
+                value_buf[pair, j, :, HEAD:] = ones
 
     slot = step % 2
 
@@ -342,75 +364,59 @@
     def _():
         fetch(head + 1, 1 - slot)
 
-    present = jnp.minimum(filled[head], 3)
     for j in range(3):
-
-        @pl.when(j < present)
-        def _():
-            pltpu.make_async_copy(
-                arrived.at[0, pl.ds(0, BLOCK)], key_buf.at[slot, j], sems.at[slot, j, 0]
-            ).wait()
-            pltpu.make_async_copy(
-                arrived.at[0, pl.ds(BLOCK, BLOCK)],
-                value_buf.at[slot, j, :, pl.ds(0, HEAD)],
-                sems.at[slot, j, 1],
-            ).wait()
-
-    def work(count):
-        rows = 256
-        for part in range(BLOCK // rows):
-            length = (part + 1) * rows
-            span = pl.ds(part * rows, rows)
-            q = query[span, :]
-            own = scores_of(q, own_key[0:length, :])
-            row_iota = lax.broadcasted_iota(jnp.int32, (rows, length), 0) + part * rows
-            col_iota = lax.broadcasted_iota(jnp.int32, (rows, length), 1)
-            own = jnp.where(col_iota <= row_iota, own, -jnp.inf)
-            others = [scores_of(q, key_buf[slot, j]) for j in range(count)]
-            highest = jnp.max(own, axis=1, keepdims=True)
-            for other in others:
-                highest = jnp.maximum(highest, jnp.max(other, axis=1, keepdims=True))
-            weight = jnp.exp2((own - highest) * SCALE).astype(jnp.bfloat16)
-            ones = jnp.ones((length, HEAD), jnp.bfloat16)
-            total = jnp.dot(
-                weight,
-                jnp.concatenate([own_value[0:length, :], ones], axis=1),
-                preferred_element_type=jnp.float32,
-            )
-            for j, other in enumerate(others):
-                weight = jnp.exp2((other - highest) * SCALE).astype(jnp.bfloat16)
-                total = total + jnp.dot(
-                    weight, value_buf[slot, j], preferred_element_type=jnp.float32
-                )
-            out[span, :] = (total[:, :HEAD] / total[:, HEAD:]).astype(jnp.bfloat16)
-            if count < 3:
-                state[0, span, 0 : 2 * HEAD] = total
-                state[0, span, 2 * HEAD :] = jnp.broadcast_to(highest, (rows, HEAD))
-
-    for count in range(4):
-
-        @pl.when(present == count)
-        def _():
-            work(count)
-
-
-def attend(first, last, before, plan, me, queries, keys, values, others, arrived):
+        pltpu.make_async_copy(
+            arrived.at[0, pl.ds(0, BLOCK)], key_buf.at[slot, j], sems.at[slot, j, 0]
+        ).wait()
+        pltpu.make_async_copy(
+            arrived.at[0, pl.ds(BLOCK, BLOCK)],
+            value_buf.at[slot, j, :, pl.ds(0, HEAD)],
+            sems.at[slot, j, 1],
+        ).wait()
+    present = where[3 * HEADS + head]
+
+    for start in range(0, BLOCK, ROWS_AT_ONCE):
+        stop = start + ROWS_AT_ONCE
+        q = query[start:stop, :]
+        own = scores_of(q, own_key[0:stop, :])
+        row_iota = lax.broadcasted_iota(jnp.int32, own.shape, 0) + start
+        col_iota = lax.broadcasted_iota(jnp.int32, own.shape, 1)
+        own = jnp.where(col_iota <= row_iota, own, -jnp.inf)
+        highest = jnp.max(own, axis=1, keepdims=True)
+        weight = jnp.exp2((own - highest) * SCALE).astype(jnp.bfloat16)
+        ones = jnp.ones((stop, HEAD), jnp.bfloat16)
+        value = jnp.concatenate([own_value[0:stop, :], ones], axis=1)
+        total = jnp.dot(weight, value, preferred_element_type=jnp.float32)
+        for j in range(3):
+            scores = scores_of(q, key_buf[slot, j])
+            top = jnp.where(j < present, jnp.max(scores, axis=1, keepdims=True), -jnp.inf)
+            top = jnp.maximum(highest, top)
+            keep = jnp.exp2((highest - top) * SCALE)
+            base = jnp.where(j < present, top, jnp.inf)
+            weight = jnp.exp2((scores - base) * SCALE).astype(jnp.bfloat16)
+            added = jnp.dot(weight, value_buf[slot, j], preferred_element_type=jnp.float32)
+            total = total * keep + added
+            highest = top
+        out[start:stop, :] = (total[:, :HEAD] / total[:, HEAD:]).astype(jnp.bfloat16)
+        state[0, start:stop, 0 : 2 * HEAD] = total
+        state[0, start:stop, 2 * HEAD :] = jnp.broadcast_to(highest, (ROWS_AT_ONCE, HEAD))
+
+
+def attend(first, last, before, where, queries, keys, values, others, arrived):
     block = pl.BlockSpec((BLOCK, HEAD), lambda h: (0, h + first))
     count = last - first
     size = count * BLOCK * 4 * BLOCK * HEAD
     return pl.pallas_call(
         lambda *refs: attend_kernel(first, last, *refs),
         grid=(count,),
-        in_specs=[SMEM, SMEM, block, block, block, ANY, ANY, ANY] + [ANY] * len(before),
+        in_specs=[SMEM, block, block, block, ANY, ANY, ANY] + [ANY] * len(before),
         out_specs=[block, pl.BlockSpec((1, BLOCK, 3 * HEAD), lambda h: (h + first, 0, 0))],
         out_shape=[
             jax.ShapeDtypeStruct((BLOCK, HEADS * HEAD), jnp.bfloat16),
             jax.ShapeDtypeStruct((HEADS, BLOCK, 3 * HEAD), jnp.float32),
         ],
-        input_output_aliases={8: 0, 9: 1} if before else {},
+        input_output_aliases={7: 0, 8: 1} if before else {},
         scratch_shapes=[
-            pltpu.SMEM((3 * HEADS,), jnp.int32),
-            pltpu.SMEM((HEADS,), jnp.int32),
             pltpu.VMEM((2, 3, BLOCK, HEAD), jnp.bfloat16),
             pltpu.VMEM((2, 3, BLOCK, 2 * HEAD), jnp.bfloat16),
             pltpu.SemaphoreType.DMA((2, 3, 2)),
@@ -420,7 +426,7 @@
         ),
         compiler_params=BIG,
         name="attend",
-    )(plan, me, queries, keys, values, *others, arrived, *before)
+    )(where, queries, keys, values, *others, arrived, *before)
 
 
 PENDING = KINDS + SPARE
@@ -474,19 +480,12 @@
     def one_spare(index, carry):
         @pl.when(head_of(KINDS + index) > 0)
         def _():
-            from_row = pl.ds(pl.multiple_of(index * PIECE, PIECE), PIECE)
-
-            def one_piece(piece, carry):
-                for half in range(2):
-                    row = pl.multiple_of(half * BLOCK + piece * PIECE, PIECE)
-                    pltpu.make_async_copy(
-                        pieces.at[2 * piece + half, from_row],
-                        tile_buf.at[KINDS + index, pl.ds(row, PIECE)],
-                        sems.at[KINDS + index],
-                    ).start()
-                return carry
-
-            lax.fori_loop(0, BLOCK // PIECE, one_piece, 0)
+            for half in range(2):
+                pltpu.make_async_copy(
+                    pieces.at[:, half, index],
+                    tile_buf.at[KINDS + index, pl.ds(half * HALF, HALF)],
+                    sems.at[KINDS + index],
+                ).start()
 
         return carry
 
@@ -498,29 +497,22 @@
         def _():
             h = head_of(index) - 1
             pltpu.make_async_copy(tile_buf.at[0], tile_buf.at[index], sems.at[index]).wait()
-            key = tile_buf[index, 0:BLOCK, :]
+            key = tile_buf[index, 0:HALF].reshape(BLOCK, HEAD)
             ones = jnp.ones((BLOCK, HEAD), jnp.bfloat16)
-            value = jnp.concatenate([tile_buf[index, BLOCK:, :], ones], axis=1)
-            rows = 256
-            for part in range(BLOCK // rows):
-                span = pl.ds(part * rows, rows)
-                scores = scores_of(query[span, columns(h)], key)
-                old = carried[h, span, 2 * HEAD :]
-                highest = jnp.maximum(old, jnp.max(scores, axis=1, keepdims=True))
-                keep = jnp.exp2((old - highest) * SCALE)
-                weight = jnp.exp2((scores - highest[:, :1]) * SCALE).astype(jnp.bfloat16)
-                added = jnp.dot(weight, value, preferred_element_type=jnp.float32)
-                total = carried[h, span, 0:HEAD] * keep + added[:, :HEAD]
-                norm = carried[h, span, HEAD : 2 * HEAD] * keep + added[:, HEAD:]
-                carried[h, span, 0:HEAD] = total
-                carried[h, span, HEAD : 2 * HEAD] = norm
-                carried[h, span, 2 * HEAD :] = highest
-                done_buf[h, span, :] = (total / norm).astype(jnp.bfloat16)
+            value = tile_buf[index, HALF : 2 * HALF].reshape(BLOCK, HEAD)
+            value = jnp.concatenate([value, ones], axis=1)
+            add_tile(query.at[:, columns(h)], key, value, carried.at[h])
 
         return carry
 
     lax.fori_loop(0, PENDING, one_tile, 0)
-    each_waiting(lambda h: store_out(h).start())
+
+    def finish(h):
+        total, norm = carried[h, :, 0:HEAD], carried[h, :, HEAD : 2 * HEAD]
+        done_buf[h] = (total / norm).astype(jnp.bfloat16)
+        store_out(h).start()
+
+    each_waiting(finish)
     each_waiting(lambda h: store_out(h).wait())
 
 
@@ -534,7 +526,7 @@
         scratch_shapes=[
             pltpu.SMEM((HEADS,), jnp.int32),
             pltpu.VMEM((HEADS, BLOCK, 3 * HEAD), jnp.float32),
-            pltpu.VMEM((PENDING, 2 * BLOCK, HEAD), jnp.bfloat16),
+            pltpu.VMEM((PENDING, 2 * HALF, PIECE, HEAD), jnp.bfloat16),
             pltpu.VMEM((HEADS, BLOCK, HEAD), jnp.bfloat16),
             pltpu.SemaphoreType.DMA((HEADS,)),
             pltpu.SemaphoreType.DMA((PENDING,)),
@@ -542,7 +534,7 @@
         ],
         compiler_params=BIG,
         name="merge",
-    )(plan, me, queries, state, out, pieces, *forwarded)
+    )(plan, me, queries, state, out, pieces.reshape(HALF, 2, SPARE, PIECE, HEAD), *forwarded)
 
 
 LANES = [[2 * chip + core for chip in range(CHIPS)] for core in range(2)]
@@ -589,24 +581,23 @@
     chosen_all = lax.all_to_all(spread, "ctx", 0, 0, tiled=True)
     plan = make_plan(chosen_all.T)
     send = pack(plan, me_ref, keys, values, other_keys, other_values)
-    held = (exchange(send), plan, queries, keys, values, other_keys, other_values, me_ref)
+    sent = exchange(send.reshape(CHIPS, SLOT_ROWS, HEAD))
+    held = (sent, plan, queries, keys, values, other_keys, other_values, me_ref)
     held = lax.optimization_barrier(held)
     arrived, plan, queries, keys, values, other_keys, other_values, me_ref = held
-    pieces, *outgoing = forward(plan, me_ref, arrived)
+    pieces, *outgoing, where = forward(plan, me_ref, arrived)
     pieces = exchange(pieces)
     forwarded = [
         lax.ppermute(array, "ctx", shift_pairs(SHIFTS[0] if n == 0 else SHIFTS[PARTNER + n - 1]))
         for n, array in enumerate(outgoing)
     ]
     parts = ()
-    step = HEADS // PARTS
-    for first in range(0, HEADS, step):
+    for first, last in zip(PARTS[:-1], PARTS[1:]):
         parts = attend(
             first,
-            first + step,
+            last,
             parts,
-            plan,
-            me_ref,
+            where,
             queries,
             keys,
             values,

time: 387 us -> 352 us (0.910)
  Pallas kernels: 106 us -> 83.2 us
  starting transfers between devices: 59.6 us -> 45.7 us
    pallas_call x4 -> x3, Pallas kernels: 57 us -> 39.5 us  [attend(): pl.pallas_call(lambda *refs: attend_kernel(first, last, *refs), grid=(cou...]
    ppermute x13, starting transfers between devices: 30.7 us -> 17.1 us  [body(): lax.ppermute(array, 'ctx', shift_pairs(SHIFTS[0] if n == 0 else SHIFTS[PA...]
    pallas_call x1, Pallas kernels: 16.5 us -> 11.3 us  [forward(): pl.pallas_call(forward_kernel, in_specs=[SMEM, SMEM, ANY], out_specs=[ANY...]
  transfers between devices with their start and end apart: 17 -> 17, of which waited for: 1 -> 1; matrix products, arithmetic and copies ran while one was open for 1% -> 1% of each run, Pallas kernels for 16% -> 13%
where the time goes in v5:
time: 352 us; the launch traced here: 349 us
  blocking collectives  206 us (59%)
  Pallas kernels  83.2 us (24%)
  starting transfers between devices  45.7 us (13%)
  waiting for transfers between devices  7.91 us (2%)
  local copies, waits for them, and re-layouts  5.15 us (1%)
    all_to_all x1, blocking collectives, exchange(): lax.all_to_all(array, 'ctx', 0, 0, axis_index_groups=LANES, tiled=True)  206 us
    pallas_call x3, Pallas kernels, attend(): pl.pallas_call(lambda *refs: attend_kernel(first, last, *refs), grid=(cou...  39.5 us
    all_to_all x1, starting transfers between devices, exchange(): lax.all_to_all(array, 'ctx', 0, 0, axis_index_groups=LANES, tiled=True)  17.2 us
    pallas_call x1, Pallas kernels, merge(): pl.pallas_call(merge_kernel, in_specs=[SMEM, SMEM, VMEM, ANY, ANY, ANY] +...  17.2 us
    ppermute x13, starting transfers between devices, body(): lax.ppermute(array, 'ctx', shift_pairs(SHIFTS[0] if n == 0 else SHIFTS[PA...  17.1 us
    pallas_call x1, Pallas kernels, forward(): pl.pallas_call(forward_kernel, in_specs=[SMEM, SMEM, ANY], out_specs=[ANY...  11.3 us
    all_to_all x1, starting transfers between devices, body(): chosen_all = lax.all_to_all(spread, 'ctx', 0, 0, tiled=True)  10.6 us
    pallas_call x1, Pallas kernels, pack(): pl.pallas_call(pack_kernel, in_specs=[SMEM, SMEM, VMEM, VMEM, VMEM, VMEM]...  9.74 us
  transfers between devices with their start and end apart: 17, of which 1 were waited for; matrix products, arithmetic and copies ran while one was open for 1% of the time, Pallas kernels for 13%

profile of v5, /device:TPU:7, one launch (start us, length us, event | category | flops | bytes accessed | tf_op | source)
XLA Modules:
  0.0 348.6 jit_solution(11380442862804802019)
XLA Ops:
  0.0 0.7 collective-permute-start
  0.7 0.0 collective-permute-start.1
  0.7 0.8 copy.32
  1.4 0.1 broadcast_in_dim.55
  1.5 0.7 broadcast_in_dim.56
  2.2 10.6 %all-to-all-start.2 = ((s32[128,1,48]{2,1,0:T(1,128)}), s32[128,1,48]{2,1,0:T(1,128)S(1)}, u32[]{:S(2)}, u32[]{:S(2)}) async-start(s32[128,1,48]{2,1,0:T(1,128)} %broadcast_in_dim.56), calls=%async_computation.2 | async-start | bytes 131072 | tf_op jit(solution)/shard_map/all_to_all | solution.py:581
  12.8 7.9 %all-to-all-done.2 = s32[128,1,48]{2,1,0:T(1,128)S(1)} async-done(((s32[128,1,48]{2,1,0:T(1,128)}), s32[128,1,48]{2,1,0:T(1,128)S(1)}, u32[]{:S(2)}, u32[]{:S(2)}) %all-to-all-start.2) | async-done | bytes 24608 | tf_op jit(solution)/shard_map/all_to_all | solution.py:581
  20.7 0.1 copy.33
  20.8 5.4 %plan.1 = s32[248,128]{1,0:T(8,128)} custom-call(s32[48,128]{1,0:T(8,128)S(1)} %bitcast.73), custom_call_target="tpu_custom_call" | custom-call | tf_op jit(solution)/shard_map/plan/pallas_call | solution.py:143
  26.2 0.0 collective-permute-done.refs_4_
  26.2 0.0 copy-start.3
  26.2 0.0 collective-permute-done.1.refs_5_
  26.2 1.3 copy-done.3
  27.5 9.7 %pack.1 = bf16[32,2,69,16,128]{4,3,2,1,0:T(8,128)(2,1)} custom-call(s32[248,128]{1,0:T(8,128)} %plan.1, s32[1]{0:T(128)} %bitcast.12.me_ref, bf16[32,16,2048]{2,1,0:T(8,128)(2,1)} %bitcast.64, bf16[32,16,2048]{2,1,0:T(8,128)(2,1)} %bitcast.65, bf16[32,16,2048]{2,1,0:T(8,128)(2,1)} %bitcast.66, bf16[32,16,2048]{2,1,0:T(8,128)(2,1)} %bitcast.16.other_values), custom_call_target="tpu_custom_call" | custom-call | tf_op jit(solution)/shard_map/pack/pallas_call | solution.py:215
  37.2 205.7 %all_to_all.28.refs_6_ = bf16[64,1104,128]{2,1,0:T(8,128)(2,1)} all-to-all(bf16[64,1104,128]{2,1,0:T(8,128)(2,1)} %bitcast.63), channel_id=1, replica_groups={{0,2,4,6,8,10,12,14,16,18,20,22,24,26,28,30,32,34,36,38,40,42,44,46,48,..., dimensions={0} | all-to-all | bytes 36175872 | tf_op jit(solution)/shard_map/all_to_all | solution.py:545
  243.0 0.0 copy-start.1
  243.0 11.3 %forward.1 = (bf16[64,5,16,128]{3,2,1,0:T(8,128)(2,1)}, bf16[6,64,16,128]{3,2,1,0:T(8,128)(2,1)}, bf16[1,64,16,128]{3,2,1,0:T(8,128)(2,1)}, bf16[1,64,16,128]{3,...) custom-call(s32[248,128]{1,0:T(8,128)} %plan.1, ...), custom_call_target="tpu_custom_call" | custom-call | tf_op jit(solution)/shard_map/forward/pallas_call | solution.py:281
  254.3 1.8 collective-permute-start.2
  256.1 1.8 collective-permute-start.10
  257.9 0.7 collective-permute-start.11
  258.6 1.0 collective-permute-start.12
  259.6 1.1 collective-permute-start.13
  260.7 17.2 %all-to-all-start.4 = ((bf16[64,5,16,128]{3,2,1,0:T(8,128)(2,1)}), bf16[64,5,16,128]{3,2,1,0:T(8,128)(2,1)S(1)}, u32[]{:S(2)}, u32[]{:S(2)}) async-start(bf16[64,5,16,128]{3,2,1,0:T(8,128)(2,1)} %get-tuple-element.194), calls=%async_computation.4 | async-start | bytes 2621440 | tf_op jit(solution)/shard_map/all_to_all | solution.py:545
  277.9 0.0 copy-done.1
  277.9 14.4 %attend.3 = (bf16[512,2048]{1,0:T(8,128)(2,1)}, f32[16,512,384]{2,1,0:T(8,128)}) custom-call(s32[64]{0:T(128)} %get-tuple-element.183.refs_0_, bf16[512,2048]{1,0:T(8,128)(2,1)S(1)} %copy-done.1, bf16[512,2048]{1,0:T(8,128)(2,1)} %refs_2_.2, bf16[512,2048]{1,0:T(8,128)(2,1)} %refs_3_.2, bf16[512,2048]{1,0:T(8,128)(2,1)} %copy-done.3, ...), custom_call_target="tpu_custom_call" | custom-call | flops 12884901888 | bytes 18874368 | tf_op jit(solution)/shard_map/attend/pallas_call | solution.py:409
  292.4 0.0 collective-permute-done.10.rest_8_
  292.4 2.3 collective-permute-start.14
  294.7 0.0 collective-permute-done.11.rest_9_
  294.7 2.7 collective-permute-start.3
  297.4 0.0 collective-permute-done.12.rest_10_
  297.4 0.0 collective-permute-start.4
  297.4 0.0 collective-permute-done.13.rest_11_
  297.4 0.9 collective-permute-start.5
  298.3 12.5 %attend.4 = (bf16[512,2048]{1,0:T(8,128)(2,1)}, f32[16,512,384]{2,1,0:T(8,128)}) custom-call(s32[64]{0:T(128)} %get-tuple-element.183.refs_0_, bf16[512,2048]{1,0:T(8,128)(2,1)S(1)} %copy-done.1, bf16[512,2048]{1,0:T(8,128)(2,1)} %refs_2_.2, bf16[512,2048]{1,0:T(8,128)(2,1)} %refs_3_.2, ...), custom_call_target="tpu_custom_call", output_to_operand_aliasing={{0}: (7, {}), {1}: (8, {})} | custom-call | flops 10737418240 | bytes 15728640 | tf_op jit(solution)/shard_map/attend/pallas_call | solution.py:409
  310.9 0.0 collective-permute-done.14.rest_12_
  310.9 0.0 copy-start.5
  310.9 0.9 collective-permute-start.6
  311.8 0.0 collective-permute-done.3.rest_1_
  311.8 0.0 copy-start.6
  311.8 0.6 collective-permute-start.7
  312.4 0.0 collective-permute-done.4.rest_2_
  312.4 0.9 collective-permute-start.8
  313.3 0.0 collective-permute-done.5.rest_3_
  313.3 2.4 collective-permute-start.9
  315.7 12.5 %attend.5 = (bf16[512,2048]{1,0:T(8,128)(2,1)}, f32[16,512,384]{2,1,0:T(8,128)}) custom-call(s32[64]{0:T(128)} %get-tuple-element.183.refs_0_, bf16[512,2048]{1,0:T(8,128)(2,1)S(1)} %copy-done.1, bf16[512,2048]{1,0:T(8,128)(2,1)} %refs_2_.2, bf16[512,2048]{1,0:T(8,128)(2,1)} %refs_3_.2, ...), custom_call_target="tpu_custom_call", output_to_operand_aliasing={{0}: (7, {}), {1}: (8, {})} | custom-call | flops 10737418240 | bytes 15728640 | tf_op jit(solution)/shard_map/attend/pallas_call | solution.py:409
  328.2 0.0 copy-done.5
  328.2 0.0 copy-done.6
  328.2 1.2 slice.3
  330.1 0.0 collective-permute-done.6.rest_4_
  330.1 0.0 collective-permute-done.7.rest_5_
  330.1 0.0 collective-permute-done.8.rest_6_
  330.1 0.0 collective-permute-done.9.rest_7_
  330.1 0.0 all-to-all-done.4
  330.1 0.0 copy-start.4
  330.1 0.0 collective-permute-done.2.rest_0_
  330.1 1.1 copy-done.4
  331.2 17.2 %merge.1 = bf16[512,2048]{1,0:T(8,128)(2,1)} custom-call(s32[248,128]{1,0:T(8,128)} %plan.1, s32[1]{0:T(128)} %bitcast.12.me_ref, bf16[512,2048]{1,0:T(8,128)(2,1)S(1)} %copy-done.1, f32[16,512,384]{2,1,0:T(8,128)} %get-tuple-element.192.state, bf16[512,2048]{1,0:T(8,128)(2,1)} %get-tuple-element.193.out_before, ...), custom_call_target="tpu_custom_call", output_to_operand_aliasing={{}: (4, {})} | custom-call | tf_op jit(solution)/shard_map/merge/pallas_call | solution.py:520
  (1 shorter events, 0.0 us)
Async XLA Ops:
  0.0 26.2 %collective-permute-start = (bf16[512,2048]{1,0:T(8,128)(2,1)}, bf16[512,2048]{1,0:T(8,128)(2,1)S(1)}, u32[]{:S(2)}, u32[]{:S(2)}) collective-permute-start(bf16[512,2048]{1,0:T(8,128)(2,1)} %refs_2_.2), channel_id=1, source_target_pairs={{0,1},{1,0},{2,3},{3,2},{4,5},{5,4},{6,7},{7,6},{8,9},{9,8},{10,11... | collective-permute-start | bytes 6291464 | tf_op jit(solution)/shard_map/ppermute | solution.py:578
  0.7 25.5 %collective-permute-start.1 = (bf16[512,2048]{1,0:T(8,128)(2,1)}, bf16[512,2048]{1,0:T(8,128)(2,1)}, u32[]{:S(2)}, u32[]{:S(2)}) collective-permute-start(bf16[512,2048]{1,0:T(8,128)(2,1)} %refs_3_.2), channel_id=1, source_target_pairs={{0,1},{1,0},{2,3},{3,2},{4,5},{5,4},{6,7},{7,6},{8,9},{9,8},{10,11... | collective-permute-start | bytes 6291464 | tf_op jit(solution)/shard_map/ppermute | solution.py:579
  2.2 18.5 %all-to-all-start.2 = ((s32[128,1,48]{2,1,0:T(1,128)}), s32[128,1,48]{2,1,0:T(1,128)S(1)}, u32[]{:S(2)}, u32[]{:S(2)}) async-start(s32[128,1,48]{2,1,0:T(1,128)} %broadcast_in_dim.56), calls=%async_computation.2 | async-start | bytes 131072 | tf_op jit(solution)/shard_map/all_to_all | solution.py:581
  26.2 1.3 copy-start.3
  243.0 34.9 %copy-start.1 = (bf16[512,2048]{1,0:T(8,128)(2,1)S(1)}, bf16[512,2048]{1,0:T(8,128)(2,1)}, u32[]{:S(2)}) copy-start(bf16[512,2048]{1,0:T(8,128)(2,1)} %query) | copy-start | bytes 6291460
  254.3 75.9 %collective-permute-start.2 = (bf16[6,64,16,128]{3,2,1,0:T(8,128)(2,1)}, bf16[6,64,16,128]{3,2,1,0:T(8,128)(2,1)}, u32[]{:S(2)}, u32[]{:S(2)}) collective-permute-start(bf16[6,64,16,128]{3,2,1,0:T(8,128)(2,1)} %get-tuple-element.195), channel_id=1, source_target_pairs={{1,0},{0,1},{3,2},{2,3},{5,4},{4,5},{7,6},{6,7},{9,8},{8,9},{11,10... | collective-permute-start | bytes 4718600 | tf_op jit(solution)/shard_map/ppermute | solution.py:591
  256.1 36.3 %collective-permute-start.10 = (bf16[1,64,16,128]{3,2,1,0:T(8,128)(2,1)}, bf16[1,64,16,128]{3,2,1,0:T(8,128)(2,1)}, u32[]{:S(2)}, u32[]{:S(2)}) collective-permute-start(bf16[1,64,16,128]{3,2,1,0:T(8,128)(2,1)} %get-tuple-element.203), channel_id=1, source_target_pairs={{25,0},{24,1},{27,2},{26,3},{29,4},{28,5},{31,6},{30,7},{1,8},{0,9... | collective-permute-start | bytes 786440 | tf_op jit(solution)/shard_map/ppermute | solution.py:591
  257.9 36.9 %collective-permute-start.11 = (bf16[1,64,16,128]{3,2,1,0:T(8,128)(2,1)}, bf16[1,64,16,128]{3,2,1,0:T(8,128)(2,1)}, u32[]{:S(2)}, u32[]{:S(2)}) collective-permute-start(bf16[1,64,16,128]{3,2,1,0:T(8,128)(2,1)} %get-tuple-element.204), channel_id=1, source_target_pairs={{2,0},{3,1},{4,2},{5,3},{6,4},{7,5},{0,6},{1,7},{10,8},{11,9},{12,... | collective-permute-start | bytes 786440 | tf_op jit(solution)/shard_map/ppermute | solution.py:591
  258.6 38.8 %collective-permute-start.12 = (bf16[1,64,16,128]{3,2,1,0:T(8,128)(2,1)}, bf16[1,64,16,128]{3,2,1,0:T(8,128)(2,1)}, u32[]{:S(2)}, u32[]{:S(2)}) collective-permute-start(bf16[1,64,16,128]{3,2,1,0:T(8,128)(2,1)} %get-tuple-element.205), channel_id=1, source_target_pairs={{3,0},{2,1},{5,2},{4,3},{7,4},{6,5},{1,6},{0,7},{11,8},{10,9},{13,... | collective-permute-start | bytes 786440 | tf_op jit(solution)/shard_map/ppermute | solution.py:591
  259.6 37.8 %collective-permute-start.13 = (bf16[1,64,16,128]{3,2,1,0:T(8,128)(2,1)}, bf16[1,64,16,128]{3,2,1,0:T(8,128)(2,1)}, u32[]{:S(2)}, u32[]{:S(2)}) collective-permute-start(bf16[1,64,16,128]{3,2,1,0:T(8,128)(2,1)} %get-tuple-element.206), channel_id=1, source_target_pairs={{6,0},{7,1},{0,2},{1,3},{2,4},{3,5},{4,6},{5,7},{14,8},{15,9},{8,1... | collective-permute-start | bytes 786440 | tf_op jit(solution)/shard_map/ppermute | solution.py:591
  260.7 69.5 %all-to-all-start.4 = ((bf16[64,5,16,128]{3,2,1,0:T(8,128)(2,1)}), bf16[64,5,16,128]{3,2,1,0:T(8,128)(2,1)S(1)}, u32[]{:S(2)}, u32[]{:S(2)}) async-start(bf16[64,5,16,128]{3,2,1,0:T(8,128)(2,1)} %get-tuple-element.194), calls=%async_computation.4 | async-start | bytes 2621440 | tf_op jit(solution)/shard_map/all_to_all | solution.py:545
  292.4 18.5 %collective-permute-start.14 = (bf16[1,64,16,128]{3,2,1,0:T(8,128)(2,1)}, bf16[1,64,16,128]{3,2,1,0:T(8,128)(2,1)S(1)}, u32[]{:S(2)}, u32[]{:S(2)}) collective-permute-start(bf16[1,64,16,128]{3,2,1,0:T(8,128)(2,1)} %get-tuple-element.207), channel_id=1, source_target_pairs={{7,0},{6,1},{1,2},{0,3},{3,4},{2,5},{5,6},{4,7},{15,8},{14,9},{9,1... | collective-permute-start | bytes 786440 | tf_op jit(solution)/shard_map/ppermute | solution.py:591
  294.7 17.1 %collective-permute-start.3 = (bf16[1,64,16,128]{3,2,1,0:T(8,128)(2,1)}, bf16[1,64,16,128]{3,2,1,0:T(8,128)(2,1)S(1)}, u32[]{:S(2)}, u32[]{:S(2)}) collective-permute-start(bf16[1,64,16,128]{3,2,1,0:T(8,128)(2,1)} %get-tuple-element.196), channel_id=1, source_target_pairs={{32,0},{33,1},{34,2},{35,3},{36,4},{37,5},{38,6},{39,7},{40,8},{41... | collective-permute-start | bytes 786440 | tf_op jit(solution)/shard_map/ppermute | solution.py:591
  297.4 15.0 %collective-permute-start.4 = (bf16[1,64,16,128]{3,2,1,0:T(8,128)(2,1)}, bf16[1,64,16,128]{3,2,1,0:T(8,128)(2,1)}, u32[]{:S(2)}, u32[]{:S(2)}) collective-permute-start(bf16[1,64,16,128]{3,2,1,0:T(8,128)(2,1)} %get-tuple-element.197), channel_id=1, source_target_pairs={{33,0},{32,1},{35,2},{34,3},{37,4},{36,5},{39,6},{38,7},{41,8},{40... | collective-permute-start | bytes 786440 | tf_op jit(solution)/shard_map/ppermute | solution.py:591
  297.4 15.9 %collective-permute-start.5 = (bf16[1,64,16,128]{3,2,1,0:T(8,128)(2,1)}, bf16[1,64,16,128]{3,2,1,0:T(8,128)(2,1)}, u32[]{:S(2)}, u32[]{:S(2)}) collective-permute-start(bf16[1,64,16,128]{3,2,1,0:T(8,128)(2,1)} %get-tuple-element.198), channel_id=1, source_target_pairs={{96,0},{97,1},{98,2},{99,3},{100,4},{101,5},{102,6},{103,7},{104,8... | collective-permute-start | bytes 786440 | tf_op jit(solution)/shard_map/ppermute | solution.py:591
  310.9 17.3 %copy-start.5 = (bf16[1,64,16,128]{3,2,1,0:T(8,128)(2,1)}, bf16[1,64,16,128]{3,2,1,0:T(8,128)(2,1)S(1)}, u32[]{:S(2)}) copy-start(bf16[1,64,16,128]{3,2,1,0:T(8,128)(2,1)S(1)} %collective-permute-done.14.rest_12_) | copy-start | bytes 786436
  310.9 19.2 %collective-permute-start.6 = (bf16[1,64,16,128]{3,2,1,0:T(8,128)(2,1)}, bf16[1,64,16,128]{3,2,1,0:T(8,128)(2,1)}, u32[]{:S(2)}, u32[]{:S(2)}) collective-permute-start(bf16[1,64,16,128]{3,2,1,0:T(8,128)(2,1)} %get-tuple-element.199), channel_id=1, source_target_pairs={{97,0},{96,1},{99,2},{98,3},{101,4},{100,5},{103,6},{102,7},{105,8... | collective-permute-start | bytes 786440 | tf_op jit(solution)/shard_map/ppermute | solution.py:591
  311.8 16.4 %copy-start.6 = (bf16[1,64,16,128]{3,2,1,0:T(8,128)(2,1)}, bf16[1,64,16,128]{3,2,1,0:T(8,128)(2,1)S(1)}, u32[]{:S(2)}) copy-start(bf16[1,64,16,128]{3,2,1,0:T(8,128)(2,1)S(1)} %collective-permute-done.3.rest_1_) | copy-start | bytes 786436
  311.8 18.3 %collective-permute-start.7 = (bf16[1,64,16,128]{3,2,1,0:T(8,128)(2,1)}, bf16[1,64,16,128]{3,2,1,0:T(8,128)(2,1)}, u32[]{:S(2)}, u32[]{:S(2)}) collective-permute-start(bf16[1,64,16,128]{3,2,1,0:T(8,128)(2,1)} %get-tuple-element.200), channel_id=1, source_target_pairs={{8,0},{9,1},{10,2},{11,3},{12,4},{13,5},{14,6},{15,7},{16,8},{17,9... | collective-permute-start | bytes 786440 | tf_op jit(solution)/shard_map/ppermute | solution.py:591
  312.4 17.7 %collective-permute-start.8 = (bf16[1,64,16,128]{3,2,1,0:T(8,128)(2,1)}, bf16[1,64,16,128]{3,2,1,0:T(8,128)(2,1)}, u32[]{:S(2)}, u32[]{:S(2)}) collective-permute-start(bf16[1,64,16,128]{3,2,1,0:T(8,128)(2,1)} %get-tuple-element.201), channel_id=1, source_target_pairs={{9,0},{8,1},{11,2},{10,3},{13,4},{12,5},{15,6},{14,7},{17,8},{16,9... | collective-permute-start | bytes 786440 | tf_op jit(solution)/shard_map/ppermute | solution.py:591
  313.3 16.8 %collective-permute-start.9 = (bf16[1,64,16,128]{3,2,1,0:T(8,128)(2,1)}, bf16[1,64,16,128]{3,2,1,0:T(8,128)(2,1)}, u32[]{:S(2)}, u32[]{:S(2)}) collective-permute-start(bf16[1,64,16,128]{3,2,1,0:T(8,128)(2,1)} %get-tuple-element.202), channel_id=1, source_target_pairs={{24,0},{25,1},{26,2},{27,3},{28,4},{29,5},{30,6},{31,7},{0,8},{1,9... | collective-permute-start | bytes 786440 | tf_op jit(solution)/shard_map/ppermute | solution.py:591
  330.1 1.1 copy-start.4

commit v6 on v5

v6 whole, which is shorter than its diff:
```python
import math

import jax
import jax.numpy as jnp
from jax import lax
from jax.experimental import pallas as pl
from jax.experimental.pallas import tpu as pltpu
from jax.sharding import PartitionSpec as P

HEAD = 128
HEADS = 16
BLOCK = 512
DEVICES = 128
CHIPS = 64
SCALE = math.log2(math.e) / math.sqrt(HEAD)

ONE = [(1, 0, 0), (3, 0, 0), (0, 1, 0), (0, 3, 0), (0, 0, 1), (0, 0, 3)]
PARTNER = 6
SHIFTS = [(0, 0, 0, 1)] * PARTNER
SHIFTS += [(*s, c) for s in ONE for c in (0, 1)]
KINDS = len(SHIFTS)
SPARE = 5
PIECE = 16
WAVES = 4
WAVE_OF = [1] * (PARTNER + 4) + [2] * 4 + [3] * 4
CODE_PARTNER = CHIPS
CODE_FORWARD = CODE_PARTNER + 1
CODE_SPARE = CODE_FORWARD + KINDS
LIST = 3 * HEADS
COUNT = LIST + WAVES * HEADS
NEED = COUNT + WAVES
TABLE = NEED + 2 * HEADS
HALF = BLOCK // PIECE
SLOT_PIECES = 2 * HALF + SPARE
SLOT_ROWS = SLOT_PIECES * PIECE

ROW_DIRECT = CHIPS
ROW_SPARE = ROW_DIRECT + CHIPS
ROW_FORWARD = ROW_SPARE + CHIPS
ROW_FORWARD_HEAD = ROW_FORWARD + KINDS
ROW_FROM_HEAD = ROW_FORWARD_HEAD + KINDS
ROW_FROM = ROW_FROM_HEAD + SPARE
ROW_FROM_RANK = ROW_FROM + SPARE
ROW_PARTNER = ROW_FROM_RANK + SPARE
ROW_LEFT = ROW_PARTNER + 1
ROWS = -(-(ROW_LEFT + 1) // 8) * 8


def through(device, shift):
    z, x, y, c = device // 32, device // 8 % 4, device // 2 % 4, device % 2
    dz, dx, dy, dc = shift
    return (((z + dz) % 4 * 4 + (x + dx) % 4) * 4 + (y + dy) % 4) * 2 + (c ^ dc)


def shift_pairs(shift):
    return [(through(b, shift), b) for b in range(DEVICES)]


def roll_lanes(array, amount):
    amount = amount % DEVICES
    return pltpu.roll(array, amount, 1) if amount else array


def permuted(array, shift, lane, inverse=False):
    dz, dx, dy, dc = shift
    if inverse:
        dz, dx, dy = -dz % 4, -dx % 4, -dy % 4
    if dz:
        array = roll_lanes(array, -32 * dz)
    if dx:
        inside = (lane // 8) % 4 + dx < 4
        array = jnp.where(inside, roll_lanes(array, -8 * dx), roll_lanes(array, 32 - 8 * dx))
    if dy:
        inside = (lane // 2) % 4 + dy < 4
        array = jnp.where(inside, roll_lanes(array, -2 * dy), roll_lanes(array, 8 - 2 * dy))
    if dc:
        array = jnp.where(lane % 2 == 0, roll_lanes(array, -1), roll_lanes(array, 1))
    return array


def plan_kernel(chosen_ref, out_ref):
    chip = lax.broadcasted_iota(jnp.int32, (CHIPS, DEVICES), 0)
    lane = lax.broadcasted_iota(jnp.int32, (CHIPS, DEVICES), 1)
    even = jnp.zeros((CHIPS, DEVICES), jnp.int32)
    odd = jnp.zeros((CHIPS, DEVICES), jnp.int32)
    for entry in range(3 * HEADS):
        owner = chosen_ref[entry : entry + 1, :]
        even = even + jnp.where(owner == 2 * chip, entry // 3 + 1, 0)
        odd = odd + jnp.where(owner == 2 * chip + 1, entry // 3 + 1, 0)
    home = lane // 2 == chip
    partner = jnp.sum(jnp.where(home, even + odd, 0), axis=0, keepdims=True)
    even = jnp.where(home, 0, even)
    odd = jnp.where(home, 0, odd)
    waiting = jnp.where(even > 0, odd, 0)
    slot = jnp.where(even > 0, even - 1, jnp.where(odd > 0, odd + 15, 0))
    direct = jnp.where(even > 0, even, odd)
    free = jnp.where(home, 0, jnp.where(direct > 0, 0, 1))
    options = jnp.zeros((CHIPS, DEVICES), jnp.int32)
    for shift in sorted(set(SHIFTS)):
        options = options + permuted(free, shift, lane)
    score = options * 64 + (chip + 17 * lane) % 64
    big = 1 << 20
    out_ref[...] = jnp.zeros((ROWS, DEVICES), jnp.int32)
    for kind, shift in enumerate(SHIFTS):
        able = (waiting > 0) & (permuted(free, shift, lane) > 0)
        rated = jnp.where(able, score, big)
        best = jnp.min(rated, axis=0, keepdims=True)
        picked = able & (rated == best)
        head = jnp.sum(jnp.where(picked, waiting, 0), axis=0, keepdims=True)
        back = permuted(jnp.where(picked, waiting + 16, 0), shift, lane, inverse=True)
        waiting = jnp.where(picked, 0, waiting)
        slot = jnp.where(back > 0, back - 1, slot)
        free = jnp.where(back > 0, 0, free)
        forward = jnp.sum(jnp.where(back > 0, chip, 0), axis=0, keepdims=True)
        out_ref[ROW_FORWARD + kind : ROW_FORWARD + kind + 1, :] = forward
        out_ref[ROW_FORWARD_HEAD + kind : ROW_FORWARD_HEAD + kind + 1, :] = head
    before = lax.broadcasted_iota(jnp.int32, (DEVICES, DEVICES), 0)
    after = lax.broadcasted_iota(jnp.int32, (DEVICES, DEVICES), 1)
    earlier = jnp.where((before < after) & (before % 2 == after % 2), 1.0, 0.0)
    rank = jnp.dot(
        jnp.where(waiting > 0, 1.0, 0.0), earlier, preferred_element_type=jnp.float32
    ).astype(jnp.int32)
    spare = jnp.zeros((CHIPS, DEVICES), jnp.int32)
    for index in range(SPARE):
        for core in range(2):
            chosen = (rank == index) & (lane % 2 == core)
            head = jnp.sum(jnp.where(chosen, waiting, 0), axis=1, keepdims=True)
            spare = jnp.where(lane == 2 * index + core, head, spare)
    out_ref[ROW_SPARE : ROW_SPARE + CHIPS, :] = spare
    excess = jnp.where((waiting > 0) & (rank >= SPARE), 1, 0)
    for index in range(SPARE):
        best = jnp.min(jnp.where(waiting > 0, chip, big), axis=0, keepdims=True)
        picked = (waiting > 0) & (chip == best)
        out_ref[ROW_FROM + index : ROW_FROM + index + 1, :] = jnp.where(best < big, best, 0)
        out_ref[ROW_FROM_RANK + index : ROW_FROM_RANK + index + 1, :] = jnp.minimum(
            jnp.sum(jnp.where(picked, rank, 0), axis=0, keepdims=True), SPARE - 1
        )
        out_ref[ROW_FROM_HEAD + index : ROW_FROM_HEAD + index + 1, :] = jnp.sum(
            jnp.where(picked, waiting, 0), axis=0, keepdims=True
        )
        waiting = jnp.where(picked, 0, waiting)
    excess = excess + waiting
    out_ref[ROW_PARTNER : ROW_PARTNER + 1, :] = partner
    left = jnp.max(jnp.max(excess, axis=0, keepdims=True), axis=1, keepdims=True)
    out_ref[ROW_LEFT : ROW_LEFT + 1, :] = jnp.broadcast_to(left, (1, DEVICES))
    out_ref[0:CHIPS, :] = slot
    out_ref[ROW_DIRECT : ROW_DIRECT + CHIPS, :] = direct


def make_plan(chosen_all):
    return pl.pallas_call(
        plan_kernel,
        out_shape=jax.ShapeDtypeStruct((ROWS, DEVICES), jnp.int32),
        name="plan",
    )(chosen_all)


def columns(head):
    return pl.ds(pl.multiple_of(head * HEAD, HEAD), HEAD)


def make_table(plan, me, table):
    for entry in range(TABLE):
        table[entry] = 0

    def note(head_plus, code, wave):
        @pl.when(head_plus > 0)
        def _():
            head = head_plus - 1
            at = table[NEED + HEADS + head]
            table[head * 3 + jnp.minimum(at, 2)] = code
            table[NEED + HEADS + head] = at + 1
            table[NEED + head] = jnp.maximum(table[NEED + head], wave)

    def direct(chip, carry):
        note(plan[ROW_DIRECT + chip, me], chip, 0)
        return carry

    lax.fori_loop(0, CHIPS, direct, 0)
    note(plan[ROW_PARTNER, me], CODE_PARTNER, 0)
    for kind in range(KINDS):
        note(plan[ROW_FORWARD_HEAD + kind, me], CODE_FORWARD + kind, WAVE_OF[kind])
    for index in range(SPARE):
        note(plan[ROW_FROM_HEAD + index, me], CODE_SPARE + index, WAVES - 1)
    for head in range(HEADS):
        wave = table[NEED + head]
        at = table[COUNT + wave]
        table[LIST + wave * HEADS + at] = head
        table[COUNT + wave] = at + 1


def pack_kernel(plan, me_ref, keys, values, other_keys, other_values, send, table, sem):
    me = me_ref[0]
    chip, core = me // 2, me % 2

    def one_slot(dest, carry):
        code = plan[chip, 2 * dest + core]

        def copy(*sources):
            for half, source in enumerate(sources):
                pltpu.make_async_copy(
                    source.at[:, :, columns(code % 16)],
                    send.at[dest // 2, dest % 2, pl.ds(half * HALF, HALF)],
                    sem,
                ).start()

        @pl.when(code // 16 == core)
        def _():
            copy(keys, values)

        @pl.when(code // 16 != core)
        def _():
            copy(other_keys, other_values)

        return carry

    lax.fori_loop(0, CHIPS, one_slot, 0)

    def one_spare(index, carry):
        head = jnp.maximum(plan[ROW_SPARE + chip, 2 * index + core] - 1, 0)

        def copy(*sources):
            for half, source in enumerate(sources):
                pltpu.make_async_copy(
                    source.at[:, :, columns(head)], send.at[:, half, 2 * HALF + index], sem
                ).start()

        @pl.when(core == 1)
        def _():
            copy(keys, values)

        @pl.when(core == 0)
        def _():
            copy(other_keys, other_values)

        return carry

    lax.fori_loop(0, SPARE, one_spare, 0)
    make_table(plan, me, table)
    pltpu.make_async_copy(send, send, sem).wait()


ANY = pl.BlockSpec(memory_space=pl.ANY)
SMEM = pl.BlockSpec(memory_space=pltpu.SMEM)
VMEM = pl.BlockSpec(memory_space=pltpu.VMEM)
BIG = pltpu.CompilerParams(vmem_limit_bytes=60 * 1024 * 1024)


def tiles(count):
    return jax.ShapeDtypeStruct((count, 2 * HALF, PIECE, HEAD), jnp.bfloat16)


def in_pieces(array):
    return array.reshape(HALF, PIECE, -1)


def pack(plan, me, keys, values, other_keys, other_values):
    return pl.pallas_call(
        pack_kernel,
        in_specs=[SMEM, SMEM, VMEM, VMEM, VMEM, VMEM],
        out_specs=[ANY, SMEM],
        out_shape=[
            jax.ShapeDtypeStruct((HALF, 2, SLOT_PIECES, PIECE, HEAD), jnp.bfloat16),
            jax.ShapeDtypeStruct((TABLE,), jnp.int32),
        ],
        scratch_shapes=[pltpu.SemaphoreType.DMA],
        compiler_params=BIG,
        name="pack",
    )(plan, me, *map(in_pieces, (keys, values, other_keys, other_values)))


def forward_kernel(plan, me_ref, arrived, *rest):
    outs, (moving, spare, gathered, sems, out_sems) = rest[:-5], rest[-5:]
    me = me_ref[0]
    core = me % 2
    loads, stores = [], []
    for kind in range(KINDS):
        out = outs[1].at[kind] if kind < PARTNER else outs[kind - PARTNER + 2].at[0]
        source = arrived.at[plan[ROW_FORWARD + kind, me], pl.ds(0, 2 * HALF)]
        loads.append(pltpu.make_async_copy(source, moving.at[kind], sems.at[kind]))
        stores.append(pltpu.make_async_copy(moving.at[kind], out, out_sems.at[kind]))
    for load in loads:
        load.start()

    load_spare = pltpu.make_async_copy(
        arrived.at[:, pl.ds(2 * HALF, SPARE)], spare, sems.at[KINDS]
    )
    load_spare.start()

    for load, store in zip(loads, stores):
        load.wait()
        store.start()
    load_spare.wait()

    def one_dest(dest, carry):
        for index in range(SPARE):
            chip = plan[ROW_FROM + index, 2 * dest + core]
            rank = plan[ROW_FROM_RANK + index, 2 * dest + core]
            gathered[dest, index] = spare[chip, rank]
        return carry

    lax.fori_loop(0, CHIPS, one_dest, 0)
    last = pltpu.make_async_copy(gathered, outs[0], out_sems.at[KINDS])
    last.start()
    for store in stores:
        store.wait()
    last.wait()


def forward(plan, me, arrived):
    return pl.pallas_call(
        forward_kernel,
        in_specs=[SMEM, SMEM, ANY],
        out_specs=[ANY] * (KINDS - PARTNER + 2),
        out_shape=[jax.ShapeDtypeStruct((CHIPS, SPARE, PIECE, HEAD), jnp.bfloat16)]
        + [tiles(PARTNER)]
        + [tiles(1)] * (KINDS - PARTNER),
        scratch_shapes=[
            pltpu.VMEM((KINDS, 2 * HALF, PIECE, HEAD), jnp.bfloat16),
            pltpu.VMEM((CHIPS, SPARE, PIECE, HEAD), jnp.bfloat16),
            pltpu.VMEM((CHIPS, SPARE, PIECE, HEAD), jnp.bfloat16),
            pltpu.SemaphoreType.DMA((KINDS + 1,)),
            pltpu.SemaphoreType.DMA((KINDS + 1,)),
        ],
        compiler_params=BIG,
        name="forward",
    )(plan, me, arrived)


ROWS_AT_ONCE = 256


def scores_of(query, key):
    return lax.dot_general(
        query, key, (((1,), (1,)), ((), ())), preferred_element_type=jnp.float32
    )


ROWS_AT_ONCE = 256


def attend_kernel(wave, kinds, table, queries, keys, values, *rest):
    other_keys, other_values, arrived = rest[:3]
    forwarded = dict(zip(kinds, rest[3 : 3 + len(kinds)]))
    pieces = rest[3 + len(kinds)] if wave == WAVES - 1 else None
    out, query_buf, key_buf, value_buf, out_buf, sems, out_sems = rest[-7:]
    count = table[COUNT + wave]

    def head_at(index):
        return table[LIST + wave * HEADS + index]

    def load(index, slot):
        head = head_at(index)

        def start(j, source_key, source_value):
            into_value = value_buf.at[slot, j, :, :, pl.ds(0, HEAD)]
            pltpu.make_async_copy(source_key, key_buf.at[slot, j], sems.at[slot, 2 * j]).start()
            pltpu.make_async_copy(source_value, into_value, sems.at[slot, 2 * j + 1]).start()

        cut = columns(head)
        pltpu.make_async_copy(queries.at[:, :, cut], query_buf.at[slot], sems.at[slot, 8]).start()
        start(3, keys.at[:, :, cut], values.at[:, :, cut])
        for j in range(3):
            code = table[head * 3 + j]

            @pl.when(code < CHIPS)
            def _():
                start(j, arrived.at[code, pl.ds(0, HALF)], arrived.at[code, pl.ds(HALF, HALF)])

            @pl.when(code >= CHIPS)
            def _():
                @pl.when(code == CODE_PARTNER)
                def _():
                    start(j, other_keys.at[:, :, cut], other_values.at[:, :, cut])

                for kind, ref in forwarded.items():
                    last = kind + (PARTNER if kind == 0 else 1)

                    @pl.when((code >= CODE_FORWARD + kind) & (code < CODE_FORWARD + last))
                    def _():
                        tile = ref.at[code - CODE_FORWARD - kind]
                        start(j, tile.at[pl.ds(0, HALF)], tile.at[pl.ds(HALF, HALF)])

                if pieces is not None:

                    @pl.when(code >= CODE_SPARE)
                    def _():
                        start(j, pieces.at[:, 0, code - CODE_SPARE], pieces.at[:, 1, code - CODE_SPARE])

    def store(index, slot):
        return pltpu.make_async_copy(
            out_buf.at[slot], out.at[:, :, columns(head_at(index))], out_sems.at[slot]
        )

    @pl.when(count > 0)
    def _():
        load(0, 0)
        ones = jnp.ones((HALF, PIECE, HEAD), jnp.bfloat16)
        for slot in range(2):
            for j in range(4):
                value_buf[slot, j, :, :, HEAD:] = ones

    def one_head(index, carry):
        slot = index % 2

        @pl.when(index + 1 < count)
        def _():
            load(index + 1, 1 - slot)

        for j in range(4):
            into_value = value_buf.at[slot, j, :, :, pl.ds(0, HEAD)]
            tile = arrived.at[0, pl.ds(0, HALF)]
            pltpu.make_async_copy(tile, key_buf.at[slot, j], sems.at[slot, 2 * j]).wait()
            pltpu.make_async_copy(tile, into_value, sems.at[slot, 2 * j + 1]).wait()
        pltpu.make_async_copy(tile, query_buf.at[slot], sems.at[slot, 8]).wait()

        @pl.when(index >= 2)
        def _():
            store(index - 2, slot).wait()

        query = query_buf[slot].reshape(BLOCK, HEAD)
        for start in range(0, BLOCK, ROWS_AT_ONCE):
            stop = start + ROWS_AT_ONCE
            q = query[start:stop, :]
            total = highest = None
            for j in (3, 0, 1, 2):
                seen = stop if j == 3 else BLOCK
                scores = scores_of(q, key_buf[slot, j, 0 : seen // PIECE].reshape(seen, HEAD))
                if j == 3:
                    row_iota = lax.broadcasted_iota(jnp.int32, scores.shape, 0) + start
                    col_iota = lax.broadcasted_iota(jnp.int32, scores.shape, 1)
                    scores = jnp.where(col_iota <= row_iota, scores, -jnp.inf)
                top = jnp.max(scores, axis=1, keepdims=True)
                if highest is not None:
                    top = jnp.maximum(highest, top)
                weight = jnp.exp2((scores - top) * SCALE).astype(jnp.bfloat16)
                value = value_buf[slot, j, 0 : seen // PIECE].reshape(seen, 2 * HEAD)
                added = jnp.dot(weight, value, preferred_element_type=jnp.float32)
                if highest is None:
                    total = added
                else:
                    total = total * jnp.exp2((highest - top) * SCALE) + added
                highest = top
            result = (total[:, :HEAD] / total[:, HEAD:]).astype(jnp.bfloat16)
            span = slice(start // PIECE, stop // PIECE)
            out_buf[slot, span] = result.reshape(ROWS_AT_ONCE // PIECE, PIECE, HEAD)
        store(index, slot).start()
        return carry

    lax.fori_loop(0, count, one_head, 0)

    @pl.when(count >= 2)
    def _():
        store(count - 2, count % 2).wait()

    @pl.when(count >= 1)
    def _():
        store(count - 1, (count - 1) % 2).wait()


HEADS_EXPECTED = (9, 4, 2, 2)


def attend(wave, before, table, queries, keys, values, others, arrived, forwarded, pieces):
    kinds = [kind for kind in forwarded if WAVE_OF[kind] <= wave]
    operands = [table, *map(in_pieces, (queries, keys, values, *others)), arrived]
    operands += [forwarded[kind] for kind in kinds]
    if wave == WAVES - 1:
        operands.append(pieces.reshape(HALF, 2, SPARE, PIECE, HEAD))
    if before is not None:
        operands.append(before)
    size = HEADS_EXPECTED[wave] * BLOCK * 4 * BLOCK * HEAD
    return pl.pallas_call(
        lambda *refs: attend_kernel(wave, kinds, *refs),
        in_specs=[SMEM] + [ANY] * (len(operands) - 1),
        out_specs=ANY,
        out_shape=jax.ShapeDtypeStruct((HALF, PIECE, HEADS * HEAD), jnp.bfloat16),
        input_output_aliases={} if before is None else {len(operands) - 1: 0},
        scratch_shapes=[
            pltpu.VMEM((2, HALF, PIECE, HEAD), jnp.bfloat16),
            pltpu.VMEM((2, 4, HALF, PIECE, HEAD), jnp.bfloat16),
            pltpu.VMEM((2, 4, HALF, PIECE, 2 * HEAD), jnp.bfloat16),
            pltpu.VMEM((2, HALF, PIECE, HEAD), jnp.bfloat16),
            pltpu.SemaphoreType.DMA((2, 9)),
            pltpu.SemaphoreType.DMA((2,)),
        ],
        cost_estimate=pl.CostEstimate(
            flops=16 * size, bytes_accessed=3 * 2**20, transcendentals=size // HEAD
        ),
        compiler_params=BIG,
        name="attend",
    )(*operands)


LANES = [[2 * chip + core for chip in range(CHIPS)] for core in range(2)]
SWAP = [(device, device ^ 1) for device in range(DEVICES)]


def exchange(array):
    return lax.all_to_all(array, "ctx", 0, 0, axis_index_groups=LANES, tiled=True)


def full_attention(queries, keys, values, chosen_all, me):
    heads = jnp.arange(3 * HEADS, dtype=jnp.int32) // 3
    mine = lax.dynamic_index_in_dim(chosen_all, me, 0, keepdims=False)
    wants = chosen_all == me
    which = jnp.max(jnp.where(wants, heads[None, :], 0), axis=1)
    key_heads = keys.reshape(BLOCK, HEADS, HEAD).transpose(1, 0, 2)
    value_heads = values.reshape(BLOCK, HEADS, HEAD).transpose(1, 0, 2)
    got_key = lax.all_to_all(jnp.take(key_heads, which, axis=0), "ctx", 0, 0, tiled=True)
    got_value = lax.all_to_all(jnp.take(value_heads, which, axis=0), "ctx", 0, 0, tiled=True)
    q_heads = queries.reshape(BLOCK, HEADS, HEAD).transpose(1, 0, 2)
    allowed = jnp.arange(4 * BLOCK)[None, :] >= BLOCK
    allowed = allowed | (jnp.arange(4 * BLOCK)[None, :] <= jnp.arange(BLOCK)[:, None])

    def one_head(head):
        picks = lax.dynamic_slice(mine, (3 * head,), (3,))
        k = jnp.concatenate([key_heads[head], got_key[picks].reshape(3 * BLOCK, HEAD)], axis=0)
        v = jnp.concatenate([value_heads[head], got_value[picks].reshape(3 * BLOCK, HEAD)], axis=0)
        s = jnp.where(allowed, scores_of(q_heads[head], k), -jnp.inf)
        weight = jnp.exp2((s - jnp.max(s, axis=1, keepdims=True)) * SCALE)
        total = jnp.sum(weight, axis=1, keepdims=True)
        o = jnp.dot(weight.astype(jnp.bfloat16), v, preferred_element_type=jnp.float32)
        return (o / total).astype(jnp.bfloat16)

    out = lax.map(one_head, jnp.arange(HEADS))
    return out.transpose(1, 0, 2).reshape(BLOCK, HEADS * HEAD)


def body(queries, keys, values, chosen):
    me = lax.axis_index("ctx").astype(jnp.int32)
    me_ref = me.reshape(1)
    other_keys = lax.ppermute(keys, "ctx", SWAP)
    other_values = lax.ppermute(values, "ctx", SWAP)
    spread = jnp.broadcast_to(chosen.reshape(1, 3 * HEADS), (DEVICES, 3 * HEADS))
    chosen_all = lax.all_to_all(spread, "ctx", 0, 0, tiled=True)
    plan = make_plan(chosen_all.T)
    send, table = pack(plan, me_ref, keys, values, other_keys, other_values)
    sent = exchange(send.reshape(CHIPS, SLOT_ROWS, HEAD))
    held = (sent, plan, table, queries, keys, values, other_keys, other_values, me_ref)
    held = lax.optimization_barrier(held)
    arrived, plan, table, queries, keys, values, other_keys, other_values, me_ref = held
    arrived = arrived.reshape(CHIPS, SLOT_PIECES, PIECE, HEAD)
    pieces, *outgoing = forward(plan, me_ref, arrived)
    outgoing = dict(zip([0, *range(PARTNER, KINDS)], outgoing))
    forwarded = {}
    out = None
    for wave in range(WAVES):
        if wave:
            for kind in [kind for kind in outgoing if WAVE_OF[kind] == wave]:
                forwarded[kind] = lax.ppermute(outgoing[kind], "ctx", shift_pairs(SHIFTS[kind]))
        if wave == 1:
            pieces, out = lax.optimization_barrier((pieces, out))
            pieces = exchange(pieces)
        out = attend(
            wave,
            out,
            table,
            queries,
            keys,
            values,
            (other_keys, other_values),
            arrived,
            forwarded,
            pieces,
        )
    out = out.reshape(BLOCK, HEADS * HEAD)
    return lax.cond(
        plan[ROW_LEFT, 0] > 0,
        lambda: full_attention(queries, keys, values, chosen_all, me),
        lambda: out,
    )


def solution(mesh):
    placed = (P("ctx", None), P("ctx", None), P("ctx", None), P("ctx", None, None))
    return jax.shard_map(
        body, mesh=mesh, in_specs=placed, out_specs=P("ctx", None), check_vma=False
    )
```

time: 352 us -> 351 us (level)
  Pallas kernels: 83.2 us -> 65.6 us
  waiting for transfers between devices: 7.91 us -> 20.7 us
    pallas_call x4, Pallas kernels: 56.7 us -> 39.6 us  [attend(): pl.pallas_call(lambda *refs: attend_kernel(wave, kinds, *refs), in_specs=...]
    ppermute x13, waiting for transfers between devices: 0.03 us -> 12.9 us  [body(): lax.ppermute(outgoing[kind], 'ctx', shift_pairs(SHIFTS[kind]))]
  transfers between devices with their start and end apart: 17 -> 17, of which waited for: 1 -> 5; matrix products, arithmetic and copies ran while one was open for 1% -> 1% of each run, Pallas kernels for 13% -> 12%
where the time goes in v6:
time: 351 us; the launch traced here: 346 us
  blocking collectives  206 us (59%)
  Pallas kernels  65.6 us (19%)
  starting transfers between devices  47.6 us (14%)
  waiting for transfers between devices  20.7 us (6%)
  local copies, waits for them, and re-layouts  5.16 us (1%)
    all_to_all x1, blocking collectives, exchange(): lax.all_to_all(array, 'ctx', 0, 0, axis_index_groups=LANES, tiled=True)  206 us
    pallas_call x4, Pallas kernels, attend(): pl.pallas_call(lambda *refs: attend_kernel(wave, kinds, *refs), in_specs=...  39.6 us
    all_to_all x1, starting transfers between devices, exchange(): lax.all_to_all(array, 'ctx', 0, 0, axis_index_groups=LANES, tiled=True)  20 us
    ppermute x13, starting transfers between devices, body(): lax.ppermute(outgoing[kind], 'ctx', shift_pairs(SHIFTS[kind]))  16.3 us
    ppermute x13, waiting for transfers between devices, body(): lax.ppermute(outgoing[kind], 'ctx', shift_pairs(SHIFTS[kind]))  12.9 us
    all_to_all x1, starting transfers between devices, body(): chosen_all = lax.all_to_all(spread, 'ctx', 0, 0, tiled=True)  10.6 us
    pallas_call x1, Pallas kernels, forward(): pl.pallas_call(forward_kernel, in_specs=[SMEM, SMEM, ANY], out_specs=[ANY...  10.4 us
    pallas_call x1, Pallas kernels, pack(): pl.pallas_call(pack_kernel, in_specs=[SMEM, SMEM, VMEM, VMEM, VMEM, VMEM]...  10.2 us
  transfers between devices with their start and end apart: 17, of which 5 were waited for; matrix products, arithmetic and copies ran while one was open for 1% of the time, Pallas kernels for 12%

profile of v6, /device:TPU:7, one launch (start us, length us, event | category | flops | bytes accessed | tf_op | source)
XLA Modules:
  0.0 345.8 jit_solution(13205940148426929905)
XLA Ops:
  0.0 0.7 collective-permute-start
  0.7 0.0 collective-permute-start.1
  0.7 0.8 copy.30
  1.4 0.1 broadcast_in_dim.55
  1.5 0.7 broadcast_in_dim.56
  2.2 10.6 %all-to-all-start.2 = ((s32[128,1,48]{2,1,0:T(1,128)}), s32[128,1,48]{2,1,0:T(1,128)S(1)}, u32[]{:S(2)}, u32[]{:S(2)}) async-start(s32[128,1,48]{2,1,0:T(1,128)} %broadcast_in_dim.56), calls=%async_computation.2 | async-start | bytes 131072 | tf_op jit(solution)/shard_map/all_to_all | solution.py:536
  12.8 7.9 %all-to-all-done.2 = s32[128,1,48]{2,1,0:T(1,128)S(1)} async-done(((s32[128,1,48]{2,1,0:T(1,128)}), s32[128,1,48]{2,1,0:T(1,128)S(1)}, u32[]{:S(2)}, u32[]{:S(2)}) %all-to-all-start.2) | async-done | bytes 24608 | tf_op jit(solution)/shard_map/all_to_all | solution.py:536
  20.7 0.1 copy.31
  20.8 5.4 %plan.1 = s32[248,128]{1,0:T(8,128)} custom-call(s32[48,128]{1,0:T(8,128)S(1)} %bitcast.100), custom_call_target="tpu_custom_call" | custom-call | tf_op jit(solution)/shard_map/plan/pallas_call | solution.py:151
  26.2 0.0 collective-permute-done
  26.2 0.0 copy-start.3
  26.2 0.0 collective-permute-done.1
  26.2 1.3 copy-done.3
  27.5 10.2 %pack.1 = (bf16[32,2,69,16,128]{4,3,2,1,0:T(8,128)(2,1)}, s32[148]{0:T(256)}) custom-call(s32[248,128]{1,0:T(8,128)} %plan.1, s32[1]{0:T(128)} %bitcast.13.me_ref, bf16[32,16,2048]{2,1,0:T(8,128)(2,1)} %bitcast.73, bf16[32,16,2048]{2,1,0:T(8,128)(2,1)} %bitcast.78, bf16[32,16,2048]{2,1,0:T(8,128)(2,1)} %bitcast.83, bf16[32,16,2048]{2,1,0:T(8,128)(2,1)} %bitcast.17.other_values), custom_call_target="tpu_custom_call" | custom-call | tf_op jit(solution)/shard_map/pack/pallas_call | solution.py:258
  37.8 205.7 %all_to_all.28 = bf16[64,1104,128]{2,1,0:T(8,128)(2,1)} all-to-all(bf16[64,1104,128]{2,1,0:T(8,128)(2,1)} %bitcast.93), channel_id=1, replica_groups={{0,2,4,6,8,10,12,14,16,18,20,22,24,26,28,30,32,34,36,38,40,42,44,46,48,..., dimensions={0} | all-to-all | bytes 36175872 | tf_op jit(solution)/shard_map/all_to_all | solution.py:500
  243.5 0.0 copy-start.1
  243.5 10.4 %forward.1 = (bf16[64,5,16,128]{3,2,1,0:T(8,128)(2,1)}, bf16[6,64,16,128]{3,2,1,0:T(8,128)(2,1)}, bf16[1,64,16,128]{3,2,1,0:T(8,128)(2,1)}, bf16[1,64,16,128]{3,...) custom-call(s32[248,128]{1,0:T(8,128)} %plan.1, ...), custom_call_target="tpu_custom_call" | custom-call | tf_op jit(solution)/shard_map/forward/pallas_call | solution.py:311
  253.9 1.3 collective-permute-start.2
  255.2 0.8 collective-permute-start.3
  256.0 1.1 collective-permute-start.4
  257.1 0.6 collective-permute-start.5
  257.7 1.0 collective-permute-start.6
  258.8 0.0 copy-done.1
  258.8 20.4 %attend.4.refs_12_ = bf16[32,16,2048]{2,1,0:T(8,128)(2,1)} custom-call(s32[148]{0:T(256)} %get-tuple-element.182.refs_0_, bf16[32,16,2048]{2,1,0:T(8,128)(2,1)} %bitcast.88, bf16[32,16,2048]{2,1,0:T(8,128)(2,1)S(1)} %bitcast.74, bf16[32,16,2048]{2,1,0:T(8,128)(2,1)} %bitcast.79, bf16[32,16,2048]{2,1,0:T(8,128)(2,1)} %bitcast.84, ...), custom_call_target="tpu_custom_call" | custom-call | flops 19327352832 | bytes 3145728 | tf_op jit(solution)/shard_map/attend/pallas_call | solution.py:473
  279.2 20.0 %all-to-all-start.4 = ((bf16[64,5,16,128]{3,2,1,0:T(8,128)(2,1)}), bf16[64,5,16,128]{3,2,1,0:T(8,128)(2,1)S(1)}, u32[]{:S(2)}, u32[]{:S(2)}) async-start(bf16[64,5,16,128]{3,2,1,0:T(8,128)(2,1)} %get-tuple-element.204), calls=%async_computation.4 | async-start | bytes 2621440 | tf_op jit(solution)/shard_map/all_to_all | solution.py:500
  299.2 1.2 slice.3
  301.0 0.0 collective-permute-done.3.refs_8_
  301.0 2.8 collective-permute-start.10
  303.8 0.0 collective-permute-done.4.refs_9_
  303.8 1.3 collective-permute-start.7
  305.1 0.0 collective-permute-done.5.refs_10_
  305.1 0.0 collective-permute-start.8
  305.1 0.0 collective-permute-done.6.refs_11_
  305.1 2.1 collective-permute-start.9
  307.2 0.0 collective-permute-done.2.refs_7_
  307.2 2.4 collective-permute-start.11
  309.6 10.1 %attend.5.refs_16_ = bf16[32,16,2048]{2,1,0:T(8,128)(2,1)} custom-call(s32[148]{0:T(256)} %get-tuple-element.182.refs_0_, bf16[32,16,2048]{2,1,0:T(8,128)(2,1)} %bitcast.89, bf16[32,16,2048]{2,1,0:T(8,128)(2,1)S(1)} %bitcast.75, bf16[32,16,2048]{2,1,0:T(8,128)(2,1)} %bitcast.80, bf16[32,16,2048]{2,1,0:T(8,128)(2,1)} %bitcast.85, ...), custom_call_target="tpu_custom_call", output_to_operand_aliasing={{}: (12, {})} | custom-call | flops 8589934592 | bytes 3145728 | tf_op jit(solution)/shard_map/attend/pallas_call | solution.py:473
  319.7 3.7 %collective-permute-done.10.refs_15_ = bf16[1,64,16,128]{3,2,1,0:T(8,128)(2,1)S(1)} collective-permute-done((bf16[1,64,16,128]{3,2,1,0:T(8,128)(2,1)}, bf16[1,64,16,128]{3,2,1,0:T(8,128)(2,1)S(1)}, u32[]{:S(2)}, u32[]{:S(2)}) %collective-permute-start.10) | collective-permute-done | bytes 262176 | tf_op jit(solution)/shard_map/ppermute | solution.py:551
  323.4 0.0 copy-start.5
  323.4 0.2 collective-permute-start.12
  323.6 0.0 collective-permute-done.7.refs_12_
  323.6 0.0 copy-start.6
  323.6 1.0 collective-permute-start.13
  324.7 1.0 collective-permute-done.8.refs_13_
  325.7 1.6 collective-permute-start.14
  327.3 0.0 collective-permute-done.9.refs_14_
  327.3 0.0 copy-done.5
  327.3 0.0 copy-done.6
  327.3 4.6 %attend.6.refs_21_ = bf16[32,16,2048]{2,1,0:T(8,128)(2,1)} custom-call(s32[148]{0:T(256)} %get-tuple-element.182.refs_0_, bf16[32,16,2048]{2,1,0:T(8,128)(2,1)} %bitcast.90, bf16[32,16,2048]{2,1,0:T(8,128)(2,1)S(1)} %bitcast.76, bf16[32,16,2048]{2,1,0:T(8,128)(2,1)} %bitcast.81, bf16[32,16,2048]{2,1,0:T(8,128)(2,1)} %bitcast.86, ...), custom_call_target="tpu_custom_call", output_to_operand_aliasing={{}: (16, {})} | custom-call | flops 4294967296 | bytes 3145728 | tf_op jit(solution)/shard_map/attend/pallas_call | solution.py:473
  331.9 0.0 collective-permute-done.11.refs_16_
  331.9 0.0 collective-permute-done.12.refs_17_
  331.9 0.9 collective-permute-done.13.refs_18_
  332.8 7.2 %collective-permute-done.14.refs_19_ = bf16[1,64,16,128]{3,2,1,0:T(8,128)(2,1)} collective-permute-done((bf16[1,64,16,128]{3,2,1,0:T(8,128)(2,1)}, bf16[1,64,16,128]{3,2,1,0:T(8,128)(2,1)}, u32[]{:S(2)}, u32[]{:S(2)}) %collective-permute-start.14) | collective-permute-done | bytes 262176 | tf_op jit(solution)/shard_map/ppermute | solution.py:551
  340.0 0.0 all-to-all-done.4
  340.0 0.0 copy-start.4
  340.0 1.1 copy-done.4
  341.1 4.5 %attend.7 = bf16[32,16,2048]{2,1,0:T(8,128)(2,1)} custom-call(s32[148]{0:T(256)} %get-tuple-element.182.refs_0_, bf16[32,16,2048]{2,1,0:T(8,128)(2,1)} %bitcast.91, bf16[32,16,2048]{2,1,0:T(8,128)(2,1)S(1)} %bitcast.77, bf16[32,16,2048]{2,1,0:T(8,128)(2,1)} %bitcast.82, bf16[32,16,2048]{2,1,0:T(8,128)(2,1)} %bitcast.87, ...), custom_call_target="tpu_custom_call", output_to_operand_aliasing={{}: (21, {})} | custom-call | flops 4294967296 | bytes 3145728 | tf_op jit(solution)/shard_map/attend/pallas_call | solution.py:473
  (1 shorter events, 0.0 us)
Async XLA Ops:
  0.0 26.2 %collective-permute-start = (bf16[512,2048]{1,0:T(8,128)(2,1)}, bf16[512,2048]{1,0:T(8,128)(2,1)S(1)}, u32[]{:S(2)}, u32[]{:S(2)}) collective-permute-start(bf16[512,2048]{1,0:T(8,128)(2,1)} %param.11), channel_id=1, source_target_pairs={{0,1},{1,0},{2,3},{3,2},{4,5},{5,4},{6,7},{7,6},{8,9},{9,8},{10,11... | collective-permute-start | bytes 6291464 | tf_op jit(solution)/shard_map/ppermute | solution.py:533
  0.7 25.5 %collective-permute-start.1 = (bf16[512,2048]{1,0:T(8,128)(2,1)}, bf16[512,2048]{1,0:T(8,128)(2,1)}, u32[]{:S(2)}, u32[]{:S(2)}) collective-permute-start(bf16[512,2048]{1,0:T(8,128)(2,1)} %param.12), channel_id=1, source_target_pairs={{0,1},{1,0},{2,3},{3,2},{4,5},{5,4},{6,7},{7,6},{8,9},{9,8},{10,11... | collective-permute-start | bytes 6291464 | tf_op jit(solution)/shard_map/ppermute | solution.py:534
  2.2 18.5 %all-to-all-start.2 = ((s32[128,1,48]{2,1,0:T(1,128)}), s32[128,1,48]{2,1,0:T(1,128)S(1)}, u32[]{:S(2)}, u32[]{:S(2)}) async-start(s32[128,1,48]{2,1,0:T(1,128)} %broadcast_in_dim.56), calls=%async_computation.2 | async-start | bytes 131072 | tf_op jit(solution)/shard_map/all_to_all | solution.py:536
  26.2 1.3 copy-start.3
  243.5 15.3 %copy-start.1 = (bf16[512,2048]{1,0:T(8,128)(2,1)S(1)}, bf16[512,2048]{1,0:T(8,128)(2,1)}, u32[]{:S(2)}) copy-start(bf16[512,2048]{1,0:T(8,128)(2,1)} %param.11) | copy-start | bytes 6291460
  253.9 53.3 %collective-permute-start.2 = (bf16[6,64,16,128]{3,2,1,0:T(8,128)(2,1)}, bf16[6,64,16,128]{3,2,1,0:T(8,128)(2,1)}, u32[]{:S(2)}, u32[]{:S(2)}) collective-permute-start(bf16[6,64,16,128]{3,2,1,0:T(8,128)(2,1)} %get-tuple-element.190), channel_id=1, source_target_pairs={{1,0},{0,1},{3,2},{2,3},{5,4},{4,5},{7,6},{6,7},{9,8},{8,9},{11,10... | collective-permute-start | bytes 4718600 | tf_op jit(solution)/shard_map/ppermute | solution.py:551
  255.2 45.7 %collective-permute-start.3 = (bf16[1,64,16,128]{3,2,1,0:T(8,128)(2,1)}, bf16[1,64,16,128]{3,2,1,0:T(8,128)(2,1)}, u32[]{:S(2)}, u32[]{:S(2)}) collective-permute-start(bf16[1,64,16,128]{3,2,1,0:T(8,128)(2,1)} %get-tuple-element.191), channel_id=1, source_target_pairs={{32,0},{33,1},{34,2},{35,3},{36,4},{37,5},{38,6},{39,7},{40,8},{41... | collective-permute-start | bytes 786440 | tf_op jit(solution)/shard_map/ppermute | solution.py:551
  256.0 47.7 %collective-permute-start.4 = (bf16[1,64,16,128]{3,2,1,0:T(8,128)(2,1)}, bf16[1,64,16,128]{3,2,1,0:T(8,128)(2,1)}, u32[]{:S(2)}, u32[]{:S(2)}) collective-permute-start(bf16[1,64,16,128]{3,2,1,0:T(8,128)(2,1)} %get-tuple-element.192), channel_id=1, source_target_pairs={{33,0},{32,1},{35,2},{34,3},{37,4},{36,5},{39,6},{38,7},{41,8},{40... | collective-permute-start | bytes 786440 | tf_op jit(solution)/shard_map/ppermute | solution.py:551
  257.1 48.0 %collective-permute-start.5 = (bf16[1,64,16,128]{3,2,1,0:T(8,128)(2,1)}, bf16[1,64,16,128]{3,2,1,0:T(8,128)(2,1)}, u32[]{:S(2)}, u32[]{:S(2)}) collective-permute-start(bf16[1,64,16,128]{3,2,1,0:T(8,128)(2,1)} %get-tuple-element.193), channel_id=1, source_target_pairs={{96,0},{97,1},{98,2},{99,3},{100,4},{101,5},{102,6},{103,7},{104,8... | collective-permute-start | bytes 786440 | tf_op jit(solution)/shard_map/ppermute | solution.py:551
  257.7 47.3 %collective-permute-start.6 = (bf16[1,64,16,128]{3,2,1,0:T(8,128)(2,1)}, bf16[1,64,16,128]{3,2,1,0:T(8,128)(2,1)}, u32[]{:S(2)}, u32[]{:S(2)}) collective-permute-start(bf16[1,64,16,128]{3,2,1,0:T(8,128)(2,1)} %get-tuple-element.194), channel_id=1, source_target_pairs={{97,0},{96,1},{99,2},{98,3},{101,4},{100,5},{103,6},{102,7},{105,8... | collective-permute-start | bytes 786440 | tf_op jit(solution)/shard_map/ppermute | solution.py:551
  279.2 60.9 %all-to-all-start.4 = ((bf16[64,5,16,128]{3,2,1,0:T(8,128)(2,1)}), bf16[64,5,16,128]{3,2,1,0:T(8,128)(2,1)S(1)}, u32[]{:S(2)}, u32[]{:S(2)}) async-start(bf16[64,5,16,128]{3,2,1,0:T(8,128)(2,1)} %get-tuple-element.204), calls=%async_computation.4 | async-start | bytes 2621440 | tf_op jit(solution)/shard_map/all_to_all | solution.py:500
  301.0 22.4 %collective-permute-start.10 = (bf16[1,64,16,128]{3,2,1,0:T(8,128)(2,1)}, bf16[1,64,16,128]{3,2,1,0:T(8,128)(2,1)S(1)}, u32[]{:S(2)}, u32[]{:S(2)}) collective-permute-start(bf16[1,64,16,128]{3,2,1,0:T(8,128)(2,1)} %get-tuple-element.198), channel_id=1, source_target_pairs={{25,0},{24,1},{27,2},{26,3},{29,4},{28,5},{31,6},{30,7},{1,8},{0,9... | collective-permute-start | bytes 786440 | tf_op jit(solution)/shard_map/ppermute | solution.py:551
  303.8 19.9 %collective-permute-start.7 = (bf16[1,64,16,128]{3,2,1,0:T(8,128)(2,1)}, bf16[1,64,16,128]{3,2,1,0:T(8,128)(2,1)S(1)}, u32[]{:S(2)}, u32[]{:S(2)}) collective-permute-start(bf16[1,64,16,128]{3,2,1,0:T(8,128)(2,1)} %get-tuple-element.195), channel_id=1, source_target_pairs={{8,0},{9,1},{10,2},{11,3},{12,4},{13,5},{14,6},{15,7},{16,8},{17,9... | collective-permute-start | bytes 786440 | tf_op jit(solution)/shard_map/ppermute | solution.py:551
  305.1 20.6 %collective-permute-start.8 = (bf16[1,64,16,128]{3,2,1,0:T(8,128)(2,1)}, bf16[1,64,16,128]{3,2,1,0:T(8,128)(2,1)}, u32[]{:S(2)}, u32[]{:S(2)}) collective-permute-start(bf16[1,64,16,128]{3,2,1,0:T(8,128)(2,1)} %get-tuple-element.196), channel_id=1, source_target_pairs={{9,0},{8,1},{11,2},{10,3},{13,4},{12,5},{15,6},{14,7},{17,8},{16,9... | collective-permute-start | bytes 786440 | tf_op jit(solution)/shard_map/ppermute | solution.py:551
  305.1 22.2 %collective-permute-start.9 = (bf16[1,64,16,128]{3,2,1,0:T(8,128)(2,1)}, bf16[1,64,16,128]{3,2,1,0:T(8,128)(2,1)}, u32[]{:S(2)}, u32[]{:S(2)}) collective-permute-start(bf16[1,64,16,128]{3,2,1,0:T(8,128)(2,1)} %get-tuple-element.197), channel_id=1, source_target_pairs={{24,0},{25,1},{26,2},{27,3},{28,4},{29,5},{30,6},{31,7},{0,8},{1,9... | collective-permute-start | bytes 786440 | tf_op jit(solution)/shard_map/ppermute | solution.py:551
  307.2 24.6 %collective-permute-start.11 = (bf16[1,64,16,128]{3,2,1,0:T(8,128)(2,1)}, bf16[1,64,16,128]{3,2,1,0:T(8,128)(2,1)}, u32[]{:S(2)}, u32[]{:S(2)}) collective-permute-start(bf16[1,64,16,128]{3,2,1,0:T(8,128)(2,1)} %get-tuple-element.199), channel_id=1, source_target_pairs={{2,0},{3,1},{4,2},{5,3},{6,4},{7,5},{0,6},{1,7},{10,8},{11,9},{12,... | collective-permute-start | bytes 786440 | tf_op jit(solution)/shard_map/ppermute | solution.py:551
  323.4 3.9 %copy-start.5 = (bf16[1,64,16,128]{3,2,1,0:T(8,128)(2,1)}, bf16[1,64,16,128]{3,2,1,0:T(8,128)(2,1)S(1)}, u32[]{:S(2)}) copy-start(bf16[1,64,16,128]{3,2,1,0:T(8,128)(2,1)S(1)} %collective-permute-done.10.refs_15_) | copy-start | bytes 786436
  323.4 8.5 %collective-permute-start.12 = (bf16[1,64,16,128]{3,2,1,0:T(8,128)(2,1)}, bf16[1,64,16,128]{3,2,1,0:T(8,128)(2,1)}, u32[]{:S(2)}, u32[]{:S(2)}) collective-permute-start(bf16[1,64,16,128]{3,2,1,0:T(8,128)(2,1)} %get-tuple-element.200), channel_id=1, source_target_pairs={{3,0},{2,1},{5,2},{4,3},{7,4},{6,5},{1,6},{0,7},{11,8},{10,9},{13,... | collective-permute-start | bytes 786440 | tf_op jit(solution)/shard_map/ppermute | solution.py:551
  323.6 3.7 %copy-start.6 = (bf16[1,64,16,128]{3,2,1,0:T(8,128)(2,1)}, bf16[1,64,16,128]{3,2,1,0:T(8,128)(2,1)S(1)}, u32[]{:S(2)}) copy-start(bf16[1,64,16,128]{3,2,1,0:T(8,128)(2,1)S(1)} %collective-permute-done.7.refs_12_) | copy-start | bytes 786436
  323.6 9.2 %collective-permute-start.13 = (bf16[1,64,16,128]{3,2,1,0:T(8,128)(2,1)}, bf16[1,64,16,128]{3,2,1,0:T(8,128)(2,1)}, u32[]{:S(2)}, u32[]{:S(2)}) collective-permute-start(bf16[1,64,16,128]{3,2,1,0:T(8,128)(2,1)} %get-tuple-element.201), channel_id=1, source_target_pairs={{6,0},{7,1},{0,2},{1,3},{2,4},{3,5},{4,6},{5,7},{14,8},{15,9},{8,1... | collective-permute-start | bytes 786440 | tf_op jit(solution)/shard_map/ppermute | solution.py:551
  325.7 14.3 %collective-permute-start.14 = (bf16[1,64,16,128]{3,2,1,0:T(8,128)(2,1)}, bf16[1,64,16,128]{3,2,1,0:T(8,128)(2,1)}, u32[]{:S(2)}, u32[]{:S(2)}) collective-permute-start(bf16[1,64,16,128]{3,2,1,0:T(8,128)(2,1)} %get-tuple-element.202), channel_id=1, source_target_pairs={{7,0},{6,1},{1,2},{0,3},{3,4},{2,5},{5,6},{4,7},{15,8},{14,9},{9,1... | collective-permute-start | bytes 786440 | tf_op jit(solution)/shard_map/ppermute | solution.py:551
  340.0 1.1 copy-start.4

commit v7 on v6

--- a/solution.py
+++ b/solution.py
@@ -44,6 +44,10 @@
 ROW_PARTNER = ROW_FROM_RANK + SPARE
 ROW_LEFT = ROW_PARTNER + 1
 ROWS = -(-(ROW_LEFT + 1) // 8) * 8
+
+
+def place(chip):
+    return chip % 4 * 16 + chip // 4 % 4 * 4 + chip // 16
 
 
 def through(device, shift):
@@ -173,7 +177,7 @@
             table[NEED + head] = jnp.maximum(table[NEED + head], wave)
 
     def direct(chip, carry):
-        note(plan[ROW_DIRECT + chip, me], chip, 0)
+        note(plan[ROW_DIRECT + chip, me], place(chip), 0)
         return carry
 
     lax.fori_loop(0, CHIPS, direct, 0)
@@ -195,12 +199,13 @@
 
     def one_slot(dest, carry):
         code = plan[chip, 2 * dest + core]
+        at = place(dest)
 
         def copy(*sources):
             for half, source in enumerate(sources):
                 pltpu.make_async_copy(
                     source.at[:, :, columns(code % 16)],
-                    send.at[dest // 2, dest % 2, pl.ds(half * HALF, HALF)],
+                    send.at[at // 2, at % 2, pl.ds(half * HALF, HALF)],
                     sem,
                 ).start()
 
@@ -276,7 +281,7 @@
     loads, stores = [], []
     for kind in range(KINDS):
         out = outs[1].at[kind] if kind < PARTNER else outs[kind - PARTNER + 2].at[0]
-        source = arrived.at[plan[ROW_FORWARD + kind, me], pl.ds(0, 2 * HALF)]
+        source = arrived.at[place(plan[ROW_FORWARD + kind, me]), pl.ds(0, 2 * HALF)]
         loads.append(pltpu.make_async_copy(source, moving.at[kind], sems.at[kind]))
         stores.append(pltpu.make_async_copy(moving.at[kind], out, out_sems.at[kind]))
     for load in loads:
@@ -296,7 +301,7 @@
         for index in range(SPARE):
             chip = plan[ROW_FROM + index, 2 * dest + core]
             rank = plan[ROW_FROM_RANK + index, 2 * dest + core]
-            gathered[dest, index] = spare[chip, rank]
+            gathered[place(dest), index] = spare[place(chip), rank]
         return carry
 
     lax.fori_loop(0, CHIPS, one_dest, 0)
@@ -492,7 +497,7 @@
     )(*operands)
 
 
-LANES = [[2 * chip + core for chip in range(CHIPS)] for core in range(2)]
+LANES = [[2 * place(at) + core for at in range(CHIPS)] for core in range(2)]
 SWAP = [(device, device ^ 1) for device in range(DEVICES)]
 
 
@@ -542,6 +547,7 @@
     arrived, plan, table, queries, keys, values, other_keys, other_values, me_ref = held
     arrived = arrived.reshape(CHIPS, SLOT_PIECES, PIECE, HEAD)
     pieces, *outgoing = forward(plan, me_ref, arrived)
+    pieces = exchange(pieces)
     outgoing = dict(zip([0, *range(PARTNER, KINDS)], outgoing))
     forwarded = {}
     out = None
@@ -549,9 +555,6 @@
         if wave:
             for kind in [kind for kind in outgoing if WAVE_OF[kind] == wave]:
                 forwarded[kind] = lax.ppermute(outgoing[kind], "ctx", shift_pairs(SHIFTS[kind]))
-        if wave == 1:
-            pieces, out = lax.optimization_barrier((pieces, out))
-            pieces = exchange(pieces)
         out = attend(
             wave,
             out,

time: 351 us -> 345 us (0.983)
  the two profiles are of different devices: /device:TPU:7 before, /device:TPU:40 now
where the time goes in v7:
time: 345 us; the launch traced here: 343 us
  blocking collectives  207 us (60%)
  Pallas kernels  69.8 us (20%)
  starting transfers between devices  42.4 us (12%)
  waiting for transfers between devices  17.5 us (5%)
  local copies, waits for them, and re-layouts  5.16 us (1%)
    all_to_all x1, blocking collectives, exchange(): lax.all_to_all(array, 'ctx', 0, 0, axis_index_groups=LANES, tiled=True)  207 us
    pallas_call x4, Pallas kernels, attend(): pl.pallas_call(lambda *refs: attend_kernel(wave, kinds, *refs), in_specs=...  39.4 us
    ppermute x13, starting transfers between devices, body(): lax.ppermute(outgoing[kind], 'ctx', shift_pairs(SHIFTS[kind]))  21 us
    pallas_call x1, Pallas kernels, forward(): pl.pallas_call(forward_kernel, in_specs=[SMEM, SMEM, ANY], out_specs=[ANY...  14.5 us
    all_to_all x1, starting transfers between devices, exchange(): lax.all_to_all(array, 'ctx', 0, 0, axis_index_groups=LANES, tiled=True)  10.7 us
    pallas_call x1, Pallas kernels, pack(): pl.pallas_call(pack_kernel, in_specs=[SMEM, SMEM, VMEM, VMEM, VMEM, VMEM]...  10.4 us
    all_to_all x1, starting transfers between devices, body(): chosen_all = lax.all_to_all(spread, 'ctx', 0, 0, tiled=True)  10.2 us
    ppermute x13, waiting for transfers between devices, body(): lax.ppermute(outgoing[kind], 'ctx', shift_pairs(SHIFTS[kind]))  9.88 us
  transfers between devices with their start and end apart: 17, of which 3 were waited for; matrix products, arithmetic and copies ran while one was open for 1% of the time, Pallas kernels for 11%

profile of v7, /device:TPU:40, one launch (start us, length us, event | category | flops | bytes accessed | tf_op | source)
XLA Modules:
  0.0 342.9 jit_solution(1003233815318913025)
XLA Ops:
  0.0 0.0 collective-permute-start
  0.0 0.5 collective-permute-start.1
  0.5 0.8 copy.30
  1.3 0.1 broadcast_in_dim.55
  1.4 0.7 broadcast_in_dim.56
  2.0 10.2 %all-to-all-start.2 = ((s32[128,1,48]{2,1,0:T(1,128)}), s32[128,1,48]{2,1,0:T(1,128)S(1)}, u32[]{:S(2)}, u32[]{:S(2)}) async-start(s32[128,1,48]{2,1,0:T(1,128)} %broadcast_in_dim.56), calls=%async_computation.2 | async-start | bytes 131072 | tf_op jit(solution)/shard_map/all_to_all | solution.py:541
  12.2 7.6 %all-to-all-done.2 = s32[128,1,48]{2,1,0:T(1,128)S(1)} async-done(((s32[128,1,48]{2,1,0:T(1,128)}), s32[128,1,48]{2,1,0:T(1,128)S(1)}, u32[]{:S(2)}, u32[]{:S(2)}) %all-to-all-start.2) | async-done | bytes 24608 | tf_op jit(solution)/shard_map/all_to_all | solution.py:541
  19.8 0.1 copy.31
  19.8 5.4 %plan.1 = s32[248,128]{1,0:T(8,128)} custom-call(s32[48,128]{1,0:T(8,128)S(1)} %bitcast.100), custom_call_target="tpu_custom_call" | custom-call | tf_op jit(solution)/shard_map/plan/pallas_call | solution.py:155
  25.3 0.0 collective-permute-done
  25.3 0.0 copy-start.3
  25.3 0.0 collective-permute-done.1
  25.3 1.3 copy-done.3
  26.6 10.4 %pack.1 = (bf16[32,2,69,16,128]{4,3,2,1,0:T(8,128)(2,1)}, s32[148]{0:T(256)}) custom-call(s32[248,128]{1,0:T(8,128)} %plan.1, s32[1]{0:T(128)} %bitcast.13.me_ref, bf16[32,16,2048]{2,1,0:T(8,128)(2,1)} %bitcast.73, bf16[32,16,2048]{2,1,0:T(8,128)(2,1)} %bitcast.78, bf16[32,16,2048]{2,1,0:T(8,128)(2,1)} %bitcast.83, bf16[32,16,2048]{2,1,0:T(8,128)(2,1)} %bitcast.17.other_values), custom_call_target="tpu_custom_call" | custom-call | tf_op jit(solution)/shard_map/pack/pallas_call | solution.py:263
  37.0 206.8 %all_to_all.28 = bf16[64,1104,128]{2,1,0:T(8,128)(2,1)} all-to-all(bf16[64,1104,128]{2,1,0:T(8,128)(2,1)} %bitcast.93), channel_id=1, replica_groups={{0,32,64,96,8,40,72,104,16,48,80,112,24,56,88,120,2,34,66,98,10,42,74,1..., dimensions={0} | all-to-all | bytes 36175872 | tf_op jit(solution)/shard_map/all_to_all | solution.py:505
  243.8 0.0 copy-start.1
  243.8 14.5 %forward.1 = (bf16[64,5,16,128]{3,2,1,0:T(8,128)(2,1)}, bf16[6,64,16,128]{3,2,1,0:T(8,128)(2,1)}, bf16[1,64,16,128]{3,2,1,0:T(8,128)(2,1)}, bf16[1,64,16,128]{3,...) custom-call(s32[248,128]{1,0:T(8,128)} %plan.1, ...), custom_call_target="tpu_custom_call" | custom-call | tf_op jit(solution)/shard_map/forward/pallas_call | solution.py:316
  258.3 0.1 collective-permute-start.2
  258.4 1.9 collective-permute-start.3
  260.4 0.1 collective-permute-start.4
  260.4 1.7 collective-permute-start.5
  262.2 0.0 collective-permute-start.6
  262.2 10.7 %all-to-all-start.4 = ((bf16[64,5,16,128]{3,2,1,0:T(8,128)(2,1)}), bf16[64,5,16,128]{3,2,1,0:T(8,128)(2,1)S(1)}, u32[]{:S(2)}, u32[]{:S(2)}) async-start(bf16[64,5,16,128]{3,2,1,0:T(8,128)(2,1)} %get-tuple-element.201), calls=%async_computation.4 | async-start | bytes 2621440 | tf_op jit(solution)/shard_map/all_to_all | solution.py:505
  272.9 0.0 copy-done.1
  272.9 16.9 %attend.4.refs_12_ = bf16[32,16,2048]{2,1,0:T(8,128)(2,1)} custom-call(s32[148]{0:T(256)} %get-tuple-element.180.refs_0_, bf16[32,16,2048]{2,1,0:T(8,128)(2,1)} %bitcast.88, bf16[32,16,2048]{2,1,0:T(8,128)(2,1)S(1)} %bitcast.74, bf16[32,16,2048]{2,1,0:T(8,128)(2,1)} %bitcast.79, bf16[32,16,2048]{2,1,0:T(8,128)(2,1)} %bitcast.84, ...), custom_call_target="tpu_custom_call" | custom-call | flops 19327352832 | bytes 3145728 | tf_op jit(solution)/shard_map/attend/pallas_call | solution.py:478
  289.8 1.2 slice.3
  291.6 0.0 collective-permute-done.3.refs_8_
  291.6 4.6 %collective-permute-start.10 = (bf16[1,64,16,128]{3,2,1,0:T(8,128)(2,1)}, bf16[1,64,16,128]{3,2,1,0:T(8,128)(2,1)S(1)}, u32[]{:S(2)}, u32[]{:S(2)}) collective-permute-start(bf16[1,64,16,128]{3,2,1,0:T(8,128)(2,1)} %get-tuple-element.196), channel_id=1, source_target_pairs={{25,0},{24,1},{27,2},{26,3},{29,4},{28,5},{31,6},{30,7},{1,8},{0,9... | collective-permute-start | bytes 786440 | tf_op jit(solution)/shard_map/ppermute | solution.py:557
  296.2 0.0 collective-permute-done.4.refs_9_
  296.2 1.8 collective-permute-start.7
  298.0 0.0 collective-permute-done.5.refs_10_
  298.0 0.0 collective-permute-start.8
  298.0 0.0 collective-permute-done.6.refs_11_
  298.0 0.3 collective-permute-start.9
  298.3 0.0 collective-permute-done.2.refs_7_
  298.3 1.9 collective-permute-start.11
  300.2 11.7 %attend.5.refs_16_ = bf16[32,16,2048]{2,1,0:T(8,128)(2,1)} custom-call(s32[148]{0:T(256)} %get-tuple-element.180.refs_0_, bf16[32,16,2048]{2,1,0:T(8,128)(2,1)} %bitcast.89, bf16[32,16,2048]{2,1,0:T(8,128)(2,1)S(1)} %bitcast.75, bf16[32,16,2048]{2,1,0:T(8,128)(2,1)} %bitcast.80, bf16[32,16,2048]{2,1,0:T(8,128)(2,1)} %bitcast.85, ...), custom_call_target="tpu_custom_call", output_to_operand_aliasing={{}: (12, {})} | custom-call | flops 8589934592 | bytes 3145728 | tf_op jit(solution)/shard_map/attend/pallas_call | solution.py:478
  311.9 0.0 collective-permute-done.10.refs_15_
  312.0 0.0 copy-start.5
  312.0 1.8 collective-permute-start.12
  313.8 0.0 collective-permute-done.7.refs_12_
  313.8 0.0 copy-start.6
  313.8 0.0 collective-permute-start.13
  313.8 0.0 collective-permute-done.8.refs_13_
  313.8 6.8 %collective-permute-start.14 = (bf16[1,64,16,128]{3,2,1,0:T(8,128)(2,1)}, bf16[1,64,16,128]{3,2,1,0:T(8,128)(2,1)}, u32[]{:S(2)}, u32[]{:S(2)}) collective-permute-start(bf16[1,64,16,128]{3,2,1,0:T(8,128)(2,1)} %get-tuple-element.200), channel_id=1, source_target_pairs={{7,0},{6,1},{1,2},{0,3},{3,4},{2,5},{5,6},{4,7},{15,8},{14,9},{9,1... | collective-permute-start | bytes 786440 | tf_op jit(solution)/shard_map/ppermute | solution.py:557
  320.6 0.0 collective-permute-done.9.refs_14_
  320.6 0.0 copy-done.5
  320.6 0.0 copy-done.6
  320.6 4.5 %attend.6.refs_21_ = bf16[32,16,2048]{2,1,0:T(8,128)(2,1)} custom-call(s32[148]{0:T(256)} %get-tuple-element.180.refs_0_, bf16[32,16,2048]{2,1,0:T(8,128)(2,1)} %bitcast.90, bf16[32,16,2048]{2,1,0:T(8,128)(2,1)S(1)} %bitcast.76, bf16[32,16,2048]{2,1,0:T(8,128)(2,1)} %bitcast.81, bf16[32,16,2048]{2,1,0:T(8,128)(2,1)} %bitcast.86, ...), custom_call_target="tpu_custom_call", output_to_operand_aliasing={{}: (16, {})} | custom-call | flops 4294967296 | bytes 3145728 | tf_op jit(solution)/shard_map/attend/pallas_call | solution.py:478
  325.2 0.0 collective-permute-done.11.refs_16_
  325.2 0.0 collective-permute-done.12.refs_17_
  325.2 3.2 collective-permute-done.13.refs_18_
  328.4 6.7 %collective-permute-done.14.refs_19_ = bf16[1,64,16,128]{3,2,1,0:T(8,128)(2,1)} collective-permute-done((bf16[1,64,16,128]{3,2,1,0:T(8,128)(2,1)}, bf16[1,64,16,128]{3,2,1,0:T(8,128)(2,1)}, u32[]{:S(2)}, u32[]{:S(2)}) %collective-permute-start.14) | collective-permute-done | bytes 262176 | tf_op jit(solution)/shard_map/ppermute | solution.py:557
  335.1 0.0 all-to-all-done.4
  335.1 0.0 copy-start.4
  335.1 1.1 copy-done.4
  336.1 6.3 %attend.7 = bf16[32,16,2048]{2,1,0:T(8,128)(2,1)} custom-call(s32[148]{0:T(256)} %get-tuple-element.180.refs_0_, bf16[32,16,2048]{2,1,0:T(8,128)(2,1)} %bitcast.91, bf16[32,16,2048]{2,1,0:T(8,128)(2,1)S(1)} %bitcast.77, bf16[32,16,2048]{2,1,0:T(8,128)(2,1)} %bitcast.82, bf16[32,16,2048]{2,1,0:T(8,128)(2,1)} %bitcast.87, ...), custom_call_target="tpu_custom_call", output_to_operand_aliasing={{}: (21, {})} | custom-call | flops 4294967296 | bytes 3145728 | tf_op jit(solution)/shard_map/attend/pallas_call | solution.py:478
  342.4 0.3 conditional.1
Async XLA Ops:
  0.0 25.3 %collective-permute-start = (bf16[512,2048]{1,0:T(8,128)(2,1)}, bf16[512,2048]{1,0:T(8,128)(2,1)S(1)}, u32[]{:S(2)}, u32[]{:S(2)}) collective-permute-start(bf16[512,2048]{1,0:T(8,128)(2,1)} %param.11), channel_id=1, source_target_pairs={{0,1},{1,0},{2,3},{3,2},{4,5},{5,4},{6,7},{7,6},{8,9},{9,8},{10,11... | collective-permute-start | bytes 6291464 | tf_op jit(solution)/shard_map/ppermute | solution.py:538
  0.0 25.3 %collective-permute-start.1 = (bf16[512,2048]{1,0:T(8,128)(2,1)}, bf16[512,2048]{1,0:T(8,128)(2,1)}, u32[]{:S(2)}, u32[]{:S(2)}) collective-permute-start(bf16[512,2048]{1,0:T(8,128)(2,1)} %param.12), channel_id=1, source_target_pairs={{0,1},{1,0},{2,3},{3,2},{4,5},{5,4},{6,7},{7,6},{8,9},{9,8},{10,11... | collective-permute-start | bytes 6291464 | tf_op jit(solution)/shard_map/ppermute | solution.py:539
  2.0 17.8 %all-to-all-start.2 = ((s32[128,1,48]{2,1,0:T(1,128)}), s32[128,1,48]{2,1,0:T(1,128)S(1)}, u32[]{:S(2)}, u32[]{:S(2)}) async-start(s32[128,1,48]{2,1,0:T(1,128)} %broadcast_in_dim.56), calls=%async_computation.2 | async-start | bytes 131072 | tf_op jit(solution)/shard_map/all_to_all | solution.py:541
  25.3 1.3 copy-start.3
  243.8 29.1 %copy-start.1 = (bf16[512,2048]{1,0:T(8,128)(2,1)S(1)}, bf16[512,2048]{1,0:T(8,128)(2,1)}, u32[]{:S(2)}) copy-start(bf16[512,2048]{1,0:T(8,128)(2,1)} %param.11) | copy-start | bytes 6291460
  258.3 40.0 %collective-permute-start.2 = (bf16[6,64,16,128]{3,2,1,0:T(8,128)(2,1)}, bf16[6,64,16,128]{3,2,1,0:T(8,128)(2,1)}, u32[]{:S(2)}, u32[]{:S(2)}) collective-permute-start(bf16[6,64,16,128]{3,2,1,0:T(8,128)(2,1)} %get-tuple-element.188), channel_id=1, source_target_pairs={{1,0},{0,1},{3,2},{2,3},{5,4},{4,5},{7,6},{6,7},{9,8},{8,9},{11,10... | collective-permute-start | bytes 4718600 | tf_op jit(solution)/shard_map/ppermute | solution.py:557
  258.4 33.2 %collective-permute-start.3 = (bf16[1,64,16,128]{3,2,1,0:T(8,128)(2,1)}, bf16[1,64,16,128]{3,2,1,0:T(8,128)(2,1)}, u32[]{:S(2)}, u32[]{:S(2)}) collective-permute-start(bf16[1,64,16,128]{3,2,1,0:T(8,128)(2,1)} %get-tuple-element.189), channel_id=1, source_target_pairs={{32,0},{33,1},{34,2},{35,3},{36,4},{37,5},{38,6},{39,7},{40,8},{41... | collective-permute-start | bytes 786440 | tf_op jit(solution)/shard_map/ppermute | solution.py:557
  260.4 35.8 %collective-permute-start.4 = (bf16[1,64,16,128]{3,2,1,0:T(8,128)(2,1)}, bf16[1,64,16,128]{3,2,1,0:T(8,128)(2,1)}, u32[]{:S(2)}, u32[]{:S(2)}) collective-permute-start(bf16[1,64,16,128]{3,2,1,0:T(8,128)(2,1)} %get-tuple-element.190), channel_id=1, source_target_pairs={{33,0},{32,1},{35,2},{34,3},{37,4},{36,5},{39,6},{38,7},{41,8},{40... | collective-permute-start | bytes 786440 | tf_op jit(solution)/shard_map/ppermute | solution.py:557
  260.4 37.5 %collective-permute-start.5 = (bf16[1,64,16,128]{3,2,1,0:T(8,128)(2,1)}, bf16[1,64,16,128]{3,2,1,0:T(8,128)(2,1)}, u32[]{:S(2)}, u32[]{:S(2)}) collective-permute-start(bf16[1,64,16,128]{3,2,1,0:T(8,128)(2,1)} %get-tuple-element.191), channel_id=1, source_target_pairs={{96,0},{97,1},{98,2},{99,3},{100,4},{101,5},{102,6},{103,7},{104,8... | collective-permute-start | bytes 786440 | tf_op jit(solution)/shard_map/ppermute | solution.py:557
  262.2 35.8 %collective-permute-start.6 = (bf16[1,64,16,128]{3,2,1,0:T(8,128)(2,1)}, bf16[1,64,16,128]{3,2,1,0:T(8,128)(2,1)}, u32[]{:S(2)}, u32[]{:S(2)}) collective-permute-start(bf16[1,64,16,128]{3,2,1,0:T(8,128)(2,1)} %get-tuple-element.192), channel_id=1, source_target_pairs={{97,0},{96,1},{99,2},{98,3},{101,4},{100,5},{103,6},{102,7},{105,8... | collective-permute-start | bytes 786440 | tf_op jit(solution)/shard_map/ppermute | solution.py:557
  262.2 72.9 %all-to-all-start.4 = ((bf16[64,5,16,128]{3,2,1,0:T(8,128)(2,1)}), bf16[64,5,16,128]{3,2,1,0:T(8,128)(2,1)S(1)}, u32[]{:S(2)}, u32[]{:S(2)}) async-start(bf16[64,5,16,128]{3,2,1,0:T(8,128)(2,1)} %get-tuple-element.201), calls=%async_computation.4 | async-start | bytes 2621440 | tf_op jit(solution)/shard_map/all_to_all | solution.py:505
  291.6 20.3 %collective-permute-start.10 = (bf16[1,64,16,128]{3,2,1,0:T(8,128)(2,1)}, bf16[1,64,16,128]{3,2,1,0:T(8,128)(2,1)S(1)}, u32[]{:S(2)}, u32[]{:S(2)}) collective-permute-start(bf16[1,64,16,128]{3,2,1,0:T(8,128)(2,1)} %get-tuple-element.196), channel_id=1, source_target_pairs={{25,0},{24,1},{27,2},{26,3},{29,4},{28,5},{31,6},{30,7},{1,8},{0,9... | collective-permute-start | bytes 786440 | tf_op jit(solution)/shard_map/ppermute | solution.py:557
  296.2 17.6 %collective-permute-start.7 = (bf16[1,64,16,128]{3,2,1,0:T(8,128)(2,1)}, bf16[1,64,16,128]{3,2,1,0:T(8,128)(2,1)S(1)}, u32[]{:S(2)}, u32[]{:S(2)}) collective-permute-start(bf16[1,64,16,128]{3,2,1,0:T(8,128)(2,1)} %get-tuple-element.193), channel_id=1, source_target_pairs={{8,0},{9,1},{10,2},{11,3},{12,4},{13,5},{14,6},{15,7},{16,8},{17,9... | collective-permute-start | bytes 786440 | tf_op jit(solution)/shard_map/ppermute | solution.py:557
  298.0 15.8 %collective-permute-start.8 = (bf16[1,64,16,128]{3,2,1,0:T(8,128)(2,1)}, bf16[1,64,16,128]{3,2,1,0:T(8,128)(2,1)}, u32[]{:S(2)}, u32[]{:S(2)}) collective-permute-start(bf16[1,64,16,128]{3,2,1,0:T(8,128)(2,1)} %get-tuple-element.194), channel_id=1, source_target_pairs={{9,0},{8,1},{11,2},{10,3},{13,4},{12,5},{15,6},{14,7},{17,8},{16,9... | collective-permute-start | bytes 786440 | tf_op jit(solution)/shard_map/ppermute | solution.py:557
  298.0 22.7 %collective-permute-start.9 = (bf16[1,64,16,128]{3,2,1,0:T(8,128)(2,1)}, bf16[1,64,16,128]{3,2,1,0:T(8,128)(2,1)}, u32[]{:S(2)}, u32[]{:S(2)}) collective-permute-start(bf16[1,64,16,128]{3,2,1,0:T(8,128)(2,1)} %get-tuple-element.195), channel_id=1, source_target_pairs={{24,0},{25,1},{26,2},{27,3},{28,4},{29,5},{30,6},{31,7},{0,8},{1,9... | collective-permute-start | bytes 786440 | tf_op jit(solution)/shard_map/ppermute | solution.py:557
  298.3 26.9 %collective-permute-start.11 = (bf16[1,64,16,128]{3,2,1,0:T(8,128)(2,1)}, bf16[1,64,16,128]{3,2,1,0:T(8,128)(2,1)}, u32[]{:S(2)}, u32[]{:S(2)}) collective-permute-start(bf16[1,64,16,128]{3,2,1,0:T(8,128)(2,1)} %get-tuple-element.197), channel_id=1, source_target_pairs={{2,0},{3,1},{4,2},{5,3},{6,4},{7,5},{0,6},{1,7},{10,8},{11,9},{12,... | collective-permute-start | bytes 786440 | tf_op jit(solution)/shard_map/ppermute | solution.py:557
  312.0 8.7 %copy-start.5 = (bf16[1,64,16,128]{3,2,1,0:T(8,128)(2,1)}, bf16[1,64,16,128]{3,2,1,0:T(8,128)(2,1)S(1)}, u32[]{:S(2)}) copy-start(bf16[1,64,16,128]{3,2,1,0:T(8,128)(2,1)S(1)} %collective-permute-done.10.refs_15_) | copy-start | bytes 786436
  312.0 13.2 %collective-permute-start.12 = (bf16[1,64,16,128]{3,2,1,0:T(8,128)(2,1)}, bf16[1,64,16,128]{3,2,1,0:T(8,128)(2,1)}, u32[]{:S(2)}, u32[]{:S(2)}) collective-permute-start(bf16[1,64,16,128]{3,2,1,0:T(8,128)(2,1)} %get-tuple-element.198), channel_id=1, source_target_pairs={{3,0},{2,1},{5,2},{4,3},{7,4},{6,5},{1,6},{0,7},{11,8},{10,9},{13,... | collective-permute-start | bytes 786440 | tf_op jit(solution)/shard_map/ppermute | solution.py:557
  313.8 6.9 %copy-start.6 = (bf16[1,64,16,128]{3,2,1,0:T(8,128)(2,1)}, bf16[1,64,16,128]{3,2,1,0:T(8,128)(2,1)S(1)}, u32[]{:S(2)}) copy-start(bf16[1,64,16,128]{3,2,1,0:T(8,128)(2,1)S(1)} %collective-permute-done.7.refs_12_) | copy-start | bytes 786436
  313.8 14.6 %collective-permute-start.13 = (bf16[1,64,16,128]{3,2,1,0:T(8,128)(2,1)}, bf16[1,64,16,128]{3,2,1,0:T(8,128)(2,1)}, u32[]{:S(2)}, u32[]{:S(2)}) collective-permute-start(bf16[1,64,16,128]{3,2,1,0:T(8,128)(2,1)} %get-tuple-element.199), channel_id=1, source_target_pairs={{6,0},{7,1},{0,2},{1,3},{2,4},{3,5},{4,6},{5,7},{14,8},{15,9},{8,1... | collective-permute-start | bytes 786440 | tf_op jit(solution)/shard_map/ppermute | solution.py:557
  313.8 21.3 %collective-permute-start.14 = (bf16[1,64,16,128]{3,2,1,0:T(8,128)(2,1)}, bf16[1,64,16,128]{3,2,1,0:T(8,128)(2,1)}, u32[]{:S(2)}, u32[]{:S(2)}) collective-permute-start(bf16[1,64,16,128]{3,2,1,0:T(8,128)(2,1)} %get-tuple-element.200), channel_id=1, source_target_pairs={{7,0},{6,1},{1,2},{0,3},{3,4},{2,5},{5,6},{4,7},{15,8},{14,9},{9,1... | collective-permute-start | bytes 786440 | tf_op jit(solution)/shard_map/ppermute | solution.py:557
  335.1 1.1 copy-start.4
